TPU v7x, 32 devices: a whole 2x2x4 slice. The times are simulated.
32 devices in a mesh: ctx: 8 (over z, core), fsdp: 4 (over y, x).
Axes of the slice: x: 2, y: 2, z: 4, core: 2. Of those that a mesh axis runs over, the one named last changes fastest.
Arguments:
- tokens: bfloat16 [4, 2048, 1600], P('fsdp', 'ctx'), may hold values from -6 to 6
- out_grad: bfloat16 [4, 2048, 1600], P('fsdp', 'ctx'), may hold values from -6 to 6
- teacher: bfloat16 [4, 2048, 1600], P('fsdp', 'ctx'), may hold values from -9 to 9
- valid: int32 [4, 2048], P('fsdp', 'ctx'), may hold values from 0 to 1, as said below
- w_query: bfloat16 [1600, 1600], P('ctx', 'fsdp'), may hold values from -0.15625 to 0.15625
- w_keyval: bfloat16 [1600, 640], P('ctx', 'fsdp'), may hold values from -0.15625 to 0.15625
- w_attn_out: bfloat16 [1600, 1600], P('ctx', 'fsdp'), may hold values from -0.15625 to 0.15625
- w_in: bfloat16 [1600, 6400], P('ctx', 'fsdp'), may hold values from -0.15625 to 0.15625
- w_mamba_out: bfloat16 [3200, 1600], P('ctx', 'fsdp'), may hold values from -0.109375 to 0.109375
- w_gate: bfloat16 [1600, 5504], P('ctx', 'fsdp'), may hold values from -0.15625 to 0.15625
- w_up: bfloat16 [1600, 5504], P('ctx', 'fsdp'), may hold values from -0.15625 to 0.15625
- w_down: bfloat16 [5504, 1600], P('ctx', 'fsdp'), may hold values from -0.078125 to 0.078125
- x_proj: bfloat16 [3200, 132], P(('ctx', 'fsdp')), may hold values from -0.109375 to 0.109375
- dt_proj: bfloat16 [3200, 100], P(('ctx', 'fsdp')), may hold values from -0.625 to 0.625
- a_log: bfloat16 [3200, 16], P(('ctx', 'fsdp')), may hold values from -9 to -1
- conv_taps: bfloat16 [3200, 4], P(('ctx', 'fsdp')), may hold values from -3 to 3
- conv_bias: bfloat16 [3200], P(('ctx', 'fsdp')), may hold values from -3 to 3
- dt_bias: bfloat16 [3200], P(('ctx', 'fsdp')), may hold values from -4.5 to -2
- skip_gain: bfloat16 [3200], P(('ctx', 'fsdp')), may hold values from 0.5 to 1.5
- norm_gains: bfloat16 [6400], P(('ctx', 'fsdp')), may hold values from 0.5 to 1.5
Outputs:
- loss: float32 [], replicated
- output: bfloat16 [4, 2048, 1600], P('fsdp', 'ctx')
- input_grad: float32 [4, 2048, 1600], P('fsdp', 'ctx')
- w_query_grad: float32 [1600, 1600], P('ctx', 'fsdp')
- w_keyval_grad: float32 [1600, 640], P('ctx', 'fsdp')
- w_attn_out_grad: float32 [1600, 1600], P('ctx', 'fsdp')
- w_in_grad: float32 [1600, 6400], P('ctx', 'fsdp')
- w_mamba_out_grad: float32 [3200, 1600], P('ctx', 'fsdp')
- w_gate_grad: float32 [1600, 5504], P('ctx', 'fsdp')
- w_up_grad: float32 [1600, 5504], P('ctx', 'fsdp')
- w_down_grad: float32 [5504, 1600], P('ctx', 'fsdp')
- x_proj_grad: float32 [3200, 132], P(('ctx', 'fsdp'))
- dt_proj_grad: float32 [3200, 100], P(('ctx', 'fsdp'))
- a_log_grad: float32 [3200, 16], P(('ctx', 'fsdp'))
- conv_taps_grad: float32 [3200, 4], P(('ctx', 'fsdp'))
- conv_bias_grad: float32 [3200], P(('ctx', 'fsdp'))
- dt_bias_grad: float32 [3200], P(('ctx', 'fsdp'))
- skip_gain_grad: float32 [3200], P(('ctx', 'fsdp'))
- norm_gains_grad: float32 [6400], P(('ctx', 'fsdp'))
Inputs may be any that keep to these rules, and one draw needn't show every extreme that they name: `valid`: 1 marks a token that counts in the loss; the last token of every sequence counts.
All inputs are finite; a program needn't handle non-finite values.
Results may differ from a plain program's by a relative error of at most 0.014.
The roundings to bfloat16 on the way count: a program that leaves them out, or rounds other values in their place, can miss the bound.
Values may be sent and summed in bfloat16 or wider, within the bound.
A program may use at most 448 MiB of HBM per device.

v0:
```python
import jax
import jax.numpy as jnp
from jax import lax
from jax.sharding import PartitionSpec as P

D = 1600
H = 25
HD = 64
KVH = 5
WINDOW = 1024
DI = 3200
DS = 16
KC = 4
R = 100


def passed_along(block, axis, distance):
    devices = range(lax.axis_size(axis))
    route = [(i - distance, i) for i in devices if i - distance in devices]
    return lax.ppermute(block, axis, route)


def carried_in(value, axis, join, neutral, backward):
    count, mine = (lax.axis_size(axis), lax.axis_index(axis))
    pieces = jax.tree.map(lambda part: lax.all_gather(part, axis), value)
    if backward:
        pieces = jax.tree.map(lambda part: part[::-1], pieces)
        mine = count - 1 - mine
    so_far = jax.tree.map(
        lambda part, zero: jnp.full_like(part, 0) + jnp.asarray(zero, part.dtype), value, neutral
    )

    def hop(position, so_far):
        longer = join(so_far, jax.tree.map(lambda part: part[position], pieces))
        return jax.tree.map(lambda new, old: jnp.where(position < mine, new, old), longer, so_far)

    return lax.fori_loop(0, count - 1, hop, so_far)


def matmul(left, right):
    return jnp.dot(left, right, preferred_element_type=jnp.float32)


def matmul_tn(left, right):
    return lax.dot_general(
        left, right, (((0,), (0,)), ((), ())), preferred_element_type=jnp.float32
    )


def matmul_nt(left, right):
    return lax.dot_general(
        left, right, (((1,), (1,)), ((), ())), preferred_element_type=jnp.float32
    )


def norm_forward(values, gain_vec):
    factor = lax.rsqrt(jnp.mean(values * values, axis=-1, keepdims=True) + 1e-06)
    return (values * factor * gain_vec, factor)


def norm_backward(values, factor, gain_vec, grad_out):
    weighted = grad_out * gain_vec
    inner_mean = jnp.mean(weighted * values, axis=-1, keepdims=True)
    grad_in = factor * weighted - values * (factor * factor * factor) * inner_mean
    return (grad_in, jnp.sum(grad_out * values * factor, axis=0))


def silu_slope(values):
    sigmoid_v = jax.nn.sigmoid(values)
    return sigmoid_v * (1.0 + values * (1.0 - sigmoid_v))


def chain_combine(earlier, later):
    return (earlier[0] * later[0], earlier[1] * later[0] + later[1])


def body(
    tokens,
    out_grad,
    teacher,
    valid,
    w_query,
    w_keyval,
    w_attn_out,
    w_in,
    w_mamba_out,
    w_gate,
    w_up,
    w_down,
    x_proj,
    dt_proj,
    a_log,
    conv_taps,
    conv_bias,
    dt_bias,
    skip_gain,
    norm_gains,
):
    (
        query_cols,
        keyval_cols,
        attn_out_cols,
        in_cols,
        mamba_out_cols,
        gate_cols,
        up_cols,
        down_cols,
        xproj_rows,
        dtproj_rows,
        alog_rows,
        taps_rows,
        cbias_rows,
        dtbias_rows,
        skip_rows,
        gain_rows,
    ) = (
        lax.all_gather(w_query, "fsdp", axis=1, tiled=True),
        lax.all_gather(w_keyval, "fsdp", axis=1, tiled=True),
        lax.all_gather(w_attn_out, "fsdp", axis=1, tiled=True),
        lax.all_gather(w_in, "fsdp", axis=1, tiled=True),
        lax.all_gather(w_mamba_out, "fsdp", axis=1, tiled=True),
        lax.all_gather(w_gate, "fsdp", axis=1, tiled=True),
        lax.all_gather(w_up, "fsdp", axis=1, tiled=True),
        lax.all_gather(w_down, "fsdp", axis=1, tiled=True),
        lax.all_gather(x_proj, "fsdp", axis=0, tiled=True),
        lax.all_gather(dt_proj, "fsdp", axis=0, tiled=True),
        lax.all_gather(a_log, "fsdp", axis=0, tiled=True),
        lax.all_gather(conv_taps, "fsdp", axis=0, tiled=True),
        lax.all_gather(conv_bias, "fsdp", axis=0, tiled=True),
        lax.all_gather(dt_bias, "fsdp", axis=0, tiled=True),
        lax.all_gather(skip_gain, "fsdp", axis=0, tiled=True),
        lax.all_gather(norm_gains, "fsdp", axis=0, tiled=True),
    )
    (
        query_weight,
        keyval_weight,
        attn_weight,
        in_weight,
        mamba_weight,
        gate_weight,
        up_weight,
        down_weight,
        xproj_weight,
        dtproj_weight,
        alog_full,
        taps_full,
        cbias_full,
        dtbias_full,
        skip_full,
        gains_full,
    ) = (
        lax.all_gather(query_cols, "ctx", axis=0, tiled=True),
        lax.all_gather(keyval_cols, "ctx", axis=0, tiled=True),
        lax.all_gather(attn_out_cols, "ctx", axis=0, tiled=True),
        lax.all_gather(in_cols, "ctx", axis=0, tiled=True),
        lax.all_gather(mamba_out_cols, "ctx", axis=0, tiled=True),
        lax.all_gather(gate_cols, "ctx", axis=0, tiled=True),
        lax.all_gather(up_cols, "ctx", axis=0, tiled=True),
        lax.all_gather(down_cols, "ctx", axis=0, tiled=True),
        lax.all_gather(xproj_rows, "ctx", axis=0, tiled=True),
        lax.all_gather(dtproj_rows, "ctx", axis=0, tiled=True),
        lax.all_gather(alog_rows, "ctx", axis=0, tiled=True),
        lax.all_gather(taps_rows, "ctx", axis=0, tiled=True),
        lax.all_gather(cbias_rows, "ctx", axis=0, tiled=True),
        lax.all_gather(dtbias_rows, "ctx", axis=0, tiled=True),
        lax.all_gather(skip_rows, "ctx", axis=0, tiled=True),
        lax.all_gather(gain_rows, "ctx", axis=0, tiled=True),
    )
    ctx_count = lax.axis_size("ctx")
    ctx_index = lax.axis_index("ctx")
    rows_here = tokens.shape[1]
    group_size = H // KVH
    head_scale = HD ** (-0.5)
    hidden = tokens[0].astype(jnp.float32)
    gain_set = gains_full.astype(jnp.float32).reshape(4, D)
    taps = taps_full.astype(jnp.float32)
    skip_vec = skip_full.astype(jnp.float32)
    a_mat = -jnp.exp(alog_full.astype(jnp.float32))
    zero_state = jnp.zeros((DI, DS), jnp.float32)
    ones_state = jnp.ones((DI, DS), jnp.float32)
    normed, factor_one = norm_forward(hidden, gain_set[0])
    normed_low = normed.astype(jnp.bfloat16)
    query_low = matmul(normed_low, query_weight).astype(jnp.bfloat16)
    keyval = matmul(normed_low, keyval_weight).astype(jnp.bfloat16)
    inner_low = matmul(normed_low, in_weight).astype(jnp.bfloat16)
    x_branch = inner_low[:, :DI]
    z_branch = inner_low[:, DI:].astype(jnp.float32)
    reach_blocks = min((WINDOW - 1 + rows_here - 1) // rows_here, ctx_count - 1)
    x_tail = x_branch[rows_here - (KC - 1) :]
    near_keyval, near_tail = passed_along((keyval, x_tail), "ctx", 1)
    far_rows = []
    for distance in range(2, reach_blocks + 1):
        far_rows.append(passed_along(keyval, "ctx", distance))
    key_rows = jnp.concatenate(far_rows[::-1] + [near_keyval, keyval], 0)
    span = key_rows.shape[0]
    query_pos = ctx_index * rows_here + jnp.arange(rows_here, dtype=jnp.int32)
    key_pos = (ctx_index - reach_blocks) * rows_here + jnp.arange(span, dtype=jnp.int32)
    gap_rows = query_pos[:, None] - key_pos[None, :]
    visible = (gap_rows >= 0) & (gap_rows < WINDOW) & (key_pos[None, :] >= 0)
    query_heads = query_low.reshape(rows_here, KVH, group_size, HD)
    key_heads = key_rows[:, : KVH * HD].reshape(span, KVH, HD)
    value_heads = key_rows[:, KVH * HD :].reshape(span, KVH, HD)

    def scores_of():
        raw_scores = jnp.einsum(
            "ikgd,jkd->kgij", query_heads, key_heads, preferred_element_type=jnp.float32
        )
        return jnp.where(visible, raw_scores * head_scale, -1e30)

    scores = scores_of()
    row_max = jnp.max(scores, axis=-1, keepdims=True)
    exponent = jnp.exp(scores - row_max)
    row_total = jnp.sum(exponent, axis=-1, keepdims=True)
    log_total = row_max + jnp.log(row_total)
    prob_low = (exponent / row_total).astype(jnp.bfloat16)
    attn_full = jnp.einsum(
        "kgij,jkd->ikgd", prob_low, value_heads, preferred_element_type=jnp.float32
    ).reshape(rows_here, H * HD)
    attn_low = attn_full.astype(jnp.bfloat16)
    attn_proj = matmul(attn_low, attn_weight)
    padded = jnp.concatenate([near_tail, x_branch], 0).astype(jnp.float32)
    pre_conv = cbias_full.astype(jnp.float32)
    for shift_index in range(KC):
        pre_conv = pre_conv + taps[:, shift_index] * padded[shift_index : shift_index + rows_here]
    ssm_in = jax.nn.silu(pre_conv)
    ssm_low = ssm_in.astype(jnp.bfloat16)
    x_dbl = matmul(ssm_low, xproj_weight).astype(jnp.bfloat16)
    dt_in = x_dbl[:, :R]
    b_sel = x_dbl[:, R : R + DS].astype(jnp.float32)
    c_sel = x_dbl[:, R + DS :].astype(jnp.float32)
    dt_pre = matmul_nt(dt_in, dtproj_weight) + dtbias_full.astype(jnp.float32)
    step_size = jax.nn.softplus(dt_pre)
    block_len = min(16, rows_here)
    block_count = rows_here // block_len

    def in_blocks(arrays):
        return arrays.reshape((block_count, block_len) + arrays.shape[1:])

    def chain_local(running, block_item):
        step_blk, input_blk, b_blk = block_item
        for position in range(block_len):
            running = (
                jnp.exp(step_blk[position][:, None] * a_mat) * running
                + (step_blk[position] * input_blk[position])[:, None] * b_blk[position][None, :]
            )
        return (running, None)

    local_end, unused_out = lax.scan(
        chain_local, zero_state, (in_blocks(step_size), in_blocks(ssm_in), in_blocks(b_sel))
    )
    decay_total = jnp.exp(a_mat * jnp.sum(step_size, axis=0)[:, None])
    start_state = carried_in(
        (decay_total, local_end), "ctx", chain_combine, (ones_state, zero_state), False
    )[1]

    def chain_full(running, block_item):
        step_blk, input_blk, b_blk, c_blk = block_item
        first_state = running
        out_rows = []
        for position in range(block_len):
            running = (
                jnp.exp(step_blk[position][:, None] * a_mat) * running
                + (step_blk[position] * input_blk[position])[:, None] * b_blk[position][None, :]
            )
            out_rows.append(jnp.sum(running * c_blk[position][None, :], axis=1))
        return (running, (first_state, jnp.stack(out_rows)))

    unused_end, (block_starts, ssm_rows) = lax.scan(
        chain_full,
        start_state,
        (in_blocks(step_size), in_blocks(ssm_in), in_blocks(b_sel), in_blocks(c_sel)),
    )
    ssm_out = ssm_rows.reshape(rows_here, DI) + skip_vec * ssm_in
    gate_z = jax.nn.silu(z_branch)
    mixed_low = (ssm_out * gate_z).astype(jnp.bfloat16)
    mamba_proj = matmul(mixed_low, mamba_weight)
    attn_norm, factor_attn = norm_forward(attn_proj, gain_set[1])
    mamba_norm, factor_mamba = norm_forward(mamba_proj, gain_set[2])
    residual = hidden + 0.5 * (attn_norm + mamba_norm)
    ffn_in, factor_ffn = norm_forward(residual, gain_set[3])
    ffn_low = ffn_in.astype(jnp.bfloat16)
    gate_pre = matmul(ffn_low, gate_weight)
    up_pre = matmul(ffn_low, up_weight)
    gate_act = jax.nn.silu(gate_pre)
    hidden_act = (gate_act * up_pre).astype(jnp.bfloat16)
    layer_out = residual + matmul(hidden_act, down_weight)
    mask_rows = valid[0].astype(jnp.float32)
    mismatch = layer_out - teacher[0].astype(jnp.float32)
    error_sum, valid_sum = lax.psum(
        (jnp.sum(mask_rows[:, None] * mismatch * mismatch), jnp.sum(mask_rows)), ("ctx", "fsdp")
    )
    loss = error_sum / (valid_sum * D)
    grad_layer = (
        out_grad[0].astype(jnp.float32) + 2.0 / (valid_sum * D) * mask_rows[:, None] * mismatch
    )
    grad_ffn_low = grad_layer.astype(jnp.bfloat16)
    grad_act = matmul_nt(grad_ffn_low, down_weight)
    grad_gate = (grad_act * up_pre * silu_slope(gate_pre)).astype(jnp.bfloat16)
    grad_up = (grad_act * gate_act).astype(jnp.bfloat16)
    grad_ffn_in = matmul_nt(grad_gate, gate_weight) + matmul_nt(grad_up, up_weight)
    grad_norm_res, gain_four = norm_backward(residual, factor_ffn, gain_set[3], grad_ffn_in)
    grad_resid = grad_layer + grad_norm_res
    half_grad = 0.5 * grad_resid
    grad_attn_proj, gain_two = norm_backward(attn_proj, factor_attn, gain_set[1], half_grad)
    grad_mamba_proj, gain_three = norm_backward(mamba_proj, factor_mamba, gain_set[2], half_grad)
    grad_attn_proj_low = grad_attn_proj.astype(jnp.bfloat16)
    grad_mamba_proj_low = grad_mamba_proj.astype(jnp.bfloat16)
    grad_attn_low = matmul_nt(grad_attn_proj_low, attn_weight).astype(jnp.bfloat16)
    grad_mixed = matmul_nt(grad_mamba_proj_low, mamba_weight)
    grad_heads = grad_attn_low.reshape(rows_here, KVH, group_size, HD)
    scores = scores_of()
    prob_full = jnp.exp(scores - log_total)
    prob_again = prob_full.astype(jnp.bfloat16)
    grad_probs = jnp.einsum(
        "ikgd,jkd->kgij", grad_heads, value_heads, preferred_element_type=jnp.float32
    )
    row_inner = jnp.sum(prob_full * grad_probs, axis=-1, keepdims=True)
    grad_scores = (prob_full * (grad_probs - row_inner)).astype(jnp.bfloat16)
    grad_query = (
        (
            jnp.einsum("kgij,jkd->ikgd", grad_scores, key_heads, preferred_element_type=jnp.float32)
            * head_scale
        )
        .reshape(rows_here, H * HD)
        .astype(jnp.bfloat16)
    )
    grad_keys = (
        jnp.einsum("kgij,ikgd->jkd", grad_scores, query_heads, preferred_element_type=jnp.float32)
        * head_scale
    )
    grad_values = jnp.einsum(
        "kgij,ikgd->jkd", prob_again, grad_heads, preferred_element_type=jnp.float32
    )
    grad_key_rows = jnp.concatenate(
        [grad_keys.reshape(span, KVH * HD), grad_values.reshape(span, KVH * HD)], 1
    )
    grad_ssm_out = grad_mixed * gate_z
    grad_z = grad_mixed * ssm_out * silu_slope(z_branch)
    skip_grad = jnp.sum(grad_ssm_out * ssm_in, axis=0)

    def adjoint_local(adjoint, block_item):
        step_blk, c_blk, dy_blk = block_item
        for position in reversed(range(block_len)):
            adjoint = jnp.exp(step_blk[position][:, None] * a_mat) * (
                adjoint + dy_blk[position][:, None] * c_blk[position][None, :]
            )
        return (adjoint, None)

    local_adjoint, unused_rows = lax.scan(
        adjoint_local,
        zero_state,
        (in_blocks(step_size), in_blocks(c_sel), in_blocks(grad_ssm_out)),
        reverse=True,
    )
    incoming = carried_in(
        (decay_total, local_adjoint), "ctx", chain_combine, (ones_state, zero_state), True
    )[1]

    def adjoint_full(carry, block_item):
        adjoint, a_grad = carry
        first_state, step_blk, input_blk, b_blk, c_blk, dy_blk = block_item
        history = [first_state]
        decay_list = []
        running = first_state
        for position in range(block_len):
            decay_now = jnp.exp(step_blk[position][:, None] * a_mat)
            running = (
                decay_now * running
                + (step_blk[position] * input_blk[position])[:, None] * b_blk[position][None, :]
            )
            decay_list.append(decay_now)
            history.append(running)
        step_grads = [None] * block_len
        input_grads = [None] * block_len
        b_grads = [None] * block_len
        c_grads = [None] * block_len
        for position in reversed(range(block_len)):
            adjoint = adjoint + dy_blk[position][:, None] * c_blk[position][None, :]
            through = adjoint * history[position] * decay_list[position]
            a_grad = a_grad + through * step_blk[position][:, None]
            along_b = jnp.sum(adjoint * b_blk[position][None, :], axis=1)
            step_grads[position] = jnp.sum(through * a_mat, axis=1) + input_blk[position] * along_b
            input_grads[position] = step_blk[position] * along_b
            b_grads[position] = jnp.sum(
                adjoint * (step_blk[position] * input_blk[position])[:, None], axis=0
            )
            c_grads[position] = jnp.sum(history[position + 1] * dy_blk[position][:, None], axis=0)
            adjoint = decay_list[position] * adjoint
        return (
            (adjoint, a_grad),
            (jnp.stack(step_grads), jnp.stack(input_grads), jnp.stack(b_grads), jnp.stack(c_grads)),
        )

    (unused_adjoint, a_accum), (step_grad_blk, input_grad_blk, b_grad_blk, c_grad_blk) = lax.scan(
        adjoint_full,
        (incoming, zero_state),
        (
            block_starts,
            in_blocks(step_size),
            in_blocks(ssm_in),
            in_blocks(b_sel),
            in_blocks(c_sel),
            in_blocks(grad_ssm_out),
        ),
        reverse=True,
    )
    alog_grad = a_accum * a_mat
    grad_dt_pre = (step_grad_blk.reshape(rows_here, DI) * jax.nn.sigmoid(dt_pre)).astype(
        jnp.bfloat16
    )
    dtbias_grad = jnp.sum(grad_dt_pre.astype(jnp.float32), axis=0)
    dtproj_grad = matmul_tn(grad_dt_pre, dt_in)
    grad_dt_in = matmul(grad_dt_pre, dtproj_weight)
    grad_xdbl = jnp.concatenate(
        [grad_dt_in, b_grad_blk.reshape(rows_here, DS), c_grad_blk.reshape(rows_here, DS)], 1
    ).astype(jnp.bfloat16)
    xproj_grad = matmul_tn(ssm_low, grad_xdbl)
    grad_ssm_in = (
        input_grad_blk.reshape(rows_here, DI)
        + skip_vec * grad_ssm_out
        + matmul_nt(grad_xdbl, xproj_weight)
    )
    grad_pre = grad_ssm_in * silu_slope(pre_conv)
    cbias_grad = jnp.sum(grad_pre, axis=0)
    taps_grad = jnp.stack(
        [
            jnp.sum(grad_pre * padded[shift_index : shift_index + rows_here], axis=0)
            for shift_index in range(KC)
        ],
        axis=1,
    )
    grad_padded = jnp.pad(taps[:, 0] * grad_pre, ((0, KC - 1), (0, 0)))
    for shift_index in range(1, KC):
        grad_padded = grad_padded + jnp.pad(
            taps[:, shift_index] * grad_pre, ((shift_index, KC - 1 - shift_index), (0, 0))
        )
    near_piece = grad_key_rows[(reach_blocks - 1) * rows_here : reach_blocks * rows_here]
    back_keyval, back_tail = passed_along((near_piece, grad_padded[: KC - 1]), "ctx", -1)
    total_keyval = grad_key_rows[reach_blocks * rows_here :] + back_keyval
    for distance in range(2, reach_blocks + 1):
        far_piece = grad_key_rows[
            (reach_blocks - distance) * rows_here : (reach_blocks - distance + 1) * rows_here
        ]
        total_keyval = total_keyval + passed_along(far_piece, "ctx", -distance)
    grad_keyval_low = total_keyval.astype(jnp.bfloat16)
    grad_x_branch = grad_padded[KC - 1 :] + jnp.pad(back_tail, ((rows_here - (KC - 1), 0), (0, 0)))
    grad_inner_low = jnp.concatenate([grad_x_branch, grad_z], 1).astype(jnp.bfloat16)
    grad_normed = (
        matmul_nt(grad_query, query_weight)
        + matmul_nt(grad_keyval_low, keyval_weight)
        + matmul_nt(grad_inner_low, in_weight)
    )
    grad_norm_in, gain_one = norm_backward(hidden, factor_one, gain_set[0], grad_normed)
    input_grad = grad_resid + grad_norm_in
    gains_grad = jnp.concatenate([gain_one, gain_two, gain_three, gain_four], 0)
    query_grad = matmul_tn(normed_low, grad_query)
    keyval_grad = matmul_tn(normed_low, grad_keyval_low)
    in_grad = matmul_tn(normed_low, grad_inner_low)
    attn_out_grad = matmul_tn(attn_low, grad_attn_proj_low)
    mamba_out_grad = matmul_tn(mixed_low, grad_mamba_proj_low)
    gate_grad = matmul_tn(ffn_low, grad_gate)
    up_grad = matmul_tn(ffn_low, grad_up)
    down_grad = matmul_tn(hidden_act, grad_ffn_low)
    ctx_sums = (
        lax.psum_scatter(query_grad, "ctx", scatter_dimension=0, tiled=True),
        lax.psum_scatter(keyval_grad, "ctx", scatter_dimension=0, tiled=True),
        lax.psum_scatter(attn_out_grad, "ctx", scatter_dimension=0, tiled=True),
        lax.psum_scatter(in_grad, "ctx", scatter_dimension=0, tiled=True),
        lax.psum_scatter(mamba_out_grad, "ctx", scatter_dimension=0, tiled=True),
        lax.psum_scatter(gate_grad, "ctx", scatter_dimension=0, tiled=True),
        lax.psum_scatter(up_grad, "ctx", scatter_dimension=0, tiled=True),
        lax.psum_scatter(down_grad, "ctx", scatter_dimension=0, tiled=True),
        lax.psum_scatter(xproj_grad, "ctx", scatter_dimension=0, tiled=True),
        lax.psum_scatter(dtproj_grad, "ctx", scatter_dimension=0, tiled=True),
        lax.psum_scatter(alog_grad, "ctx", scatter_dimension=0, tiled=True),
        lax.psum_scatter(taps_grad, "ctx", scatter_dimension=0, tiled=True),
        lax.psum_scatter(cbias_grad, "ctx", scatter_dimension=0, tiled=True),
        lax.psum_scatter(dtbias_grad, "ctx", scatter_dimension=0, tiled=True),
        lax.psum_scatter(skip_grad, "ctx", scatter_dimension=0, tiled=True),
        lax.psum_scatter(gains_grad, "ctx", scatter_dimension=0, tiled=True),
    )
    (
        query_sum,
        keyval_sum,
        attn_out_sum,
        in_sum,
        mamba_out_sum,
        gate_sum,
        up_sum,
        down_sum,
        xproj_sum,
        dtproj_sum,
        alog_sum,
        taps_sum,
        cbias_sum,
        dtbias_sum,
        skip_sum,
        gains_sum,
    ) = ctx_sums
    final_grads = (
        lax.psum_scatter(query_sum, "fsdp", scatter_dimension=1, tiled=True),
        lax.psum_scatter(keyval_sum, "fsdp", scatter_dimension=1, tiled=True),
        lax.psum_scatter(attn_out_sum, "fsdp", scatter_dimension=1, tiled=True),
        lax.psum_scatter(in_sum, "fsdp", scatter_dimension=1, tiled=True),
        lax.psum_scatter(mamba_out_sum, "fsdp", scatter_dimension=1, tiled=True),
        lax.psum_scatter(gate_sum, "fsdp", scatter_dimension=1, tiled=True),
        lax.psum_scatter(up_sum, "fsdp", scatter_dimension=1, tiled=True),
        lax.psum_scatter(down_sum, "fsdp", scatter_dimension=1, tiled=True),
        lax.psum_scatter(xproj_sum, "fsdp", scatter_dimension=0, tiled=True),
        lax.psum_scatter(dtproj_sum, "fsdp", scatter_dimension=0, tiled=True),
        lax.psum_scatter(alog_sum, "fsdp", scatter_dimension=0, tiled=True),
        lax.psum_scatter(taps_sum, "fsdp", scatter_dimension=0, tiled=True),
        lax.psum_scatter(cbias_sum, "fsdp", scatter_dimension=0, tiled=True),
        lax.psum_scatter(dtbias_sum, "fsdp", scatter_dimension=0, tiled=True),
        lax.psum_scatter(skip_sum, "fsdp", scatter_dimension=0, tiled=True),
        lax.psum_scatter(gains_sum, "fsdp", scatter_dimension=0, tiled=True),
    )
    return (
        loss,
        layer_out.astype(jnp.bfloat16)[None],
        input_grad[None],
        final_grads[0],
        final_grads[1],
        final_grads[2],
        final_grads[3],
        final_grads[4],
        final_grads[5],
        final_grads[6],
        final_grads[7],
        final_grads[8],
        final_grads[9],
        final_grads[10],
        final_grads[11],
        final_grads[12],
        final_grads[13],
        final_grads[14],
        final_grads[15],
    )


def solution(mesh):
    in_specs = (
        P("fsdp", "ctx", None),
        P("fsdp", "ctx", None),
        P("fsdp", "ctx", None),
        P("fsdp", "ctx"),
        P("ctx", "fsdp"),
        P("ctx", "fsdp"),
        P("ctx", "fsdp"),
        P("ctx", "fsdp"),
        P("ctx", "fsdp"),
        P("ctx", "fsdp"),
        P("ctx", "fsdp"),
        P("ctx", "fsdp"),
        P(("ctx", "fsdp"), None),
        P(("ctx", "fsdp"), None),
        P(("ctx", "fsdp"), None),
        P(("ctx", "fsdp"), None),
        P(("ctx", "fsdp")),
        P(("ctx", "fsdp")),
        P(("ctx", "fsdp")),
        P(("ctx", "fsdp")),
    )
    out_specs = (
        P(),
        P("fsdp", "ctx", None),
        P("fsdp", "ctx", None),
        P("ctx", "fsdp"),
        P("ctx", "fsdp"),
        P("ctx", "fsdp"),
        P("ctx", "fsdp"),
        P("ctx", "fsdp"),
        P("ctx", "fsdp"),
        P("ctx", "fsdp"),
        P("ctx", "fsdp"),
        P(("ctx", "fsdp"), None),
        P(("ctx", "fsdp"), None),
        P(("ctx", "fsdp"), None),
        P(("ctx", "fsdp"), None),
        P(("ctx", "fsdp")),
        P(("ctx", "fsdp")),
        P(("ctx", "fsdp")),
        P(("ctx", "fsdp")),
    )
    return jax.shard_map(body, mesh=mesh, in_specs=in_specs, out_specs=out_specs, check_vma=False)
```

profile of v0, /device:TPU:9, one launch (start us, length us, event | category | flops | bytes accessed | tf_op | source)
XLA Modules:
  0.0 5228.0 jit_solution(6158673546424899666)
XLA Ops:
  8.0 43.1 all-gather.56.cloned.1.call-done
  104.7 43.5 all-reduce.35
  180.7 25.8 all-gather.9
  213.6 25.6 all_gather.135
  297.8 275.8 %while.94 = (s32[]{:T(128)}, f32[3200,16]{0,1:T(8,128)}, f32[16,16,3200]{2,1,0:T(8,128)}, f32[3200,16]{0,1:T(8,128)S(1)}, f32[16,16,3200]{2,1,0:T(8,128)S(1)}, /...) while((s32[]{:T(128)}, f32[3200,16]{0,1:T(8,128)}, ...), condition=%wide.region_6.7_spmd.clone, body=%wide.region_5.6_spmd.clone.sunk | while | flops 3379218 | bytes 3075931 | solution.py:248
  754.6 29.7 while.95
  786.2 368.1 %while.93 = (s32[]{:T(128)}, f32[3200,16]{0,1:T(8,128)}, f32[16,3200,16]{1,2,0:T(8,128)}, f32[16,16,3200]{2,1,0:T(8,128)}, f32[16,16,3200]{2,1,0:T(8,128)}, /*in...) while((s32[]{:T(128)}, f32[3200,16]{0,1:T(8,128)}, ...), condition=%wide.region_26.27_spmd, body=%wide.region_9.26_spmd.sunk | while | flops 7372817 | bytes 6869273 | solution.py:268
  1236.8 41.6 all-reduce.32
  1335.7 140.9 %while.96 = (s32[]{:T(128)}, f32[3200,16]{0,1:T(8,128)}, f32[16,16,3200]{2,1,0:T(8,128)}, f32[3200,16]{0,1:T(8,128)S(1)}, f32[16,16,3200]{2,1,0:T(8,128)}, /*ind...) while((s32[]{:T(128)}, f32[3200,16]{0,1:T(8,128)}, ...), condition=%wide.region_38.39_spmd.clone, body=%wide.region_37.38_spmd.clone.sunk | while | flops 3328019 | bytes 1846815 | solution.py:349
  1479.4 23.2 all-gather.54.cloned.1.call-done
  1518.9 28.6 while.97
  1552.6 900.0 %while.98 = (s32[]{:T(128)}, f32[3200,16]{0,1:T(8,128)}, f32[3200,16]{0,1:T(8,128)}, f32[16,16,3200]{2,1,0:T(8,128)}, f32[16,16,3200]{2,1,0:T(8,128)}, /*index=5...) while((s32[]{:T(128)}, f32[3200,16]{0,1:T(8,128)}, ...), condition=%wide.region_106.107_spmd.clone, body=%wide.region_41.106_spmd.clone.sunk | while | flops 24165904 | bytes 28618636 | solution.py:394
  2474.7 22.3 fusion.263
  2496.9 29.0 fusion.265
  2660.7 25.1 collective-permute-done.5
  2687.9 53.8 %collective-permute-done.7 = f32[256,640]{0,1:T(8,128)S(1)} collective-permute-done((f32[256,640]{0,1:T(8,128)S(1)}, f32[256,640]{0,1:T(8,128)S(1)}, u32[]{:S(2)}, u32[]{:S(2)}) %collective-permute-start.7) | collective-permute-done | bytes 655392 | tf_op jit(solution)/shard_map/ppermute | solution.py:20
  2799.8 207.6 %reduce-scatter.60.cloned.1.call-done = f32[400,1600]{1,0:T(8,128)} async-done(((f32[3200,1600]{1,0:T(8,128)}), f32[400,1600]{1,0:T(8,128)}) %reduce-scatter.60.cloned.1.call-update) | async-done | bytes 2560016 | tf_op jit(solution)/shard_map/reduce_scatter | solution.py:469
  3011.8 398.8 %reduce-scatter.96.cloned.1.call-done = f32[200,5504]{1,0:T(8,128)} async-done(((f32[1600,5504]{1,0:T(8,128)}), f32[200,5504]{1,0:T(8,128)}) %reduce-scatter.96.cloned.1.call-update) | async-done | bytes 4403216
  3416.6 416.7 %reduce-scatter.98.cloned.1.call-done = f32[200,5504]{1,0:T(8,128)} async-done(((f32[1600,5504]{1,0:T(8,128)}), f32[200,5504]{1,0:T(8,128)}) %reduce-scatter.98.cloned.1.call-update) | async-done | bytes 4403216
  3839.2 401.9 %reduce-scatter.94.cloned.1.call-done = f32[200,6400]{1,0:T(8,128)} async-done(((f32[1600,6400]{1,0:T(8,128)}), f32[200,6400]{1,0:T(8,128)}) %reduce-scatter.94.cloned.1.call-update) | async-done | bytes 5120016
  4247.6 43.4 reduce-scatter.90.cloned.1.call-done
  4293.5 353.8 %reduce-scatter.62.cloned.1.call-done = f32[688,1600]{1,0:T(8,128)} async-done(((f32[5504,1600]{1,0:T(8,128)}), f32[688,1600]{1,0:T(8,128)}) %reduce-scatter.62.cloned.1.call-update) | async-done | bytes 4403216 | tf_op jit(solution)/shard_map/reduce_scatter | solution.py:472
  4678.1 23.6 all-reduce.33
  4748.2 25.9 fusion
  4800.1 33.4 reduce-scatter.70.cloned.1.call-done
  4835.4 32.8 reduce-scatter.66.cloned.1.call-done
  4870.1 46.5 reduce-scatter.74.cloned.1.call-done
  4918.9 65.6 %reduce-scatter.76.cloned.1.call-done = f32[1376,200]{1,0:T(8,128)} async-done(((f32[5504,200]{1,0:T(8,128)}), f32[1376,200]{1,0:T(8,128)}) %reduce-scatter.76.cloned.1.call-update) | async-done | bytes 1100816
  4987.3 65.4 %reduce-scatter.78.cloned.1.call-done = f32[1376,200]{1,0:T(8,128)} async-done(((f32[5504,200]{1,0:T(8,128)}), f32[1376,200]{1,0:T(8,128)}) %reduce-scatter.78.cloned.1.call-update) | async-done | bytes 1100816
  5055.4 73.0 %reduce-scatter.72.cloned.1.call-done = f32[1600,200]{1,0:T(8,128)} async-done(((f32[6400,200]{1,0:T(8,128)}), f32[1600,200]{1,0:T(8,128)}) %reduce-scatter.72.cloned.1.call-update) | async-done | bytes 1280016
  5131.3 25.9 reduce-scatter.68.cloned.1.call-done
  5157.3 62.3 %reduce-scatter.80.cloned.1.call-done = f32[400,688]{1,0:T(8,128)} async-done(((f32[1600,688]{1,0:T(8,128)}), f32[400,688]{1,0:T(8,128)}) %reduce-scatter.80.cloned.1.call-update) | async-done | bytes 1100816
  (4080 shorter events, 2577.7 us)
Async XLA Ops:
  57.4 517.9 %all-gather.38.cloned.1.call-start = ((), (), s32[]{:S(2)}) async-start(), calls=%async_computation.24 | async-start | bytes 2048000 | tf_op jit(solution)/shard_map/all_gather | solution.py:121
  58.4 520.5 %all-gather.58.cloned.1.call-start = ((), (), s32[]{:S(2)}) async-start(), calls=%async_computation.37 | async-start | bytes 2816000 | tf_op jit(solution)/shard_map/all_gather | solution.py:122
  59.0 540.7 %all-gather.60.cloned.1.call-start = ((), (), s32[]{:S(2)}) async-start(), calls=%async_computation.38 | async-start | bytes 2816000 | tf_op jit(solution)/shard_map/all_gather | solution.py:123
  59.5 550.8 %all-gather.30.cloned.1.call-start = ((), (), s32[]{:S(2)}) async-start(), calls=%async_computation.20 | async-start | bytes 2304000 | tf_op jit(solution)/shard_map/all_gather | solution.py:153
  67.7 554.7 %all-gather.46.cloned.1.call-start = ((), (), s32[]{:S(2)}) async-start(), calls=%async_computation.28 | async-start | bytes 3072000 | tf_op jit(solution)/shard_map/all_gather | solution.py:124
  68.4 626.2 %all-gather.32.cloned.1.call-start = ((), (), s32[]{:S(2)}) async-start(), calls=%async_computation.21 | async-start | bytes 5990400 | tf_op jit(solution)/shard_map/all_gather | solution.py:152
  80.2 661.6 %all-gather.34.cloned.1.call-start = ((), (), s32[]{:S(2)}) async-start(), calls=%async_computation.22 | async-start | bytes 5990400 | tf_op jit(solution)/shard_map/all_gather | solution.py:154
  91.6 657.2 %all-gather.52.cloned.1.call-start = ((), (), s32[]{:S(2)}) async-start(), calls=%async_computation.34 | async-start | bytes 1843200 | tf_op jit(solution)/shard_map/all_gather | solution.py:25
  575.2 583.9 %all-gather.40.cloned.1.call-start = ((), (), s32[]{:S(2)}) async-start(), calls=%async_computation.25 | async-start | bytes 11980800 | tf_op jit(solution)/shard_map/all_gather | solution.py:156
  578.8 593.1 %all-gather.42.cloned.1.call-start = ((), (), s32[]{:S(2)}) async-start(), calls=%async_computation.26 | async-start | bytes 19814400 | tf_op jit(solution)/shard_map/all_gather | solution.py:157
  587.9 597.6 %all-gather.44.cloned.1.call-start = ((), (), s32[]{:S(2)}) async-start(), calls=%async_computation.27 | async-start | bytes 19814400 | tf_op jit(solution)/shard_map/all_gather | solution.py:158
  608.7 613.7 %all-gather.48.cloned.1.call-start = ((), (), s32[]{:S(2)}) async-start(), calls=%async_computation.29 | async-start | bytes 20606976 | tf_op jit(solution)/shard_map/all_gather | solution.py:159
  626.8 875.7 %all-gather.54.cloned.1.call-start = ((), (), s32[]{:S(2)}) async-start(), calls=%async_computation.35 | async-start | bytes 1843200 | tf_op jit(solution)/shard_map/all_gather | solution.py:25
  1476.6 1294.7 %reduce-scatter.82.cloned.1.call-start = ((), (), s32[]{:S(2)}) async-start(), calls=%async_computation.47 | async-start | bytes 3686400
  2541.4 466.0 %reduce-scatter.60.cloned.1.call-start = ((), (), s32[]{:S(2)}) async-start(), calls=%async_computation.30 | async-start | bytes 23961600 | tf_op jit(solution)/shard_map/reduce_scatter | solution.py:469
  2553.5 857.2 %reduce-scatter.96.cloned.1.call-start = ((), (), s32[]{:S(2)}) async-start(), calls=%async_computation.55 | async-start | bytes 39628800
  2570.6 1262.7 %reduce-scatter.98.cloned.1.call-start = ((), (), s32[]{:S(2)}) async-start(), calls=%async_computation.56 | async-start | bytes 39628800
  2586.6 1654.5 %reduce-scatter.94.cloned.1.call-start = ((), (), s32[]{:S(2)}) async-start(), calls=%async_computation.54 | async-start | bytes 46080000
  2625.1 1665.9 %reduce-scatter.90.cloned.1.call-start = ((), (), s32[]{:S(2)}) async-start(), calls=%async_computation.52 | async-start | bytes 4608000
  2747.0 1900.3 %reduce-scatter.62.cloned.1.call-start = ((), (), s32[]{:S(2)}) async-start(), calls=%async_computation.31 | async-start | bytes 41213952 | tf_op jit(solution)/shard_map/reduce_scatter | solution.py:472
  2765.0 1940.0 %reduce-scatter.86.cloned.1.call-start = ((), (), s32[]{:S(2)}) async-start(), calls=%async_computation.49 | async-start | bytes 1843200
  2767.6 1945.3 %reduce-scatter.84.cloned.1.call-start = ((), (), s32[]{:S(2)}) async-start(), calls=%async_computation.48 | async-start | bytes 1843200
  2769.4 1978.8 %reduce-scatter.64.cloned.1.call-start = ((), (), s32[]{:S(2)}) async-start(), calls=%async_computation.32 | async-start | bytes 1843200 | tf_op jit(solution)/shard_map/reduce_scatter | solution.py:474
  2771.3 2027.2 %all-reduce.39.cloned.1.call-start = ((), (), s32[]{:S(2)}) async-start(), calls=%async_computation.50 | async-start | bytes 557056
  2773.3 2060.2 %reduce-scatter.70.cloned.1.call-start = ((), (), s32[]{:S(2)}) async-start(), calls=%async_computation.41 | async-start | bytes 2048000
  2776.3 2091.8 %reduce-scatter.66.cloned.1.call-start = ((), (), s32[]{:S(2)}) async-start(), calls=%async_computation.39 | async-start | bytes 2048000
  2799.7 2116.8 %reduce-scatter.74.cloned.1.call-start = ((), (), s32[]{:S(2)}) async-start(), calls=%async_computation.43 | async-start | bytes 4096000
  3011.8 1972.7 %reduce-scatter.76.cloned.1.call-start = ((), (), s32[]{:S(2)}) async-start(), calls=%async_computation.44 | async-start | bytes 7045120
  3416.5 1636.1 %reduce-scatter.78.cloned.1.call-start = ((), (), s32[]{:S(2)}) async-start(), calls=%async_computation.45 | async-start | bytes 7045120
  3839.2 1289.2 %reduce-scatter.72.cloned.1.call-start = ((), (), s32[]{:S(2)}) async-start(), calls=%async_computation.42 | async-start | bytes 8192000
  4247.5 909.7 %reduce-scatter.68.cloned.1.call-start = ((), (), s32[]{:S(2)}) async-start(), calls=%async_computation.40 | async-start | bytes 819200
  4293.2 926.4 %reduce-scatter.80.cloned.1.call-start = ((), (), s32[]{:S(2)}) async-start(), calls=%async_computation.46 | async-start | bytes 6144000
  (1027 other events, 16031.9 us)
Sparse Core Ops, SparseCore 0:
  9.9 41.1 all-gather.55
  57.5 195.8 all-gather.35
  255.8 32.3 all-gather.37
  289.8 36.5 all-gather.57
  328.2 36.5 all-gather.59
  397.9 37.3 all-gather.45
  437.5 55.3 all-gather.31
  495.1 55.4 all-gather.33
  599.2 29.2 all-gather.49
  630.5 110.0 all-gather.39
  742.2 158.8 all-gather.41
  902.6 156.1 all-gather.43
  1060.3 161.9 all-gather.47
  2462.5 38.8 reduce-scatter.81
  2503.7 110.5 reduce-scatter.91
  2616.7 179.8 reduce-scatter.87
  2799.0 208.3 reduce-scatter.59
  3009.8 400.7 reduce-scatter.95
  3413.1 420.0 reduce-scatter.97
  3835.8 405.2 reduce-scatter.93
  4243.3 47.6 reduce-scatter.89
  4293.5 353.7 reduce-scatter.61
  4680.2 32.6 reduce-scatter.83
  4715.2 32.9 reduce-scatter.63
  4751.8 46.6 all-reduce.38
  4801.6 31.8 reduce-scatter.69
  4836.7 31.3 reduce-scatter.65
  4871.5 45.0 reduce-scatter.73
  4919.8 64.6 reduce-scatter.75
  4987.9 64.6 reduce-scatter.77
  5055.9 72.3 reduce-scatter.71
  5160.7 58.8 reduce-scatter.79
  (5 shorter events, 132.2 us)
where the time goes:
time: 5270 us; the launch traced here: 5230 us
  waiting for transfers between devices  2530 us (48%)
  local copies, waits for them, and re-layouts  1030 us (20%)
  other arithmetic  952 us (18%)
  matrix products  344 us (7%)
  blocking collectives  296 us (6%)
    unnamed x56, waiting for transfers between devices  1710 us
    reduce_scatter x1, waiting for transfers between devices, body(): lax.psum_scatter(down_grad, 'ctx', scatter_dimension=0, tiled=True)  354 us
    reduce_scatter x1, waiting for transfers between devices, body(): lax.psum_scatter(mamba_out_grad, 'ctx', scatter_dimension=0, tiled=True)  208 us
    another operation x272, local copies, waits for them, and re-layouts, chain_full(): return (running, (first_state, jnp.stack(out_rows)))  168 us
    mul x256, other arithmetic, chain_local(): step_blk[position] * input_blk[position]  155 us
    reduce_sum x64, other arithmetic, adjoint_full(): jnp.sum(through * a_mat, axis=1) + input_blk[position] * along_b  145 us
    ppermute x10, waiting for transfers between devices, passed_along(): return lax.ppermute(block, axis, route)  143 us
    unnamed x5, blocking collectives  114 us

commit v1 on v0

v1 whole, which is shorter than its diff:
```python
from typing import Any, NamedTuple

import jax
import jax.numpy as jnp
from jax import lax
from jax.experimental import pallas as pl
from jax.experimental.pallas import tpu as pltpu
from jax.sharding import PartitionSpec as P

D = 1600
H = 25
HD = 64
KVH = 5
WINDOW = 1024
DI = 3200
DS = 16
KC = 4
R = 100
LOG2E = 1.4426950408889634
BF = jnp.bfloat16
F32 = jnp.float32

TC = 128
LW = 512

def fold_rows(parts):
    row = lax.broadcasted_iota(jnp.int32, parts[0].shape, 0)
    for shift in (1, 2, 4):
        keep = (row & shift) == 0
        merged = []
        for first, second in zip(parts[0::2], parts[1::2]):
            stay = jnp.where(keep, first, second)
            move = jnp.where(keep, second, first)
            merged.append(stay + pltpu.roll(move, shift, 0))
        parts = merged
    return parts[0]

def spread(column, lanes):
    return jnp.concatenate([column] * (lanes // 128), 1)

def ssm_forward_kernel(step_ref, u_ref, b_ref, c_ref, rate_ref, y_ref, start_ref, state):
    @pl.when(pl.program_id(0) == 0)
    def _():
        state[...] = jnp.zeros_like(state)
    start_ref[0] = state[...]
    width = state.shape[1]
    lw = min(LW, width)
    for low in range(0, width, lw):
        lanes = slice(low, low + lw)
        rate = rate_ref[:, lanes]

        def group(index, running):
            row = pl.multiple_of(index * 8, 8)
            steps = step_ref[pl.ds(row, 8), lanes]
            drive = steps * u_ref[pl.ds(row, 8), lanes]
            sums = []
            for k in range(8):
                b_now, c_now = spread(b_ref[row + k], lw), spread(c_ref[row + k], lw)
                running = jnp.exp2(rate * steps[k : k + 1]) * running + b_now * drive[k : k + 1]
                seen = running * c_now
                sums.append(seen[:8] + seen[8:])
            y_ref[pl.ds(row, 8), lanes] = fold_rows(sums)
            return running

        state[:, lanes] = lax.fori_loop(0, TC // 8, group, state[:, lanes])

def ssm_forward(step, u, b_t, c_t, rate, parcels, number):
    length, width = step.shape
    states = rate.shape[0]
    count = length // TC
    rows = pl.BlockSpec((TC, width), lambda i: (i, 0))
    cols = pl.BlockSpec((TC, states, 128), lambda i: (i, 0, 0))
    return talk(
        ssm_forward_kernel,
        [step, u, b_t, c_t, rate],
        [rows, rows, cols, cols, pl.BlockSpec((states, width), lambda i: (0, 0))],
        [jax.ShapeDtypeStruct((length, width), jnp.float32), jax.ShapeDtypeStruct((count, states, width), jnp.float32)],
        [rows, pl.BlockSpec((1, states, width), lambda i: (i, 0, 0))],
        [pltpu.VMEM((states, width), jnp.float32)],
        parcels,
        number,
        32 << 20,
        "ssm_forward",
        steps=count,
    )

def lane_sums(values):
    high = values.astype(jnp.bfloat16)
    low = (values - high.astype(jnp.float32)).astype(jnp.bfloat16)
    ones = jnp.ones((8, values.shape[1]), jnp.bfloat16)
    dims = (((1,), (1,)), ((), ()))
    return lax.dot_general(ones, high, dims, preferred_element_type=jnp.float32) + lax.dot_general(
        ones, low, dims, preferred_element_type=jnp.float32
    )

def ssm_backward_kernel(
    step_ref, u_ref, dy_ref, b_ref, c_ref, rate_ref, amat_ref, start_ref,
    dstep_ref, along_ref, db_ref, dc_ref, da_ref,
    adjoint, history, decays, b_part, c_part,
):
    states, width = adjoint.shape
    lw = min(LW, width)

    @pl.when(pl.program_id(0) == 0)
    def _():
        adjoint[...] = jnp.zeros_like(adjoint)
        da_ref[...] = jnp.zeros_like(da_ref)

    for low in range(0, width, lw):
        lanes = slice(low, low + lw)
        rate = rate_ref[:, lanes]
        amat = amat_ref[:, lanes]

        def replay(index, running):
            row = pl.multiple_of(index * 8, 8)
            steps = step_ref[pl.ds(row, 8), lanes]
            drive = steps * u_ref[pl.ds(row, 8), lanes]
            for k in range(8):
                decay = jnp.exp2(rate * steps[k : k + 1])
                history[row + k] = running
                decays[row + k] = decay
                running = decay * running + spread(b_ref[row + k], lw) * drive[k : k + 1]
            return running

        final = lax.fori_loop(0, TC // 8, replay, start_ref[0, :, lanes])

        def group(index, carry):
            lam, grown, after = carry
            row = pl.multiple_of(TC - 8 - index * 8, 8)
            steps = step_ref[pl.ds(row, 8), lanes]
            inputs = u_ref[pl.ds(row, 8), lanes]
            drive = steps * inputs
            dys = dy_ref[pl.ds(row, 8), lanes]
            through_sums = [None] * 8
            along_sums = [None] * 8
            for k in reversed(range(8)):
                before = history[row + k]
                lam = lam + spread(c_ref[row + k], lw) * dys[k : k + 1]
                passed = lam * decays[row + k]
                through = passed * before
                grown = grown + through * steps[k : k + 1]
                scaled = through * amat
                through_sums[k] = scaled[:8] + scaled[8:]
                along = lam * spread(b_ref[row + k], lw)
                along_sums[k] = along[:8] + along[8:]
                b_term = lam * drive[k : k + 1]
                c_term = after * dys[k : k + 1]
                b_sum = b_term[:, :128]
                c_sum = c_term[:, :128]
                for more in range(128, lw, 128):
                    b_sum = b_sum + b_term[:, more : more + 128]
                    c_sum = c_sum + c_term[:, more : more + 128]
                place = pl.ds(pl.multiple_of((row + k) * states, states), states)
                if low == 0:
                    b_part[place, :] = b_sum
                    c_part[place, :] = c_sum
                else:
                    b_part[place, :] += b_sum
                    c_part[place, :] += c_sum
                lam = passed
                after = before
            along_all = fold_rows(along_sums)
            along_ref[pl.ds(row, 8), lanes] = along_all
            dstep_ref[pl.ds(row, 8), lanes] = fold_rows(through_sums) + inputs * along_all
            return lam, grown, after

        lam, grown, _ = lax.fori_loop(0, TC // 8, group, (adjoint[:, lanes], da_ref[:, lanes], final))
        adjoint[:, lanes] = lam
        da_ref[:, lanes] = grown
    db_ref[0] = lane_sums(b_part[...])
    dc_ref[0] = lane_sums(c_part[...])

def ssm_backward(step, u, dy, b_t, c_t, rate, amat, starts, parcels, number):
    length, width = step.shape
    states = rate.shape[0]
    count = length // TC
    last = count - 1
    lw = min(LW, width)
    rows = pl.BlockSpec((TC, width), lambda i: (last - i, 0))
    cols = pl.BlockSpec((TC, states, 128), lambda i: (last - i, 0, 0))
    whole = pl.BlockSpec((states, width), lambda i: (0, 0))
    sums = pl.BlockSpec((1, 8, TC * states), lambda i: (last - i, 0, 0))
    (dstep, along, db, dc, da), extra = talk(
        ssm_backward_kernel,
        [step, u, dy, b_t, c_t, rate, amat, starts],
        [rows, rows, rows, cols, cols, whole, whole, pl.BlockSpec((1, states, width), lambda i: (last - i, 0, 0))],
        [
            jax.ShapeDtypeStruct((length, width), jnp.float32),
            jax.ShapeDtypeStruct((length, width), jnp.float32),
            jax.ShapeDtypeStruct((count, 8, TC * states), jnp.float32),
            jax.ShapeDtypeStruct((count, 8, TC * states), jnp.float32),
            jax.ShapeDtypeStruct((states, width), jnp.float32),
        ],
        [rows, rows, sums, sums, whole],
        [
            pltpu.VMEM((states, width), jnp.float32),
            pltpu.VMEM((TC, states, lw), jnp.float32),
            pltpu.VMEM((TC, states, lw), jnp.float32),
            pltpu.VMEM((TC * states, 128), jnp.float32),
            pltpu.VMEM((TC * states, 128), jnp.float32),
        ],
        parcels,
        number,
        40 << 20,
        "ssm_backward",
        steps=count,
    )
    return dstep, along, db[:, 0].reshape(length, states), dc[:, 0].reshape(length, states), da, extra

QB = 256

def dot_nn(a, b):
    return lax.dot_general(a, b, (((1,), (0,)), ((), ())), preferred_element_type=jnp.float32)

def dot_nt(a, b):
    return lax.dot_general(a, b, (((1,), (1,)), ((), ())), preferred_element_type=jnp.float32)

def fill_bias(bias, first_key):
    span, queries = bias.shape
    key = first_key + lax.broadcasted_iota(jnp.int32, bias.shape, 0)
    query = pl.program_id(0) * queries + lax.broadcasted_iota(jnp.int32, bias.shape, 1)
    gap = query - key
    bias[...] = jnp.where((gap >= 0) & (gap < WINDOW), 0.0, -1e30)

def first_key_of(span):
    return pl.multiple_of(jnp.maximum(pl.program_id(0) * QB - (span - QB), 0), QB)

def slot_of(heads, j):
    first = heads * lax.axis_index("ctx")
    group = H // KVH
    return lax.div(jnp.minimum(first + j, H - 1), group) - lax.div(jnp.minimum(first, H - 1), group)

def attend_kernel(q_ref, k_ref, v_ref, o_ref, lse_ref, bias):
    span = bias.shape[0]
    first = first_key_of(span)
    fill_bias(bias, first)
    lse_ref[...] = jnp.zeros_like(lse_ref)

    def head(j, _):
        slot = slot_of(q_ref.shape[0] // HD, j)
        feats = pl.ds(pl.multiple_of(j * HD, HD), HD)
        scores = dot_nn(k_ref[slot, pl.ds(first, span), :], q_ref[feats, :]) + bias[...]
        top = jnp.max(scores, axis=0, keepdims=True)
        grown = jnp.exp(scores - top)
        total = jnp.sum(grown, axis=0, keepdims=True)
        probs = (grown * (1.0 / total)).astype(jnp.bfloat16)
        o_ref[feats, :] = dot_nn(v_ref[slot, :, pl.ds(first, span)], probs).astype(o_ref.dtype)
        lse_ref[pl.ds(j, 1), :] = top + jnp.log(total)
        return 0

    lax.fori_loop(0, q_ref.shape[0] // HD, head, 0)

def attend(q_t, k, v_t, parcels, number):
    feats, length = q_t.shape
    span = min(WINDOW + QB, length)
    tokens = pl.BlockSpec((feats, QB), lambda i: (0, i))
    whole = lambda a: pl.BlockSpec(a.shape, lambda i: (0,) * a.ndim)
    return talk(
        attend_kernel,
        [q_t, k, v_t],
        [tokens, whole(k), whole(v_t)],
        [jax.ShapeDtypeStruct((feats, length), jnp.bfloat16), jax.ShapeDtypeStruct((8, length), jnp.float32)],
        [tokens, pl.BlockSpec((8, QB), lambda i: (0, i))],
        [pltpu.VMEM((span, QB), jnp.float32)],
        parcels,
        number,
        40 << 20,
        "attend",
        steps=length // QB,
    )

def attend_back_kernel(q_ref, do_ref, k_ref, kt_ref, v_ref, lse_ref, dq_ref, dk_ref, dv_ref, bias):
    span = bias.shape[0]
    first = first_key_of(span)
    fill_bias(bias, first)

    @pl.when(pl.program_id(0) == 0)
    def _():
        dk_ref[...] = jnp.zeros_like(dk_ref)
        dv_ref[...] = jnp.zeros_like(dv_ref)

    def head(j, _):
        slot = slot_of(q_ref.shape[0] // HD, j)
        feats = pl.ds(pl.multiple_of(j * HD, HD), HD)
        keys = pl.ds(first, span)
        query = q_ref[feats, :]
        grad = do_ref[feats, :]
        probs = jnp.exp(dot_nn(k_ref[slot, keys, :], query) + bias[...] - lse_ref[pl.ds(j, 1), :])
        slopes = dot_nn(v_ref[slot, keys, :], grad)
        inner = jnp.sum(probs * slopes, axis=0, keepdims=True)
        ds = (probs * (slopes - inner)).astype(jnp.bfloat16)
        dq_ref[feats, :] = (dot_nn(kt_ref[slot, :, keys], ds) * HD**-0.5).astype(dq_ref.dtype)
        dk_ref[slot, keys, :] += dot_nt(ds, query)
        dv_ref[slot, keys, :] += dot_nt(probs.astype(jnp.bfloat16), grad)
        return 0

    lax.fori_loop(0, q_ref.shape[0] // HD, head, 0)

def attend_back(q_t, do_t, k, k_t, v, lse, parcels, number):
    feats, length = q_t.shape
    span = min(WINDOW + QB, length)
    tokens = pl.BlockSpec((feats, QB), lambda i: (0, i))
    whole = lambda a: pl.BlockSpec(a.shape, lambda i: (0,) * a.ndim)
    return talk(
        attend_back_kernel,
        [q_t, do_t, k, k_t, v, lse],
        [tokens, tokens, whole(k), whole(k_t), whole(v), pl.BlockSpec((8, QB), lambda i: (0, i))],
        [
            jax.ShapeDtypeStruct((feats, length), jnp.bfloat16),
            jax.ShapeDtypeStruct(k.shape, jnp.float32),
            jax.ShapeDtypeStruct(k.shape, jnp.float32),
        ],
        [tokens, whole(k), whole(k)],
        [pltpu.VMEM((span, QB), jnp.float32)],
        parcels,
        number,
        40 << 20,
        "attend_back",
        steps=length // QB,
    )


def contract(left, right, left_dim, right_dim):
    return lax.dot_general(left, right, (((left_dim,), (right_dim,)), ((), ())), preferred_element_type=F32)


def matmul(left, right):
    return contract(left, right, 1, 0)


def matmul_tn(left, right):
    return contract(left, right, 0, 0)


def matmul_nt(left, right):
    return contract(left, right, 1, 1)


def norm_forward(values, gain_vec):
    factor = lax.rsqrt(jnp.mean(values * values, axis=-1, keepdims=True) + 1e-06)
    return (values * factor * gain_vec, factor)


def norm_backward(values, factor, gain_vec, grad_out):
    weighted = grad_out * gain_vec
    inner_mean = jnp.mean(weighted * values, axis=-1, keepdims=True)
    grad_in = factor * weighted - values * (factor * factor * factor) * inner_mean
    return (grad_in, jnp.sum(grad_out * values * factor, axis=0))


def silu_slope(values):
    sigmoid_v = jax.nn.sigmoid(values)
    return sigmoid_v * (1.0 + values * (1.0 - sigmoid_v))


def pad_to(array, size, dim):
    widths = [(0, 0)] * array.ndim
    widths[dim] = (0, size - array.shape[dim])
    return jnp.pad(array, widths)


MESH = pl.DeviceIdType.MESH


BULK = 9


class Parcel(NamedTuple):
    source: Any
    kind: str
    axis: str
    group: int
    pick: Any = None


class Line(NamedTuple):
    size: int
    me: Any
    device: Any


def line_of(axis, sizes):
    n, m = sizes
    if axis == "ctx":
        return Line(n, lax.axis_index("ctx"), lambda peer: {"ctx": peer})
    me = lax.axis_index("fsdp")
    if axis == "fsdp":
        return Line(m, me, lambda peer: {"fsdp": peer})
    half = m // 2
    own = lax.rem(me, half)
    return Line(half, own, lambda peer: {"fsdp": me - own + peer})


def parcel_shapes(parcels, sizes):
    n, m = sizes
    sizes_of = {"ctx": n, "fsdp": m, "pair": m // 2}
    shapes = []
    for parcel in parcels:
        source = shapes[parcel.source] if isinstance(parcel.source, int) else parcel.source
        size = sizes_of[parcel.axis]
        shape = source.shape
        if parcel.kind == "gather":
            shape = (size,) + shape
        elif parcel.kind == "lanes":
            shape = shape[:-1] + (size * shape[-1],)
        elif parcel.pick is not None:
            shape = (size,) + parcel.pick(None, None, shape)
        shapes.append(jax.ShapeDtypeStruct(shape, source.dtype))
    return shapes


class Mail:
    def __init__(self, parcels, sizes, in_refs, out_refs, sems):
        self.parcels, self.sizes, self.outs = parcels, sizes, out_refs
        self.send, self.recv, self.local = sems if sems else (None,) * 3
        given = iter(in_refs)
        self.sources = [out_refs[p.source] if isinstance(p.source, int) else next(given) for p in parcels]
        self.base = []
        total = 0
        for p in parcels:
            self.base.append(total)
            total += {"ctx": sizes[0], "fsdp": sizes[1], "pair": sizes[1] // 2}[p.axis]

    def parts(self, number, line, peer, owner):
        parcel, source, out = self.parcels[number], self.sources[number], self.outs[number]
        if parcel.kind == "swap":
            source = parcel.pick(source, peer, None) if parcel.pick else source.at[peer]
        if parcel.kind == "lanes":
            lanes = self.sources[number].shape[-1]
            spot = pl.ds(pl.multiple_of(owner * lanes, lanes), lanes)
            return source, out.at[(slice(None),) * (len(out.shape) - 1) + (spot,)]
        return source, out.at[owner]

    def copies(self, group, incoming):
        for number, parcel in enumerate(self.parcels):
            if parcel.group != group:
                continue
            line = line_of(parcel.axis, self.sizes)
            for d in range(1, line.size):
                peer = lax.rem(line.me + d, line.size)
                owner = lax.rem(line.me + line.size - d, line.size) if incoming else line.me
                source, target = self.parts(number, line, peer, owner)
                spot = self.base[number] + d
                yield pltpu.make_async_remote_copy(
                    src_ref=source,
                    dst_ref=target,
                    send_sem=self.send.at[spot],
                    recv_sem=self.recv.at[spot],
                    device_id=line.device(peer),
                    device_id_type=MESH,
                )

    def kept(self, group):
        for number, parcel in enumerate(self.parcels):
            if parcel.group == group:
                line = line_of(parcel.axis, self.sizes)
                source, target = self.parts(number, line, line.me, line.me)
                yield pltpu.make_async_copy(source, target, self.local.at[number])

    def start(self, group):
        for copy in self.copies(group, False):
            copy.start()
        for copy in self.kept(group):
            copy.start()

    def wait(self, group):
        for copy in self.copies(group, True):
            copy.wait_recv()
        for copy in self.copies(group, False):
            copy.wait_send()
        for copy in self.kept(group):
            copy.wait()

    def step(self, done, begun):
        if self.has(done):
            self.wait(done)
            if self.has(begun):
                self.start(begun)

    def begin(self):
        for group in (0, BULK):
            if self.has(group):
                self.start(group)

    def end(self, last):
        for group in (last, BULK):
            if self.has(group):
                self.wait(group)

    def has(self, group):
        return any(p.group == group for p in self.parcels)


def ctx_copy(source, target, send, recv, device):
    return pltpu.make_async_remote_copy(
        src_ref=source, dst_ref=target, send_sem=send, recv_sem=recv, device_id={"ctx": device}, device_id_type=MESH
    )


def line_place(n):
    me = lax.axis_index("ctx")
    core = lax.rem(me, 2)
    return me, core, me // 2, me + 1 - 2 * core


def greet(sizes, everyone, fsdp):
    n, m = sizes
    chips = n // 2
    me, core, chip, sibling = line_place(n)
    barrier = pltpu.get_barrier_semaphore()

    def hello(device):
        pl.semaphore_signal(barrier, inc=1, device_id=device, device_id_type=MESH)

    expected = 0
    if everyone:
        for d in range(1, n):
            hello({"ctx": lax.rem(me + d, n)})
        expected = n - 1
    else:
        hello({"ctx": sibling})

        @pl.when(chip > 0)
        def _():
            hello({"ctx": me - 2})

        @pl.when(chip < chips - 1)
        def _():
            hello({"ctx": me + 2})

        expected = 3 - (chip == 0).astype(jnp.int32) - (chip == chips - 1).astype(jnp.int32)
    if fsdp:
        own = lax.axis_index("fsdp")
        for d in range(1, m):
            hello({"fsdp": lax.rem(own + d, m)})
        expected = expected + m - 1
    pl.semaphore_wait(barrier, expected)


def talk(core_kernel, args, in_specs, out_shapes, out_specs, scratch, parcels, number, vmem, name, everyone=False, steps=0):
    sizes = (lax.axis_size("ctx"), lax.axis_size("fsdp"))
    arrays = [p.source for p in parcels if not isinstance(p.source, int)]
    shapes = parcel_shapes(parcels, sizes)
    total = sum({"ctx": sizes[0], "fsdp": sizes[1], "pair": sizes[1] // 2}[p.axis] for p in parcels)
    everyone = everyone or any(p.axis == "ctx" for p in parcels)
    fsdp = any(p.axis != "ctx" for p in parcels)
    anywhere = pl.BlockSpec(memory_space=pl.ANY)
    sems = []
    if parcels:
        sems = [pltpu.SemaphoreType.DMA((total,)), pltpu.SemaphoreType.DMA((total,)), pltpu.SemaphoreType.DMA((len(parcels),))]

    def kernel(*refs):
        refs = list(refs)
        take = lambda count: [refs.pop(0) for _ in range(count)]
        ins, mail_in, outs, mail_out = take(len(args)), take(len(arrays)), take(len(out_shapes)), take(len(shapes))
        own = take(len(scratch))
        mail = Mail(parcels, sizes, mail_in, mail_out, refs)
        if not steps:
            greet(sizes, everyone, fsdp)
            core_kernel(sizes[0], ins, outs, own, mail)
            return

        @pl.when(pl.program_id(0) == 0)
        def _():
            greet(sizes, everyone, fsdp)
            mail.begin()

        core_kernel(*ins, *outs, *own)

        @pl.when(pl.program_id(0) == steps - 1)
        def _():
            mail.end(0)

    results = pl.pallas_call(
        kernel,
        grid=(steps,) if steps else (),
        out_shape=list(out_shapes) + shapes,
        in_specs=list(in_specs) + [anywhere] * len(arrays),
        out_specs=list(out_specs) + [anywhere] * len(shapes),
        scratch_shapes=list(scratch) + sems,
        compiler_params=pltpu.CompilerParams(collective_id=number, has_side_effects=True, vmem_limit_bytes=vmem),
        name=name,
    )(*args, *arrays)
    return results[: len(out_shapes)], results[len(out_shapes) :]


def share_core(n, xs, outs, sems, mail):
    chips = n // 2
    me, core, chip, sibling = line_place(n)
    send, recv, side_send, side_recv, local = sems
    several = range(len(xs))
    ways = ((0, 1), (1, -1))

    def spot(hop, sign):
        held = chip - sign * hop
        onward = chip + sign
        have = (held >= 0) & (held < chips)
        return 2 * held, have, have & (onward >= 0) & (onward < chips), 2 * onward + core

    def line_copy(a, way, hop, source, block, device):
        return ctx_copy(source, outs[a].at[block], send.at[a, way, hop], recv.at[a, way, hop], device)

    def side_copy(a, way, hop, source, block):
        return ctx_copy(source, outs[a].at[block], side_send.at[a, way, hop], side_recv.at[a, way, hop], sibling)

    keeps = [pltpu.make_async_copy(xs[a], outs[a].at[me], local.at[a]) for a in several]
    for a in several:
        keeps[a].start()
        side_copy(a, 0, 0, xs[a], me).start()
    for hop in range(chips):
        for way, sign in ways:
            base, have, go, onward = spot(hop, sign)
            block = base + core
            if hop > 0:

                @pl.when(have)
                def _():
                    for a in several:
                        line_copy(a, way, hop - 1, xs[a], block, sibling).wait_recv()
                        side_copy(a, way, hop, outs[a].at[block], block).start()

            if hop < chips - 1:

                @pl.when(go)
                def _():
                    for a in several:
                        source = xs[a] if hop == 0 else outs[a].at[block]
                        line_copy(a, way, hop, source, block, onward).start()

        if hop == 0:
            mail.begin()
            mail.step(0, 1)
        if hop == 1:
            mail.step(1, 2)

    for hop in range(chips):
        for way, sign in ways:
            base, have, go, onward = spot(hop, sign)
            block = base + core
            other = base + 1 - core
            if hop > 0:

                @pl.when(have)
                def _():
                    for a in several:
                        side_copy(a, way, hop, outs[a].at[block], block).wait_send()
                        side_copy(a, way, hop, xs[a], other).wait_recv()

            if hop < chips - 1:

                @pl.when(go)
                def _():
                    for a in several:
                        line_copy(a, way, hop, xs[a], block, onward).wait_send()

    for a in several:
        side_copy(a, 0, 0, xs[a], me).wait_send()
        side_copy(a, 0, 0, xs[a], sibling).wait_recv()
        keeps[a].wait()
    mail.end(2)


def share_tokens(blocks, number, parcels=()):
    n = lax.axis_size("ctx")
    anywhere = pl.BlockSpec(memory_space=pl.ANY)
    count = len(blocks)
    return talk(
        share_core,
        blocks,
        [anywhere] * count,
        [jax.ShapeDtypeStruct((n,) + b.shape, b.dtype) for b in blocks],
        [anywhere] * count,
        [pltpu.SemaphoreType.DMA((count, 2, n // 2))] * 4 + [pltpu.SemaphoreType.DMA((count,))],
        list(parcels),
        number,
        16 << 20,
        "share_tokens",
    )


def reduce_core(n, ins, outs, own, mail):
    pairs = list(zip(ins[: len(ins) // 2], ins[len(ins) // 2 :]))
    o_ref = outs[0]
    total, to_side, from_side, inbox, side_send, side_recv, send, recv = own
    chips = n // 2
    me, core, chip, sibling = line_place(n)
    rows = o_ref.shape[0]

    def partial(block):
        place = pl.ds(pl.multiple_of(block * rows, rows), rows)
        return sum(jnp.dot(a[place, :], w[...], preferred_element_type=jnp.float32) for a, w in pairs)

    def side_copy(dest):
        return ctx_copy(to_side.at[dest], from_side.at[dest], side_send.at[dest], side_recv.at[dest], sibling)

    def line_copy(way, dest, onward):
        return ctx_copy(from_side.at[dest], inbox.at[dest + way], send.at[dest], recv.at[dest + way], onward)

    mail.begin()

    def begin(k, _):
        dest = jnp.where(chip >= chips // 2, k, chips - 1 - k)
        to_side[dest] = partial(2 * dest + 1 - core).astype(jnp.bfloat16)
        side_copy(dest).start()
        total[dest] = partial(2 * dest + core)
        return 0

    lax.fori_loop(0, chips, begin, 0)

    def spot(tick, way):
        far = (chips - 1 - chip) if way == 0 else chip
        k = tick - far
        dest = k if way == 0 else chips - 1 - k
        active = (k >= 0) & ((dest < chip) if way == 0 else (dest > chip))
        return far, k, dest, active, (me - 2 if way == 0 else me + 2)

    def advance(tick, _):
        for way in (0, 1):
            far, k, dest, active, onward = spot(tick, way)
            before = dest - 1 if way == 0 else dest + 1

            @pl.when(active)
            def _():
                side_copy(dest).wait_recv()
                total[dest] += from_side[dest].astype(jnp.float32)

                @pl.when(far > 0)
                def _():
                    line_copy(way, dest, onward).wait_recv()
                    total[dest] += inbox[dest + way].astype(jnp.float32)

                @pl.when((far == 0) & (k > 0))
                def _():
                    line_copy(way, before, onward).wait_send()

                from_side[dest] = total[dest].astype(jnp.bfloat16)
                line_copy(way, dest, onward).start()

        return 0

    lax.fori_loop(0, chips, advance, 0)
    side_copy(chip).wait_recv()
    total[chip] += from_side[chip].astype(jnp.float32)

    @pl.when(chip < chips - 1)
    def _():
        line_copy(0, chip, me - 2).wait_recv()
        total[chip] += inbox[chip].astype(jnp.float32)

    @pl.when(chip > 0)
    def _():
        line_copy(1, chip, me + 2).wait_recv()
        total[chip] += inbox[chip + 1].astype(jnp.float32)

    o_ref[...] = total[chip]

    def finish(tick, _):
        side_copy(tick).wait_send()
        for way in (0, 1):
            far, k, dest, active, onward = spot(tick, way)

            @pl.when(active & ((far > 0) | (k == chips - 2)))
            def _():
                line_copy(way, dest, onward).wait_send()

        return 0

    lax.fori_loop(0, chips, finish, 0)
    mail.end(0)


def reduce_tokens(lefts, rights, number, parcels=()):
    n = lax.axis_size("ctx")
    chips = n // 2
    rows, width = lefts[0].shape[0] // n, rights[0].shape[1]
    buffer = lambda *lead: pltpu.VMEM(lead + (rows, width), jnp.bfloat16)
    vmem = pl.BlockSpec(memory_space=pltpu.VMEM)

    outs, extra = talk(
        reduce_core,
        lefts + rights,
        [vmem] * (2 * len(lefts)),
        [jax.ShapeDtypeStruct((rows, width), jnp.float32)],
        [vmem],
        [pltpu.VMEM((chips, rows, width), jnp.float32), buffer(chips), buffer(chips), buffer(chips + 1)]
        + [pltpu.SemaphoreType.DMA((chips,))] * 3
        + [pltpu.SemaphoreType.DMA((chips + 1,))],
        list(parcels),
        number,
        56 << 20,
        "reduce_tokens",
    )
    return outs[0], extra


def total_core(n, ins, outs, own, mail):
    (x_ref,), (o_ref,) = ins, outs
    from_side, summed, inbox, outbox, side_send, side_recv, send, recv, out_send, out_recv, back_send, back_recv, local = own
    chips = n // 2
    me, core, chip, sibling = line_place(n)
    cols = outbox.shape[1]

    def place(ref, block):
        return ref.at[:, pl.ds(pl.multiple_of(block * cols, cols), cols)]

    def side_copy(d):
        dest = lax.rem(chip + d, chips)
        return ctx_copy(place(x_ref, 2 * dest + 1 - core), from_side.at[d], side_send.at[d], side_recv.at[d], sibling)

    def line_copy(d):
        return ctx_copy(summed.at[d], inbox.at[d], send.at[d], recv.at[d], lax.rem(me + 2 * d, n))

    def out_copy(d):
        return ctx_copy(outbox, place(o_ref, me), out_send.at[d], out_recv.at[d], lax.rem(me + 2 * d, n))

    order = list(range(1, chips)) + [0]
    for d in order:
        side_copy(d).start()
    mail.begin()
    for d in order:
        dest = lax.rem(chip + d, chips)
        side_copy(d).wait_recv()
        block = pl.ds(pl.multiple_of((2 * dest + core) * cols, cols), cols)
        summed[d] = x_ref[:, block] + from_side[d]
        if d:
            line_copy(d).start()
    result = summed[0]
    for d in range(1, chips):
        line_copy(d).wait_recv()
        result = result + inbox[d]
    outbox[...] = result.astype(jnp.bfloat16)
    keep = pltpu.make_async_copy(outbox, place(o_ref, me), local)
    keep.start()
    for d in range(1, chips):
        out_copy(d).start()
    side = ctx_copy(outbox, place(o_ref, me), back_send.at[0], back_recv.at[0], sibling)
    side.start()
    mail.step(0, 1)
    for d in range(1, chips):
        origin = lax.rem(me + n - 2 * d, n)
        ctx_copy(outbox, place(o_ref, origin), out_send.at[d], out_recv.at[d], origin).wait_recv()
        ctx_copy(place(o_ref, origin), place(o_ref, origin), back_send.at[d], back_recv.at[d], sibling).start()
    for d in range(chips):
        mine = lax.rem(me + n - 2 * d, n)
        theirs = lax.rem(sibling + n - 2 * d, n)
        ctx_copy(place(o_ref, mine), place(o_ref, mine), back_send.at[d], back_recv.at[d], sibling).wait_send()
        ctx_copy(outbox, place(o_ref, theirs), back_send.at[d], back_recv.at[d], sibling).wait_recv()
        side_copy(d).wait_send()
        if d:
            line_copy(d).wait_send()
            out_copy(d).wait_send()
    keep.wait()
    mail.end(1)


def total_columns(partial, number, parcels=()):
    n = lax.axis_size("ctx")
    chips = n // 2
    feats, length = partial.shape
    cols = length // n
    vmem = pl.BlockSpec(memory_space=pltpu.VMEM)
    outs, extra = talk(
        total_core,
        [partial],
        [vmem],
        [jax.ShapeDtypeStruct((feats, length), jnp.bfloat16)],
        [vmem],
        [pltpu.VMEM((chips, feats, cols), jnp.float32)] * 3
        + [pltpu.VMEM((feats, cols), jnp.bfloat16)]
        + [pltpu.SemaphoreType.DMA((chips,))] * 8
        + [pltpu.SemaphoreType.DMA],
        list(parcels),
        number,
        32 << 20,
        "total_columns",
        everyone=True,
    )
    return outs[0], extra


def send_core(n, ins, outs, own, mail):
    mail.begin()
    mail.step(0, 1)
    mail.end(1)


def send_only(parcels, number):
    return talk(send_core, [], [], [], [], [], list(parcels), number, 16 << 20, "send_only", everyone=True)[1]


def body(
    tokens,
    out_grad,
    teacher,
    valid,
    w_query,
    w_keyval,
    w_attn_out,
    w_in,
    w_mamba_out,
    w_gate,
    w_up,
    w_down,
    x_proj,
    dt_proj,
    a_log,
    conv_taps,
    conv_bias,
    dt_bias,
    skip_gain,
    norm_gains,
):
    n = lax.axis_size("ctx")
    m = lax.axis_size("fsdp")
    fsdp_index = lax.axis_index("fsdp")
    rows = tokens.shape[1]
    length = rows * n
    depth = w_in.shape[0]
    half = m // 2
    chunks = n // half
    chans = DI // n
    sub = chans // half
    subp = -(-sub // 128) * 128
    wide = half * subp
    units = w_down.shape[0]
    unit_sub = units // m
    unit_pad = -(-unit_sub // 16) * 16
    unit_wide = m * unit_pad
    heads = -(-H // n)
    group_size = H // KVH
    feats = -(-(R + 2 * DS) // 16) * 16
    slots = (heads + group_size - 2) // group_size + 1
    q_part = heads * HD // m
    kv_part = 2 * slots * HD // m
    head_pad = -(-(q_part + kv_part) // 128) * 128
    bases = [min(heads * c, H - 1) // group_size for c in range(n)]
    slot_heads = [[min(bases[c] + s, KVH - 1) for s in range(slots)] for c in range(n)]

    def wide_chans(array):
        array = array.reshape((half, sub) + array.shape[1:])
        return pad_to(array, subp, 1).reshape((wide,) + array.shape[2:])

    def true_chans(array):
        return array.reshape((half, subp) + array.shape[1:])[:, :sub].reshape((chans,) + array.shape[1:])

    mask_rows = valid[0].astype(F32)
    meta = jnp.stack([pad_to(norm_gains.astype(F32), 256, 0), jnp.full((256,), jnp.sum(mask_rows))])
    meta = pad_to(meta, 8, 0)
    in_send = pad_to(w_in.reshape(depth, chunks, half, sub).transpose(2, 1, 0, 3), subp, 3)
    head_send = jnp.concatenate([w_query, w_keyval], 1)
    ff_send = jnp.concatenate(
        [w.reshape(depth, n // m, m, unit_sub).transpose(2, 1, 0, 3) for w in (w_gate, w_up)], 3
    )
    small_send = jnp.concatenate(
        [x_proj, dt_proj, a_log, conv_taps, conv_bias[:, None], dt_bias[:, None], skip_gain[:, None]], 1
    )

    def by_chunk(ref, peer, shape):
        if ref is None:
            return shape[2:]
        return ref.at[lax.div(peer, chunks), lax.rem(peer, chunks)]

    (tokens_all, attn_rows), entry = share_tokens(
        [tokens[0], w_attn_out],
        0,
        [
            Parcel(in_send, "swap", "pair", 0),
            Parcel(meta, "gather", "fsdp", 0),
            Parcel(0, "swap", "ctx", 1, by_chunk),
            Parcel(1, "gather", "ctx", 1),
            Parcel(2, "lanes", "fsdp", 2),
            Parcel(head_send, "gather", "fsdp", BULK),
            Parcel(small_send, "gather", "fsdp", BULK),
            Parcel(ff_send, "swap", "fsdp", BULK),
        ],
    )
    meta_all, in_all, head_all, small_all, ff_all = entry[3:]
    gain_set = meta_all[:, :, 0, : norm_gains.shape[0]].reshape(4, D)
    valid_sum = jnp.sum(meta_all[:, :, 1, 0])
    in_weight = in_all.reshape(D, 2 * wide)
    small = wide_chans(small_all.reshape(chans, -1))
    xproj_weight = small[:, : R + 2 * DS]
    dtproj_weight = small[:, R + 2 * DS : 2 * R + 2 * DS]
    rest = small[:, 2 * R + 2 * DS :].astype(F32)
    amat = wide_chans(-jnp.exp(small_all.reshape(chans, -1)[:, 2 * R + 2 * DS : 2 * R + 3 * DS].astype(F32))).T
    rate = amat * LOG2E
    taps = rest[:, DS : DS + KC].T
    conv_bias_vec, dt_bias_vec, skip_vec = rest[:, DS + KC], rest[:, DS + KC + 1], rest[:, DS + KC + 2]
    query_rows = head_all[:, :, : w_query.shape[1]].transpose(1, 0, 2).reshape(depth, H * HD)
    query_rows = pad_to(query_rows, n * heads * HD, 1).reshape(depth, n, m, q_part)
    kv_rows = head_all[:, :, w_query.shape[1] :].transpose(1, 0, 2).reshape(depth, 2, KVH, HD)
    kv_rows = jnp.stack([jnp.stack([kv_rows[:, :, h] for h in slot_heads[c]], 2) for c in range(n)], 1)
    kv_rows = kv_rows.reshape(depth, n, m, kv_part)
    head_rows = lax.dynamic_index_in_dim(jnp.concatenate([query_rows, kv_rows], 3), fsdp_index, 2, False)
    head_rows = pad_to(head_rows.transpose(1, 0, 2), head_pad, 2)

    hidden = tokens[0].astype(F32)
    normed_all = norm_forward(tokens_all.reshape(length, D).astype(F32), gain_set[0])[0].astype(BF)
    factor_one = norm_forward(hidden, gain_set[0])[1]

    inner_low = matmul(normed_all, in_weight).astype(BF)
    x_branch = inner_low[:, :wide].astype(F32)
    z_branch = inner_low[:, wide:].astype(F32)
    padded = jnp.pad(x_branch, ((KC - 1, 0), (0, 0)))
    pre_conv = conv_bias_vec
    for k in range(KC):
        pre_conv = pre_conv + taps[k] * padded[k : k + length]
    ssm_in = jax.nn.silu(pre_conv)
    ssm_low = ssm_in.astype(BF)
    xdbl_t, (head_cols, head_cols_all) = total_columns(
        pad_to(contract(xproj_weight, ssm_low, 0, 1), feats, 0),
        1,
        [
            Parcel(head_rows, "swap", "ctx", 0),
            Parcel(0, "lanes", "fsdp", 1),
        ],
    )
    head_weight = head_cols_all.reshape(D, m, head_pad)
    query_weight = head_weight[:, :, :q_part].reshape(D, heads * HD)
    kv_weight = head_weight[:, :, q_part : q_part + kv_part].reshape(D, 2 * slots * HD)
    query_t = contract(query_weight, normed_all, 0, 1).astype(BF) * BF(HD**-0.5)
    kv = matmul(normed_all, kv_weight).astype(BF).reshape(length, 2, slots, HD)
    keys, values = kv[:, 0].transpose(1, 0, 2), kv[:, 1].transpose(1, 0, 2)
    (attn_part, lse), (mamba_all, down_all, ff_cols) = attend(
        query_t,
        keys,
        jnp.swapaxes(values, 1, 2),
        [
            Parcel(w_mamba_out, "gather", "fsdp", BULK),
            Parcel(w_down, "gather", "fsdp", BULK),
            Parcel(ff_all.reshape(n, depth, 2 * unit_sub), "swap", "ctx", BULK),
        ],
        11,
    )
    attn_part = attn_part.reshape(heads * HD, n, rows).transpose(1, 0, 2)
    mamba_weight = wide_chans(mamba_all.transpose(1, 0, 2).reshape(chans, D))
    down_weight = pad_to(down_all.transpose(1, 0, 2).reshape(m, unit_sub, D), unit_pad, 1).reshape(unit_wide, D)
    ff_parts = pad_to(ff_cols.reshape(D, 2, unit_sub).transpose(1, 2, 0), unit_pad, 1)

    dt_in_t = xdbl_t[:R]
    b_wide = jnp.broadcast_to(xdbl_t[R : R + DS].T.astype(F32)[:, :, None], (length, DS, 128))
    c_wide = jnp.broadcast_to(xdbl_t[R + DS : R + 2 * DS].T.astype(F32)[:, :, None], (length, DS, 128))
    dt_pre = contract(dt_in_t, dtproj_weight, 0, 1) + dt_bias_vec
    step_size = jax.nn.softplus(dt_pre)
    (state_rows, starts), (attn_t,) = ssm_forward(
        step_size, ssm_in, b_wide, c_wide, rate, [Parcel(attn_part, "swap", "ctx", BULK)], 12
    )
    ssm_out = state_rows + skip_vec * ssm_in
    gate_z = jax.nn.silu(z_branch)
    mixed_low = (ssm_out * gate_z).astype(BF)
    mamba_proj, (attn_weight_t,) = reduce_tokens(
        [mixed_low], [mamba_weight], 2, [Parcel(attn_rows.reshape(H * HD, -1).T, "gather", "fsdp", BULK)]
    )
    attn_t = attn_t.reshape(n * heads * HD, rows)[: H * HD]
    attn_weight_t = attn_weight_t.reshape(D, H * HD)
    attn_proj = contract(attn_t, attn_weight_t, 0, 1)

    attn_norm, factor_attn = norm_forward(attn_proj, gain_set[1])
    mamba_norm, factor_mamba = norm_forward(mamba_proj, gain_set[2])
    residual = hidden + 0.5 * (attn_norm + mamba_norm)
    ffn_in, factor_ffn = norm_forward(residual, gain_set[3])
    (ffn_all,), (gate_rows, up_rows) = share_tokens(
        [ffn_in.astype(BF)],
        3,
        [Parcel(ff_parts[0], "gather", "fsdp", BULK), Parcel(ff_parts[1], "gather", "fsdp", BULK)],
    )
    ffn_all = ffn_all.reshape(length, D)
    gate_rows, up_rows = gate_rows.reshape(unit_wide, D), up_rows.reshape(unit_wide, D)
    gate_pre = matmul_nt(ffn_all, gate_rows)
    up_pre = matmul_nt(ffn_all, up_rows)
    gate_act = jax.nn.silu(gate_pre)
    hidden_act = (gate_act * up_pre).astype(BF)
    layer_out = residual + reduce_tokens([hidden_act], [down_weight], 4)[0]

    mismatch = layer_out - teacher[0].astype(F32)
    error_part = jnp.sum(mask_rows[:, None] * mismatch * mismatch)
    grad_layer = out_grad[0].astype(F32) + 2.0 / (valid_sum * D) * mask_rows[:, None] * mismatch
    (grad_ffn_all,), _ = share_tokens([grad_layer.astype(BF)], 5)
    grad_ffn_all = grad_ffn_all.reshape(length, D)
    grad_act = matmul_nt(grad_ffn_all, down_weight)
    grad_gate = (grad_act * up_pre * silu_slope(gate_pre)).astype(BF)
    grad_up = (grad_act * gate_act).astype(BF)
    down_grad = matmul_tn(grad_ffn_all, hidden_act).astype(BF).reshape(m, D // m, unit_wide)
    grad_ffn_in, (down_grad,) = reduce_tokens(
        [grad_gate, grad_up], [gate_rows, up_rows], 6, [Parcel(down_grad, "swap", "fsdp", BULK)]
    )
    down_grad = jnp.sum(down_grad.astype(F32), 0).T.reshape(m, unit_pad, D // m)[:, :unit_sub].reshape(units, D // m)
    gate_grad, up_grad = [matmul_tn(g, ffn_all).astype(BF).reshape(m, unit_pad, D) for g in (grad_gate, grad_up)]

    grad_norm_res, gain_four = norm_backward(residual, factor_ffn, gain_set[3], grad_ffn_in)
    grad_resid = grad_layer + grad_norm_res
    half_grad = 0.5 * grad_resid
    grad_attn_proj, gain_two = norm_backward(attn_proj, factor_attn, gain_set[1], half_grad)
    grad_mamba_proj, gain_three = norm_backward(mamba_proj, factor_mamba, gain_set[2], half_grad)
    grad_attn_proj_low = grad_attn_proj.astype(BF)
    (grad_mamba_all,), (gate_grad, up_grad) = share_tokens(
        [grad_mamba_proj.astype(BF)],
        7,
        [Parcel(gate_grad, "swap", "fsdp", BULK), Parcel(up_grad, "swap", "fsdp", BULK)],
    )
    grad_mamba_all = grad_mamba_all.reshape(length, D)
    ff_grad = jnp.stack([jnp.sum(g.astype(F32), 0).astype(BF) for g in (gate_grad, up_grad)])
    ff_grad = ff_grad.reshape(2 * unit_pad, n, depth).transpose(1, 0, 2)
    attn_out_grad = contract(grad_attn_proj_low, attn_t, 0, 1).astype(BF).reshape(m, D // m, H * HD)
    grad_attn = contract(attn_weight_t, grad_attn_proj_low, 0, 1).astype(BF)
    grad_attn = pad_to(grad_attn, n * heads * HD, 0).reshape(n, heads * HD, rows)

    mamba_out_grad = matmul_tn(grad_mamba_all, mixed_low).astype(BF).reshape(m, D // m, wide)
    grad_mixed = matmul_nt(grad_mamba_all, mamba_weight)
    grad_y = grad_mixed * gate_z
    grad_z = grad_mixed * ssm_out * silu_slope(z_branch)
    z_grad = matmul_tn(normed_all, grad_z.astype(BF)).astype(BF)
    step_grad, along_b, b_grad, c_grad, a_accum, (attn_out_grad, grad_attn) = ssm_backward(
        step_size,
        ssm_in,
        grad_y,
        b_wide,
        c_wide,
        rate,
        amat,
        starts,
        [Parcel(attn_out_grad, "swap", "fsdp", BULK), Parcel(grad_attn, "swap", "ctx", BULK)],
        13,
    )
    attn_out_grad = jnp.sum(attn_out_grad.astype(F32), 0).T.astype(BF)
    attn_out_grad = lax.psum_scatter(attn_out_grad, "ctx", scatter_dimension=0, tiled=True).astype(F32)

    grad_attn = grad_attn.transpose(1, 0, 2).reshape(heads * HD, length)
    (grad_query, grad_keys, grad_values), (ff_grad, mamba_out_grad) = attend_back(
        query_t,
        grad_attn,
        keys,
        jnp.swapaxes(keys, 1, 2),
        values,
        lse,
        [Parcel(ff_grad, "swap", "ctx", BULK), Parcel(mamba_out_grad, "swap", "fsdp", BULK)],
        14,
    )
    grad_kv = jnp.stack([grad_keys, grad_values]).astype(BF).transpose(2, 0, 1, 3).reshape(length, 2 * slots * HD)
    mamba_out_grad = true_chans(jnp.sum(mamba_out_grad.astype(F32), 0).T)
    query_grad = contract(grad_query, normed_all, 1, 0).astype(BF).reshape(m, q_part, D)
    kv_grad = matmul_tn(grad_kv, normed_all).astype(BF).reshape(m, kv_part, D)

    grad_dt_pre = (step_grad * jax.nn.sigmoid(dt_pre)).astype(BF)
    dtproj_grad = contract(grad_dt_pre, dt_in_t, 0, 1)
    grad_xdbl_t = jnp.concatenate([contract(dtproj_weight, grad_dt_pre, 0, 1), b_grad.T, c_grad.T], 0)
    grad_xdbl_t, (query_grad, kv_grad) = total_columns(
        pad_to(grad_xdbl_t, feats, 0),
        8,
        [Parcel(query_grad, "swap", "fsdp", BULK), Parcel(kv_grad, "swap", "fsdp", BULK)],
    )
    grad_xdbl_t = grad_xdbl_t[: R + 2 * DS]
    head_grad = jnp.concatenate([jnp.sum(query_grad.astype(F32), 0), jnp.sum(kv_grad.astype(F32), 0)], 0)
    head_grad = pad_to(head_grad.astype(BF).T, head_pad, 1).reshape(n, depth, head_pad)
    xproj_grad = contract(ssm_low, grad_xdbl_t, 0, 1)
    grad_ssm_in = step_size * along_b + skip_vec * grad_y + contract(grad_xdbl_t, xproj_weight, 0, 1)
    grad_pre = grad_ssm_in * silu_slope(pre_conv)
    taps_grad = jnp.stack([jnp.sum(grad_pre * padded[k : k + length], axis=0) for k in range(KC)], 1)
    grad_after = jnp.pad(grad_pre, ((0, KC - 1), (0, 0)))
    grad_x = jnp.zeros_like(grad_pre)
    for k in range(KC):
        grad_x = grad_x + taps[k] * grad_after[KC - 1 - k : KC - 1 - k + length]
    x_grad = matmul_tn(normed_all, grad_x.astype(BF)).astype(BF)
    small_grad = jnp.concatenate(
        [
            xproj_grad,
            dtproj_grad,
            (a_accum * amat).T,
            taps_grad,
            jnp.sum(grad_pre, axis=0)[:, None],
            jnp.sum(grad_dt_pre.astype(F32), axis=0)[:, None],
            jnp.sum(grad_y * ssm_in, axis=0)[:, None],
        ],
        1,
    )
    small_grad = true_chans(small_grad).reshape(m, chans // m, -1)

    def by_lanes(ref, peer, shape):
        if ref is None:
            return (shape[0], subp)
        return ref.at[:, pl.ds(pl.multiple_of(peer * subp, subp), subp)]

    grad_normed, (ff_grad, small_grad, in_grad, head_grad) = reduce_tokens(
        [grad_query.T, grad_kv, grad_x.astype(BF), grad_z.astype(BF)],
        [query_weight.T, kv_weight.T, in_weight[:, :wide].T, in_weight[:, wide:].T],
        9,
        [
            Parcel(ff_grad.reshape(m, n // m, 2, unit_pad, depth), "swap", "fsdp", BULK),
            Parcel(small_grad, "swap", "fsdp", BULK),
            Parcel(jnp.concatenate([x_grad, z_grad], 1), "swap", "fsdp", BULK, by_lanes),
            Parcel(head_grad, "swap", "ctx", BULK),
        ],
    )
    ff_grad = ff_grad[:, :, :, :unit_sub].transpose(2, 4, 1, 0, 3)
    ff_grad = ff_grad.reshape(2, depth, units * n // m).astype(F32)
    small_grad = jnp.sum(small_grad, 0)
    in_grad = jnp.sum(in_grad.astype(F32), 0).astype(BF).reshape(n, depth, subp)

    grad_norm_in, gain_one = norm_backward(hidden, factor_one, gain_set[0], grad_normed)
    input_grad = grad_resid + grad_norm_in
    gain_grads = jnp.concatenate([gain_one, gain_two, gain_three, gain_four]).reshape(n, m, 1, -1)
    gain_grads = pad_to(gain_grads, 256, 3)
    meta_grad = pad_to(jnp.concatenate([gain_grads, jnp.full_like(gain_grads, error_part)], 2), 8, 2)

    def by_fsdp(ref, peer, shape):
        if ref is None:
            return (shape[0],) + shape[2:]
        return ref.at[:, peer]

    def by_run(ref, peer, shape):
        if ref is None:
            return (chunks,) + shape[1:]
        return ref.at[pl.ds(peer * chunks, chunks)]

    _, _, head_grad, meta_grad, in_grad = send_only(
        [
            Parcel(meta_grad, "swap", "ctx", 0),
            Parcel(in_grad, "swap", "ctx", 0),
            Parcel(head_grad, "gather", "fsdp", BULK),
            Parcel(0, "swap", "fsdp", 1, by_fsdp),
            Parcel(1, "swap", "pair", 1, by_run),
        ],
        10,
    )
    meta_grad = jnp.sum(meta_grad, (0, 1))
    gains_grad = meta_grad[0, : norm_gains.shape[0]]
    loss = meta_grad[1, 0] / (valid_sum * D)
    in_grad = in_grad[..., :sub].transpose(2, 1, 0, 3).reshape(depth, w_in.shape[1]).astype(F32)
    query_grad = head_grad[..., :q_part].transpose(2, 1, 0, 3).reshape(depth, n * heads * HD)
    query_grad = lax.dynamic_slice_in_dim(query_grad, fsdp_index * w_query.shape[1], w_query.shape[1], 1).astype(F32)
    kv_parts = head_grad[..., q_part : q_part + kv_part].astype(F32)
    kv_parts = kv_parts.transpose(1, 2, 0, 3).reshape(n, depth, 2, slots, HD)
    kv_sums = []
    for h in range(KVH):
        owners = [(c, h - bases[c]) for c in range(n) if 0 <= h - bases[c] < slots]
        kv_sums.append(sum(kv_parts[c, :, :, s] for c, s in owners))
    kv_grad = jnp.stack(kv_sums, 2).reshape(depth, 2 * KVH * HD)
    kv_grad = lax.dynamic_slice_in_dim(kv_grad, fsdp_index * w_keyval.shape[1], w_keyval.shape[1], 1)

    return (
        loss,
        layer_out.astype(BF)[None],
        input_grad[None],
        query_grad,
        kv_grad,
        attn_out_grad,
        in_grad,
        mamba_out_grad,
        ff_grad[0],
        ff_grad[1],
        down_grad,
        small_grad[:, : R + 2 * DS],
        small_grad[:, R + 2 * DS : 2 * R + 2 * DS],
        small_grad[:, 2 * R + 2 * DS : 2 * R + 3 * DS],
        small_grad[:, 2 * R + 3 * DS : 2 * R + 3 * DS + KC],
        small_grad[:, 2 * R + 3 * DS + KC],
        small_grad[:, 2 * R + 3 * DS + KC + 1],
        small_grad[:, 2 * R + 3 * DS + KC + 2],
        gains_grad,
    )


def solution(mesh):
    in_specs = (
        P("fsdp", "ctx", None),
        P("fsdp", "ctx", None),
        P("fsdp", "ctx", None),
        P("fsdp", "ctx"),
        P("ctx", "fsdp"),
        P("ctx", "fsdp"),
        P("ctx", "fsdp"),
        P("ctx", "fsdp"),
        P("ctx", "fsdp"),
        P("ctx", "fsdp"),
        P("ctx", "fsdp"),
        P("ctx", "fsdp"),
        P(("ctx", "fsdp"), None),
        P(("ctx", "fsdp"), None),
        P(("ctx", "fsdp"), None),
        P(("ctx", "fsdp"), None),
        P(("ctx", "fsdp")),
        P(("ctx", "fsdp")),
        P(("ctx", "fsdp")),
        P(("ctx", "fsdp")),
    )
    out_specs = (
        P(),
        P("fsdp", "ctx", None),
        P("fsdp", "ctx", None),
        P("ctx", "fsdp"),
        P("ctx", "fsdp"),
        P("ctx", "fsdp"),
        P("ctx", "fsdp"),
        P("ctx", "fsdp"),
        P("ctx", "fsdp"),
        P("ctx", "fsdp"),
        P("ctx", "fsdp"),
        P(("ctx", "fsdp"), None),
        P(("ctx", "fsdp"), None),
        P(("ctx", "fsdp"), None),
        P(("ctx", "fsdp"), None),
        P(("ctx", "fsdp")),
        P(("ctx", "fsdp")),
        P(("ctx", "fsdp")),
        P(("ctx", "fsdp")),
    )
    return jax.shard_map(body, mesh=mesh, in_specs=in_specs, out_specs=out_specs, check_vma=False)
```

time: 5270 us -> 1420 us (0.27)
  waiting for transfers between devices: 2530 us -> 0.02 us
  Pallas kernels: 0 us -> 903 us
  other arithmetic: 952 us -> 98.1 us
  local copies, waits for them, and re-layouts: 1030 us -> 240 us
  blocking collectives: 296 us -> 0 us
  matrix products: 344 us -> 153 us
    unnamed x56 -> x2, waiting for transfers between devices: 1710 us -> 0.02 us
    pallas_call x0 -> x15, Pallas kernels: none -> 903 us  [talk(): pl.pallas_call(kernel, grid=(steps,) if steps else (), out_shape=list(out...]
    reduce_scatter x3 -> x0, waiting for transfers between devices: 582 us -> none  [the longest x1 354 us: body(): lax.psum_scatter(down_grad, 'ctx', scatter_dimension=0, tiled=True)]
    reduce_sum x227 -> x16, other arithmetic: 395 us -> 36 us  [the longest x1 8.37 us: body(): jnp.sum(grad_pre, axis=0)[:, None]]
    another operation x345 -> x10, local copies, waits for them, and re-layouts: 324 us -> 12.8 us  [the longest x2 5.78 us: wide_chans(): array = array.reshape((half, sub) + array.shape[1:])]
    mul x833 -> x1, other arithmetic: 283 us -> 0.01 us  [body(): rate = amat * LOG2E]
    slice x103 -> x18, local copies, waits for them, and re-layouts: 279 us -> 19.3 us  [the longest x1 4.35 us: body(): head_weight[:, :, q_part:q_part + kv_part].reshape(D, 2 * slots * HD)]
    dot_general x35 -> x22, matrix products: 342 us -> 148 us  [contract(): lax.dot_general(left, right, (((left_dim,), (right_dim,)), ((), ())), pre...]
where the time goes in v1:
time: 1420 us; the launch traced here: 1410 us
  Pallas kernels  903 us (64%)
  local copies, waits for them, and re-layouts  240 us (17%)
  matrix products  153 us (11%)
  other arithmetic  98.1 us (7%)
  between operations  18.8 us (1%)
    pallas_call x15, Pallas kernels, talk(): pl.pallas_call(kernel, grid=(steps,) if steps else (), out_shape=list(out...  903 us
    dot_general x22, matrix products, contract(): lax.dot_general(left, right, (((left_dim,), (right_dim,)), ((), ())), pre...  148 us
    unnamed x340, local copies, waits for them, and re-layouts  92.4 us
  transfers between devices with their start and end apart: 1, of which 0 were waited for; matrix products, arithmetic and copies ran while one was open for 12% of the time, Pallas kernels for 14%

profile of v1, /device:TPU:9, one launch (start us, length us, event | category | flops | bytes accessed | tf_op | source)
XLA Modules:
  0.0 1414.1 jit_solution(2191201782857819469)
XLA Ops:
  26.5 95.3 %share_tokens.4 = (bf16[8,256,1600]{2,1,0:T(8,128)(2,1)S(1)}, bf16[8,200,400]{2,1,0:T(8,128)(2,1)S(1)}, bf16[2,4,200,256]{3,2,1,0:T(8,128)(2,1)}, f32[4,8,256]{2...) custom-call(bf16[256,1600]{1,0:T(8,128)(2,1)S(1)} %bitcast.319, ...), custom_call_target="tpu_custom_call" | custom-call | tf_op jit(solution)/shard_map/share_tokens/pallas_call | solution.py:574
  150.7 9.9 convolution_convert_fusion.1
  178.4 49.1 %total_columns.2 = (bf16[144,2048]{1,0:T(8,128)(2,1)S(1)}, bf16[8,200,128]{2,1,0:T(8,128)(2,1)}, bf16[8,200,512]{2,1,0:T(8,128)(2,1)S(1)}) custom-call(f32[144,2048]{1,0:T(8,128)S(1)} %pad.71.refs_0_, bf16[8,200,128]{2,1,0:T(8,128)(2,1)S(1)} %bitcast.339), custom_call_target="tpu_custom_call" | custom-call | tf_op jit(solution)/shard_map/total_columns/pallas_call | solution.py:574
  257.4 54.0 %attend.1 = (bf16[256,2048]{1,0:T(8,128)(2,1)S(1)}, f32[8,2048]{1,0:T(8,128)S(1)}, bf16[4,400,400]{2,1,0:T(8,128)(2,1)S(1)}, bf16[4,688,400]{2,1,0:T(8,128)(2,1)S(1)}, bf16[8,200,344]{2,1,0:T(8,128)(2,1)S(1)}) custom-call(bf16[256,2048]{1,0:T(8,128)(2,1)S(1)} %fusion.12.refs_0_, bf16[2,2048,64]{2,1,0:T(8,128)(2,1)S(1)} %copy.399.refs_1_.refs_2_, ...), custom_call_target="tpu_custom_call" | custom-call | tf_op jit(solution)/shard_map/attend/pallas_call | solution.py:574
  320.9 6.8 compare_select_fusion
  346.8 9.4 broadcast_in_dim.17.refs_2_.refs_3_
  356.2 9.0 broadcast_in_dim.18.refs_3_.refs_4_
  365.3 28.2 %ssm_forward.1 = (f32[2048,512]{1,0:T(8,128)S(1)}, f32[16,16,512]{2,1,0:T(8,128)S(1)}, bf16[8,256,256]{2,1,0:T(8,128)(2,1)S(1)}) custom-call(f32[2048,512]{1,0:T(8,128)S(1)} %copy-done.7, f32[2048,512]{1,0:T(8,128)S(1)} %copy-done.1, f32[2048,16,128]{2,1,0:T(8,128)} %broadcast_in_dim.17.refs_2_.refs_3_, f32[2048,16,128]{2,1,0:T(8,128)} %broadcast_in_dim.18.refs_3_.refs_4_, ...), custom_call_target="tpu_custom_call" | custom-call | tf_op jit(solution)/shard_map/ssm_forward/pallas_call | solution.py:574
  397.3 67.5 %reduce_tokens.4 = (f32[256,1600]{1,0:T(8,128)}, bf16[4,400,1600]{2,1,0:T(8,128)(2,1)}) custom-call(bf16[2048,512]{1,0:T(8,128)(2,1)} %multiply_convert_fusion.5.refs_0_, bf16[512,1600]{1,0:T(8,128)(2,1)} %bitcast.368, bf16[400,1600]{1,0:T(8,128)(2,1)} %bitcast.377), custom_call_target="tpu_custom_call" | custom-call | tf_op jit(solution)/shard_map/reduce_tokens/pallas_call | solution.py:574
  504.8 57.8 %share_tokens.5 = (bf16[8,256,1600]{2,1,0:T(8,128)(2,1)S(1)}, bf16[4,176,1600]{2,1,0:T(8,128)(2,1)S(1)}, bf16[4,176,1600]{2,1,0:T(8,128)(2,1)S(1)}) custom-call(bf16[256,1600]{1,0:T(8,128)(2,1)S(1)} %multiply_convert_fusion.6.refs_0_, bf16[176,1600]{1,0:T(8,128)(2,1)S(1)} %get-tuple-element.265.refs_1_, bf16[176,1600]{1,0:T(8,128)(2,1)S(1)} %get-tuple-element.264.refs_2_), custom_call_target="tpu_custom_call" | custom-call | tf_op jit(solution)/shard_map/share_tokens/pallas_call | solution.py:574
  562.7 6.2 fusion.70
  568.9 8.8 multiply_convert_fusion.3
  577.8 74.8 %reduce_tokens.5 = f32[256,1600]{1,0:T(8,128)} custom-call(bf16[2048,704]{1,0:T(8,128)(2,1)} %get-tuple-element.298.refs_0_, bf16[704,1600]{1,0:T(8,128)(2,1)} %bitcast.364), custom_call_target="tpu_custom_call" | custom-call | tf_op jit(solution)/shard_map/reduce_tokens/pallas_call | solution.py:574
  655.7 58.7 %share_tokens.6 = bf16[8,256,1600]{2,1,0:T(8,128)(2,1)S(1)} custom-call(bf16[256,1600]{1,0:T(8,128)(2,1)S(1)} %fusion.56.refs_0_), custom_call_target="tpu_custom_call" | custom-call | tf_op jit(solution)/shard_map/share_tokens/pallas_call | solution.py:574
  714.4 7.0 convolution_convert_fusion.4
  721.5 12.7 multiply_convert_fusion.1
  734.2 10.9 convolution_convert_fusion.2
  745.1 9.8 convolution_convert_fusion.3
  759.4 84.9 %reduce_tokens.6 = (f32[256,1600]{1,0:T(8,128)}, bf16[4,400,704]{2,1,0:T(8,128)(2,1)}) custom-call(bf16[2048,704]{1,0:T(8,128)(2,1)} %get-tuple-element.251.refs_0_, bf16[2048,704]{1,0:T(8,128)(2,1)} %get-tuple-element.250.refs_1_, bf16[704,1600]{1,0:T(8,128)(2,1)} %bitcast.334, bf16[704,1600]{1,0:T(8,128)(2,1)} %bitcast.336, bf16[4,400,704]{2,1,0:T(8,128)(2,1)} %bitcast.363), custom_call_target="tpu_custom_call" | custom-call | tf_op jit(solution)/shard_map/reduce_tokens/pallas_call | solution.py:574
  858.8 57.2 %share_tokens.7 = (bf16[8,256,1600]{2,1,0:T(8,128)(2,1)S(1)}, bf16[4,176,1600]{2,1,0:T(8,128)(2,1)S(1)}, bf16[4,176,1600]{2,1,0:T(8,128)(2,1)S(1)}) custom-call(bf16[256,1600]{1,0:T(8,128)(2,1)S(1)} %get-tuple-element.259.refs_0_, bf16[4,176,1600]{2,1,0:T(8,128)(2,1)S(1)} %bitcast.338, bf16[4,176,1600]{2,1,0:T(8,128)(2,1)S(1)} %bitcast.337), custom_call_target="tpu_custom_call" | custom-call | tf_op jit(solution)/shard_map/share_tokens/pallas_call | solution.py:574
  918.8 12.0 multiply_reduce_fusion.1
  930.9 75.8 %ssm_backward.1 = (f32[2048,512]{1,0:T(8,128)S(1)}, f32[2048,512]{1,0:T(8,128)S(1)}, f32[16,8,2048]{2,1,0:T(8,128)S(1)}, f32[16,8,2048]{2,1,0:T(8,128)S(1)}, f32...) custom-call(f32[2048,512]{1,0:T(8,128)} %get-tuple-element.294.refs_0_, ...), custom_call_target="tpu_custom_call" | custom-call | tf_op jit(solution)/shard_map/ssm_backward/pallas_call | solution.py:574
  1022.3 8.4 convolution_convert_fusion.7
  1055.1 51.1 %attend_back.1 = (bf16[256,2048]{1,0:T(8,128)(2,1)S(1)}, f32[2,2048,64]{2,1,0:T(8,128)S(1)}, f32[2,2048,64]{2,1,0:T(8,128)}, bf16[8,352,200]{2,1,0:T(8,128)(2,1)S(1)}, bf16[4,400,512]{2,1,0:T(8,128)(2,1)S(1)}) custom-call(bf16[256,2048]{1,0:T(8,128)(2,1)S(1)} %copy-done.12, bf16[256,2048]{1,0:T(8,128)(2,1)S(1)} %bitcast.325, ...), custom_call_target="tpu_custom_call" | custom-call | tf_op jit(solution)/shard_map/attend_back/pallas_call | solution.py:574
  1111.9 7.0 convolution_convert_fusion.8
  1124.7 7.4 fusion.1
  1133.4 5.7 convolution_convert_fusion.9
  1145.5 26.1 %total_columns.3 = (bf16[144,2048]{1,0:T(8,128)(2,1)S(1)}, bf16[4,64,1600]{2,1,0:T(8,128)(2,1)S(1)}, bf16[4,64,1600]{2,1,0:T(8,128)(2,1)S(1)}) custom-call(f32[144,2048]{1,0:T(8,128)S(1)} %select_maximum_fusion.refs_0_, bf16[4,64,1600]{2,1,0:T(8,128)(2,1)S(1)} %bitcast.328, bf16[4,64,1600]{2,1,0:T(8,128)(2,1)S(1)} %bitcast.327), custom_call_target="tpu_custom_call" | custom-call | tf_op jit(solution)/shard_map/total_columns/pallas_call | solution.py:574
  1177.7 7.8 multiply_multiply_fusion
  1186.3 8.4 fusion.61
  1223.1 79.2 %reduce_tokens.7 = (f32[256,1600]{1,0:T(8,128)}, bf16[4,2,2,176,200]{4,3,2,1,0:T(8,128)(2,1)}, f32[4,100,255]{2,1,0:T(8,128)}, bf16[4,1600,256]{2,1,0:T(8,128)(2,1)}, bf16[8,200,128]{2,1,0:T(8,128)(2,1)}) custom-call(bf16[2048,256]{1,0:T(8,128)(2,1)} %bitcast.381, bf16[2048,256]{1,0:T(8,128)(2,1)} %copy.443.refs_1_, bf16[2048,512]{1,0:T(8,128)(2,1)} %copy-done.84, ...), custom_call_target="tpu_custom_call" | custom-call | tf_op jit(solution)/shard_map/reduce_tokens/pallas_call | solution.py:574
  1308.2 43.7 %send_only.1 = (f32[8,4,8,256]{3,2,1,0:T(8,128)}, bf16[8,200,256]{2,1,0:T(8,128)(2,1)}, bf16[4,8,200,128]{3,2,1,0:T(8,128)(2,1)S(1)}, f32[4,8,8,256]{3,2,1,0:T(8,128)S(1)}, bf16[2,4,200,256]{3,2,1,0:T(8,128)(2,1)S(1)}) custom-call(f32[8,4,8,256]{3,2,1,0:T(8,128)S(1)} %pad_select_fusion.refs_0_, bf16[8,200,256]{2,1,0:T(8,128)(2,1)S(1)} %bitcast.331, ...), custom_call_target="tpu_custom_call" | custom-call | tf_op jit(solution)/shard_map/send_only/pallas_call | solution.py:574
  (526 shorter events, 344.6 us)
Async XLA Ops:
  7.2 1396.8 %reduce-scatter.4.cloned.1.call-start = ((), (), s32[]{:S(2)}) async-start(), calls=%async_computation.1 | async-start | bytes 1843200
  8.8 465.9 %copy-start.5 = (bf16[1,256,1600]{2,1,0:T(8,128)(2,1)}, bf16[1,256,1600]{2,1,0:T(8,128)(2,1)S(1)}, u32[]{:S(2)}) copy-start(bf16[1,256,1600]{2,1,0:T(8,128)(2,1)S(1)} %copy.375) | copy-start | bytes 2457604
  8.8 10.5 copy-start.117
  8.8 10.6 copy-start.118
  8.9 10.7 copy-start.138
  8.9 10.8 copy-start.140
  8.9 10.9 copy-start.143
  8.9 11.7 copy-start.144
  8.9 12.4 copy-start.145
  8.9 13.8 copy-start.141
  131.9 34.8 %copy-start.99 = (bf16[2,256,255]{2,1,0:T(8,128)(2,1)}, bf16[2,256,255]{2,1,0:T(8,128)(2,1)S(1)}, u32[]{:S(2)}) copy-start(bf16[2,256,255]{2,1,0:T(8,128)(2,1)S(1)} %pad.69) | copy-start | bytes 783364
  251.4 60.0 %copy-start.11 = (bf16[256,2048]{1,0:T(8,128)(2,1)}, bf16[256,2048]{1,0:T(8,128)(2,1)S(1)}, u32[]{:S(2)}) copy-start(bf16[256,2048]{1,0:T(8,128)(2,1)S(1)} %fusion.12.refs_0_) | copy-start | bytes 3145732
  332.1 33.1 %copy-start.59 = (f32[16,512]{1,0:T(8,128)}, f32[16,512]{1,0:T(8,128)S(1)}, u32[]{:S(2)}) copy-start(f32[16,512]{1,0:T(8,128)S(1)} %broadcast_multiply_fusion.refs_4_.refs_5_) | copy-start | bytes 98308
  346.8 9.4 copy-start.92
  365.2 29.0 %copy-start.81 = (bf16[2048,1024]{1,0:T(8,128)(2,1)S(1)}, bf16[2048,1024]{1,0:T(8,128)(2,1)}, u32[]{:S(2)}) copy-start(bf16[2048,1024]{1,0:T(8,128)(2,1)} %copy-done.80) | copy-start | bytes 12582916
  365.2 29.0 %copy-start.135 = (f32[512,1]{0,1:T(1,128)S(1)}, f32[512,1]{0,1:T(1,128)}, u32[]{:S(2)}) copy-start(f32[512,1]{0,1:T(1,128)} %get-tuple-element.277) | copy-start | bytes 6148
  394.3 70.5 %copy-start.49 = (bf16[8,256,256]{2,1,0:T(8,128)(2,1)}, bf16[8,256,256]{2,1,0:T(8,128)(2,1)S(1)}, u32[]{:S(2)}) copy-start(bf16[8,256,256]{2,1,0:T(8,128)(2,1)S(1)} %get-tuple-element.82) | copy-start | bytes 3145732
  577.8 75.5 %copy-start.132 = (f32[1,256]{1,0:T(1,128)S(1)}, f32[1,256]{1,0:T(1,128)}, u32[]{:S(2)}) copy-start(f32[1,256]{1,0:T(1,128)} %convert_element_type.239) | copy-start | bytes 3076
  577.8 75.5 %copy-start.71 = (f32[256,1600]{1,0:T(8,128)S(1)}, f32[256,1600]{1,0:T(8,128)}, u32[]{:S(2)}) copy-start(f32[256,1600]{1,0:T(8,128)} %get-tuple-element.246) | copy-start | bytes 4915204
  655.7 58.7 %copy-start.97 = (bf16[2048,704]{1,0:T(8,128)(2,1)S(1)}, bf16[2048,704]{1,0:T(8,128)(2,1)}, u32[]{:S(2)}) copy-start(bf16[2048,704]{1,0:T(8,128)(2,1)} %get-tuple-element.298.refs_0_) | copy-start | bytes 8650756
  734.2 10.9 copy-start.98
  759.4 84.9 %copy-start.74 = (f32[256,1600]{1,0:T(8,128)S(1)}, f32[256,1600]{1,0:T(8,128)}, u32[]{:S(2)}) copy-start(f32[256,1600]{1,0:T(8,128)} %reduce_tokens.5) | copy-start | bytes 4915204
  759.4 84.9 %copy-start.79 = (bf16[1,256,1600]{2,1,0:T(8,128)(2,1)S(1)}, bf16[1,256,1600]{2,1,0:T(8,128)(2,1)}, u32[]{:S(2)}) copy-start(bf16[1,256,1600]{2,1,0:T(8,128)(2,1)} %copy.413) | copy-start | bytes 2457604
  854.2 64.6 %copy-start.16 = (f32[2048,512]{1,0:T(8,128)S(1)}, f32[2048,512]{1,0:T(8,128)}, u32[]{:S(2)}) copy-start(f32[2048,512]{1,0:T(8,128)} %copy-done.15) | copy-start | bytes 12582916
  858.8 60.1 %copy-start.2 = (f32[2048,512]{1,0:T(8,128)S(1)}, f32[2048,512]{1,0:T(8,128)}, u32[]{:S(2)}) copy-start(f32[2048,512]{1,0:T(8,128)} %copy-done) | copy-start | bytes 12582916
  918.8 12.1 copy-start.26
  918.8 12.1 copy-start.54
  918.8 12.1 copy-start.56
  918.8 12.1 copy-start.60
  1111.9 9.3 copy-start.19
  1173.7 20.9 %slice-start = ((s8[6815744]{0:T(1024)(128)(4,1)}), s8[4194304]{0:T(1024)(128)(4,1)S(1)}, s32[]{:S(2)}) async-start(s8[6815744]{0:T(1024)(128)(4,1)} %bitcast.374), calls=%async_computation.2 | async-start | bytes 8388608
  1177.7 17.0 %slice-start.1 = ((s8[6815744]{0:T(1024)(128)(4,1)}), s8[2621440]{0:T(1024)(128)(4,1)S(1)}, s32[]{:S(2)}) async-start(s8[6815744]{0:T(1024)(128)(4,1)} %bitcast.374), calls=%async_computation.3 | async-start | bytes 5242880
  (120 other events, 468.4 us)
Sparse Core Ops, SparseCore 0:
  1022.4 29.1 reduce-scatter.3

commit v2 on v1

--- a/solution.py
+++ b/solution.py
@@ -1,3 +1,4 @@
+import functools
 from typing import Any, NamedTuple
 
 import jax
@@ -36,7 +37,7 @@
     return parts[0]
 
 def spread(column, lanes):
-    return jnp.concatenate([column] * (lanes // 128), 1)
+    return jnp.concatenate([column.astype(jnp.float32)] * (lanes // 128), 1)
 
 def ssm_forward_kernel(step_ref, u_ref, b_ref, c_ref, rate_ref, y_ref, start_ref, state):
     @pl.when(pl.program_id(0) == 0)
@@ -290,8 +291,8 @@
         inner = jnp.sum(probs * slopes, axis=0, keepdims=True)
         ds = (probs * (slopes - inner)).astype(jnp.bfloat16)
         dq_ref[feats, :] = (dot_nn(kt_ref[slot, :, keys], ds) * HD**-0.5).astype(dq_ref.dtype)
-        dk_ref[slot, keys, :] += dot_nt(ds, query)
-        dv_ref[slot, keys, :] += dot_nt(probs.astype(jnp.bfloat16), grad)
+        dk_ref[slot, :, keys] += dot_nt(query, ds)
+        dv_ref[slot, :, keys] += dot_nt(grad, probs.astype(jnp.bfloat16))
         return 0
 
     lax.fori_loop(0, q_ref.shape[0] // HD, head, 0)
@@ -307,10 +308,10 @@
         [tokens, tokens, whole(k), whole(k_t), whole(v), pl.BlockSpec((8, QB), lambda i: (0, i))],
         [
             jax.ShapeDtypeStruct((feats, length), jnp.bfloat16),
-            jax.ShapeDtypeStruct(k.shape, jnp.float32),
-            jax.ShapeDtypeStruct(k.shape, jnp.float32),
+            jax.ShapeDtypeStruct(k_t.shape, jnp.float32),
+            jax.ShapeDtypeStruct(k_t.shape, jnp.float32),
         ],
-        [tokens, whole(k), whole(k)],
+        [tokens, whole(k_t), whole(k_t)],
         [pltpu.VMEM((span, QB), jnp.float32)],
         parcels,
         number,
@@ -678,8 +679,133 @@
     )
 
 
-def reduce_core(n, ins, outs, own, mail):
-    pairs = list(zip(ins[: len(ins) // 2], ins[len(ins) // 2 :]))
+def feed_core(consume, n, ins, outs, own, mail):
+    x_ref, given = ins[0], ins[1:]
+    count = len(given)
+    gathered, held, more = own[0], own[1 : 1 + count], own[1 + count : -6]
+    send, recv, side_send, side_recv, local, load = own[-6:]
+    chips = n // 2
+    me, core, chip, sibling = line_place(n)
+
+    def line_copy(way, hop, source, block, device):
+        return ctx_copy(source, gathered.at[block], send.at[way, hop], recv.at[way, hop], device)
+
+    def side_copy(way, hop, source, block):
+        return ctx_copy(source, gathered.at[block], side_send.at[way, hop], side_recv.at[way, hop], sibling)
+
+    def spot(hop, way):
+        sign = 1 - 2 * way
+        at = chip - sign * hop
+        onward = chip + sign
+        have = (at >= 0) & (at < chips)
+        go = have & (onward >= 0) & (onward < chips)
+        return 2 * at + core, 2 * at + 1 - core, have, go, 2 * onward + core
+
+    keep = pltpu.make_async_copy(x_ref, gathered.at[me], local)
+    keep.start()
+    for way in (0, 1):
+        _, _, _, go, onward = spot(0, way)
+
+        @pl.when(go)
+        def _():
+            line_copy(way, 0, x_ref, me, onward).start()
+
+    side_copy(0, 0, x_ref, me).start()
+    loads = [pltpu.make_async_copy(source, target, load.at[i]) for i, (source, target) in enumerate(zip(given, held))]
+    for copy in loads:
+        copy.start()
+    mail.begin()
+    for copy in loads:
+        copy.wait()
+    keep.wait()
+
+    def event(number, _):
+        later = jnp.maximum(number - 2, 0)
+        hop = 1 + lax.div(later, 4)
+        kind = lax.rem(later, 4)
+        way = lax.rem(kind, 2)
+
+        @pl.when(number == 1)
+        def _():
+            side_copy(0, 0, x_ref, sibling).wait_recv()
+
+        @pl.when((number >= 2) & (kind == 0))
+        def _():
+            for w in (0, 1):
+                block, _, have, go, onward = spot(hop, w)
+
+                @pl.when(have)
+                def _():
+                    line_copy(w, hop - 1, x_ref, block, sibling).wait_recv()
+                    side_copy(w, hop, gathered.at[block], block).start()
+
+                @pl.when(go)
+                def _():
+                    line_copy(w, hop, gathered.at[block], block, onward).start()
+
+        block, other, have, _, _ = spot(hop, way)
+
+        @pl.when((number >= 2) & (kind >= 2) & have)
+        def _():
+            side_copy(way, hop, x_ref, other).wait_recv()
+
+        block = jnp.where(kind >= 2, other, block)
+        block = jnp.where(number == 0, me, jnp.where(number == 1, sibling, block))
+
+        @pl.when((number < 2) | have)
+        def _():
+            consume(block, gathered, held, outs, more, number == 0)
+
+        return 0
+
+    events = 2 + 4 * (chips - 1)
+    lax.fori_loop(0, events, event, 0)
+    consume(None, gathered, held, outs, more, None)
+    for hop in range(chips):
+        for way in (0, 1):
+            block, other, have, go, onward = spot(hop, way)
+            if hop > 0:
+
+                @pl.when(have)
+                def _():
+                    side_copy(way, hop, gathered.at[block], block).wait_send()
+
+            if hop < chips - 1:
+
+                @pl.when(go)
+                def _():
+                    line_copy(way, hop, x_ref, block, onward).wait_send()
+
+    side_copy(0, 0, x_ref, me).wait_send()
+    mail.end(0)
+
+
+def feed_tokens(block, number, consume, given, results, scratch, parcels=()):
+    n = lax.axis_size("ctx")
+    rows, width = block.shape
+    vmem = pl.BlockSpec(memory_space=pltpu.VMEM)
+    anywhere = pl.BlockSpec(memory_space=pl.ANY)
+    return talk(
+        functools.partial(feed_core, consume),
+        [block] + list(given),
+        [anywhere] * (1 + len(given)),
+        list(results),
+        [vmem] * len(results),
+        [pltpu.VMEM((n, rows, width), block.dtype)]
+        + [pltpu.VMEM(g.shape, g.dtype) for g in given]
+        + list(scratch)
+        + [pltpu.SemaphoreType.DMA((2, n // 2))] * 4
+        + [pltpu.SemaphoreType.DMA, pltpu.SemaphoreType.DMA((len(given),))],
+        list(parcels),
+        number,
+        56 << 20,
+        "feed_tokens",
+    )
+
+
+def reduce_core(job, count, n, ins, outs, own, mail):
+    terms = (len(ins) - count) // 2
+    pairs = list(zip(ins[:terms], ins[terms : 2 * terms]))
     o_ref = outs[0]
     total, to_side, from_side, inbox, side_send, side_recv, send, recv = own
     chips = n // 2
@@ -688,7 +814,7 @@
 
     def partial(block):
         place = pl.ds(pl.multiple_of(block * rows, rows), rows)
-        return sum(jnp.dot(a[place, :], w[...], preferred_element_type=jnp.float32) for a, w in pairs)
+        return sum(contract(a[place, :], w[...], 1, 0 if w.shape[0] == a.shape[1] else 1) for a, w in pairs)
 
     def side_copy(dest):
         return ctx_copy(to_side.at[dest], from_side.at[dest], side_send.at[dest], side_recv.at[dest], sibling)
@@ -698,14 +824,20 @@
 
     mail.begin()
 
-    def begin(k, _):
-        dest = jnp.where(chip >= chips // 2, k, chips - 1 - k)
+    flip = chip >= chips // 2
+    near = jnp.where(flip, chips - 1 - chip, chip)
+    lead = chips - 1 - 2 * near
+
+    def begin(k):
+        later = jnp.maximum(k - lead, 0)
+        high = chips - 1 - jnp.minimum(k, lead) - lax.div(later, 2)
+        dest = jnp.where(lax.rem(later, 2) == 1, lax.div(later, 2), high)
+        dest = jnp.where(flip, chips - 1 - dest, dest)
         to_side[dest] = partial(2 * dest + 1 - core).astype(jnp.bfloat16)
         side_copy(dest).start()
         total[dest] = partial(2 * dest + core)
-        return 0
-
-    lax.fori_loop(0, chips, begin, 0)
+
+    begin(0)
 
     def spot(tick, way):
         far = (chips - 1 - chip) if way == 0 else chip
@@ -715,6 +847,10 @@
         return far, k, dest, active, (me - 2 if way == 0 else me + 2)
 
     def advance(tick, _):
+        @pl.when(tick < chips - 1)
+        def _():
+            begin(tick + 1)
+
         for way in (0, 1):
             far, k, dest, active, onward = spot(tick, way)
             before = dest - 1 if way == 0 else dest + 1
@@ -736,6 +872,8 @@
                 from_side[dest] = total[dest].astype(jnp.bfloat16)
                 line_copy(way, dest, onward).start()
 
+        if job:
+            job(tick, ins[: len(ins) - count], ins[len(ins) - count :], outs[1:])
         return 0
 
     lax.fori_loop(0, chips, advance, 0)
@@ -769,28 +907,28 @@
     mail.end(0)
 
 
-def reduce_tokens(lefts, rights, number, parcels=()):
+def reduce_tokens(lefts, rights, number, parcels=(), job=None, job_in=(), job_out=()):
     n = lax.axis_size("ctx")
     chips = n // 2
-    rows, width = lefts[0].shape[0] // n, rights[0].shape[1]
+    rows, width = lefts[0].shape[0] // n, D
     buffer = lambda *lead: pltpu.VMEM(lead + (rows, width), jnp.bfloat16)
     vmem = pl.BlockSpec(memory_space=pltpu.VMEM)
 
     outs, extra = talk(
-        reduce_core,
-        lefts + rights,
-        [vmem] * (2 * len(lefts)),
-        [jax.ShapeDtypeStruct((rows, width), jnp.float32)],
-        [vmem],
+        functools.partial(reduce_core, job, len(job_in)),
+        lefts + rights + list(job_in),
+        [vmem] * (2 * len(lefts) + len(job_in)),
+        [jax.ShapeDtypeStruct((rows, width), jnp.float32)] + list(job_out),
+        [vmem] * (1 + len(job_out)),
         [pltpu.VMEM((chips, rows, width), jnp.float32), buffer(chips), buffer(chips), buffer(chips + 1)]
         + [pltpu.SemaphoreType.DMA((chips,))] * 3
         + [pltpu.SemaphoreType.DMA((chips + 1,))],
         list(parcels),
         number,
-        56 << 20,
+        (56 if chips <= 4 else 60) << 20,
         "reduce_tokens",
     )
-    return outs[0], extra
+    return outs, extra
 
 
 def total_core(n, ins, outs, own, mail):
@@ -949,7 +1087,7 @@
     in_send = pad_to(w_in.reshape(depth, chunks, half, sub).transpose(2, 1, 0, 3), subp, 3)
     head_send = jnp.concatenate([w_query, w_keyval], 1)
     ff_send = jnp.concatenate(
-        [w.reshape(depth, n // m, m, unit_sub).transpose(2, 1, 0, 3) for w in (w_gate, w_up)], 3
+        [pad_to(w.reshape(depth, n // m, m, unit_sub).transpose(2, 1, 0, 3), unit_pad, 3) for w in (w_gate, w_up)], 3
     )
     small_send = jnp.concatenate(
         [x_proj, dt_proj, a_log, conv_taps, conv_bias[:, None], dt_bias[:, None], skip_gain[:, None]], 1
@@ -996,6 +1134,7 @@
 
     hidden = tokens[0].astype(F32)
     normed_all = norm_forward(tokens_all.reshape(length, D).astype(F32), gain_set[0])[0].astype(BF)
+    normed_all = lax.optimization_barrier(normed_all)
     factor_one = norm_forward(hidden, gain_set[0])[1]
 
     inner_low = matmul(normed_all, in_weight).astype(BF)
@@ -1015,41 +1154,48 @@
             Parcel(0, "lanes", "fsdp", 1),
         ],
     )
-    head_weight = head_cols_all.reshape(D, m, head_pad)
-    query_weight = head_weight[:, :, :q_part].reshape(D, heads * HD)
-    kv_weight = head_weight[:, :, q_part : q_part + kv_part].reshape(D, 2 * slots * HD)
-    query_t = contract(query_weight, normed_all, 0, 1).astype(BF) * BF(HD**-0.5)
-    kv = matmul(normed_all, kv_weight).astype(BF).reshape(length, 2, slots, HD)
-    keys, values = kv[:, 0].transpose(1, 0, 2), kv[:, 1].transpose(1, 0, 2)
-    (attn_part, lse), (mamba_all, down_all, ff_cols) = attend(
+    head_weight = head_cols_all.reshape(D, m * head_pad)
+
+    head_t = contract(head_weight, normed_all, 0, 1).astype(BF).reshape(m, head_pad, length)
+    query_t = head_t[:, :q_part].reshape(heads * HD, length) * BF(HD**-0.5)
+    kv_t = head_t[:, q_part : q_part + kv_part].reshape(2, slots, HD, length)
+    keys_t, values_t = kv_t[0], kv_t[1]
+    keys, values = jnp.swapaxes(keys_t, 1, 2), jnp.swapaxes(values_t, 1, 2)
+    (attn_part, lse), (mamba_all, ff_cols) = attend(
         query_t,
         keys,
-        jnp.swapaxes(values, 1, 2),
+        values_t,
         [
-            Parcel(w_mamba_out, "gather", "fsdp", BULK),
-            Parcel(w_down, "gather", "fsdp", BULK),
-            Parcel(ff_all.reshape(n, depth, 2 * unit_sub), "swap", "ctx", BULK),
+            Parcel(wide_chans(w_mamba_out).T, "gather", "fsdp", BULK),
+            Parcel(ff_all.reshape(n, depth, 2 * unit_pad), "swap", "ctx", BULK),
         ],
         11,
     )
     attn_part = attn_part.reshape(heads * HD, n, rows).transpose(1, 0, 2)
-    mamba_weight = wide_chans(mamba_all.transpose(1, 0, 2).reshape(chans, D))
-    down_weight = pad_to(down_all.transpose(1, 0, 2).reshape(m, unit_sub, D), unit_pad, 1).reshape(unit_wide, D)
-    ff_parts = pad_to(ff_cols.reshape(D, 2, unit_sub).transpose(1, 2, 0), unit_pad, 1)
+    mamba_weight_t = mamba_all.reshape(D, wide)
+    ff_parts = ff_cols.reshape(D, 2 * unit_pad).T.reshape(2, unit_pad, D)
 
     dt_in_t = xdbl_t[:R]
-    b_wide = jnp.broadcast_to(xdbl_t[R : R + DS].T.astype(F32)[:, :, None], (length, DS, 128))
-    c_wide = jnp.broadcast_to(xdbl_t[R + DS : R + 2 * DS].T.astype(F32)[:, :, None], (length, DS, 128))
+    b_wide = jnp.broadcast_to(xdbl_t[R : R + DS].T[:, :, None], (length, DS, 128))
+    c_wide = jnp.broadcast_to(xdbl_t[R + DS : R + 2 * DS].T[:, :, None], (length, DS, 128))
     dt_pre = contract(dt_in_t, dtproj_weight, 0, 1) + dt_bias_vec
     step_size = jax.nn.softplus(dt_pre)
-    (state_rows, starts), (attn_t,) = ssm_forward(
-        step_size, ssm_in, b_wide, c_wide, rate, [Parcel(attn_part, "swap", "ctx", BULK)], 12
-    )
+    down_send = pad_to(w_down.T.reshape(-1, m, unit_sub), unit_pad, 2).reshape(-1, unit_wide)
+    (state_rows, starts), (attn_t, down_all) = ssm_forward(
+        step_size,
+        ssm_in,
+        b_wide,
+        c_wide,
+        rate,
+        [Parcel(attn_part, "swap", "ctx", BULK), Parcel(down_send, "gather", "fsdp", BULK)],
+        12,
+    )
+    down_weight_t = down_all.reshape(D, unit_wide)
     ssm_out = state_rows + skip_vec * ssm_in
     gate_z = jax.nn.silu(z_branch)
     mixed_low = (ssm_out * gate_z).astype(BF)
-    mamba_proj, (attn_weight_t,) = reduce_tokens(
-        [mixed_low], [mamba_weight], 2, [Parcel(attn_rows.reshape(H * HD, -1).T, "gather", "fsdp", BULK)]
+    (mamba_proj,), (attn_weight_t,) = reduce_tokens(
+        [mixed_low], [mamba_weight_t], 2, [Parcel(attn_rows.reshape(H * HD, -1).T, "gather", "fsdp", BULK)]
     )
     attn_t = attn_t.reshape(n * heads * HD, rows)[: H * HD]
     attn_weight_t = attn_weight_t.reshape(D, H * HD)
@@ -1068,24 +1214,70 @@
     gate_rows, up_rows = gate_rows.reshape(unit_wide, D), up_rows.reshape(unit_wide, D)
     gate_pre = matmul_nt(ffn_all, gate_rows)
     up_pre = matmul_nt(ffn_all, up_rows)
-    gate_act = jax.nn.silu(gate_pre)
-    hidden_act = (gate_act * up_pre).astype(BF)
-    layer_out = residual + reduce_tokens([hidden_act], [down_weight], 4)[0]
+    hidden_act = (jax.nn.silu(gate_pre) * up_pre).astype(BF)
+    layer_out = residual + reduce_tokens([hidden_act], [down_weight_t], 4)[0][0]
 
     mismatch = layer_out - teacher[0].astype(F32)
     error_part = jnp.sum(mask_rows[:, None] * mismatch * mismatch)
     grad_layer = out_grad[0].astype(F32) + 2.0 / (valid_sum * D) * mask_rows[:, None] * mismatch
-    (grad_ffn_all,), _ = share_tokens([grad_layer.astype(BF)], 5)
-    grad_ffn_all = grad_ffn_all.reshape(length, D)
-    grad_act = matmul_nt(grad_ffn_all, down_weight)
-    grad_gate = (grad_act * up_pre * silu_slope(gate_pre)).astype(BF)
-    grad_up = (grad_act * gate_act).astype(BF)
-    down_grad = matmul_tn(grad_ffn_all, hidden_act).astype(BF).reshape(m, D // m, unit_wide)
-    grad_ffn_in, (down_grad,) = reduce_tokens(
-        [grad_gate, grad_up], [gate_rows, up_rows], 6, [Parcel(down_grad, "swap", "fsdp", BULK)]
-    )
+
+    def feed_forward_back(block, x, held, outs, more, first):
+        if block is None:
+            outs[2][...] = more[0][...].astype(BF).reshape(outs[2].shape)
+            return
+        place = pl.ds(pl.multiple_of(block * rows, rows), rows)
+        weight, gates, ups, acts = held
+        grad = x[block]
+        slope = contract(grad, weight[...], 1, 0)
+        gate, up = gates[place, :], ups[place, :]
+        sigmoid_v = 1.0 / (1.0 + jnp.exp(-gate))
+        outs[0][place, :] = (slope * up * (sigmoid_v * (1.0 + gate * (1.0 - sigmoid_v)))).astype(BF)
+        outs[1][place, :] = (slope * (gate * sigmoid_v)).astype(BF)
+        part = contract(grad, acts[place, :], 0, 0)
+
+        @pl.when(first)
+        def _():
+            more[0][...] = part
+
+        @pl.when(jnp.logical_not(first))
+        def _():
+            more[0][...] += part
+
+    (grad_gate, grad_up, down_grad), _ = feed_tokens(
+        grad_layer.astype(BF),
+        5,
+        feed_forward_back,
+        [down_weight_t, gate_pre, up_pre, hidden_act],
+        [jax.ShapeDtypeStruct((length, unit_wide), BF)] * 2 + [jax.ShapeDtypeStruct((m, D // m, unit_wide), BF)],
+        [pltpu.VMEM((D, unit_wide), F32)],
+    )
+    grad_parts = [jax.ShapeDtypeStruct((m, unit_pad, D), BF)] * 2
+
+    def unit_grads(tick, given, more, outs):
+        for piece in range(m):
+
+            @pl.when(tick == piece * n // (2 * m))
+            def _():
+                for left, out in zip(given, outs):
+                    part = left[:, piece * unit_pad : (piece + 1) * unit_pad]
+                    out[piece] = contract(part, more[0][...], 0, 0).astype(BF)
+
+    inside = length * D <= 4 << 20
+    reduced, (down_grad,) = reduce_tokens(
+        [grad_gate, grad_up],
+        [gate_rows, up_rows],
+        6,
+        [Parcel(down_grad, "swap", "fsdp", BULK)],
+        unit_grads if inside else None,
+        [ffn_all] if inside else [],
+        grad_parts if inside else [],
+    )
+    grad_ffn_in = reduced[0]
     down_grad = jnp.sum(down_grad.astype(F32), 0).T.reshape(m, unit_pad, D // m)[:, :unit_sub].reshape(units, D // m)
-    gate_grad, up_grad = [matmul_tn(g, ffn_all).astype(BF).reshape(m, unit_pad, D) for g in (grad_gate, grad_up)]
+    if inside:
+        gate_grad, up_grad = reduced[1:]
+    else:
+        gate_grad, up_grad = [matmul_tn(g, ffn_all).astype(BF).reshape(m, unit_pad, D) for g in (grad_gate, grad_up)]
 
     grad_norm_res, gain_four = norm_backward(residual, factor_ffn, gain_set[3], grad_ffn_in)
     grad_resid = grad_layer + grad_norm_res
@@ -1093,23 +1285,49 @@
     grad_attn_proj, gain_two = norm_backward(attn_proj, factor_attn, gain_set[1], half_grad)
     grad_mamba_proj, gain_three = norm_backward(mamba_proj, factor_mamba, gain_set[2], half_grad)
     grad_attn_proj_low = grad_attn_proj.astype(BF)
-    (grad_mamba_all,), (gate_grad, up_grad) = share_tokens(
-        [grad_mamba_proj.astype(BF)],
+
+    def state_space_back(block, x, held, outs, more, first):
+        if block is None:
+            outs[2][...] = more[0][...].astype(BF).reshape(outs[2].shape)
+            return
+        place = pl.ds(pl.multiple_of(block * rows, rows), rows)
+        weight, z_part, rows_out, mixed = held
+        grad = x[block]
+        slope = contract(grad, weight[...], 1, 0)
+        z = z_part[place, :].astype(F32)
+        sigmoid_v = 1.0 / (1.0 + jnp.exp(-z))
+        outs[0][place, :] = slope * (z * sigmoid_v)
+        outs[1][place, :] = (slope * rows_out[place, :] * (sigmoid_v * (1.0 + z * (1.0 - sigmoid_v)))).astype(BF)
+        part = contract(grad, mixed[place, :], 0, 0)
+
+        @pl.when(first)
+        def _():
+            more[0][...] = part
+
+        @pl.when(jnp.logical_not(first))
+        def _():
+            more[0][...] += part
+
+    (grad_y, grad_z, mamba_out_grad), (gate_grad, up_grad) = feed_tokens(
+        grad_mamba_proj.astype(BF),
         7,
+        state_space_back,
+        [mamba_weight_t, inner_low[:, wide:], ssm_out, mixed_low],
+        [
+            jax.ShapeDtypeStruct((length, wide), F32),
+            jax.ShapeDtypeStruct((length, wide), BF),
+            jax.ShapeDtypeStruct((m, D // m, wide), BF),
+        ],
+        [pltpu.VMEM((D, wide), F32)],
         [Parcel(gate_grad, "swap", "fsdp", BULK), Parcel(up_grad, "swap", "fsdp", BULK)],
     )
-    grad_mamba_all = grad_mamba_all.reshape(length, D)
     ff_grad = jnp.stack([jnp.sum(g.astype(F32), 0).astype(BF) for g in (gate_grad, up_grad)])
     ff_grad = ff_grad.reshape(2 * unit_pad, n, depth).transpose(1, 0, 2)
     attn_out_grad = contract(grad_attn_proj_low, attn_t, 0, 1).astype(BF).reshape(m, D // m, H * HD)
     grad_attn = contract(attn_weight_t, grad_attn_proj_low, 0, 1).astype(BF)
     grad_attn = pad_to(grad_attn, n * heads * HD, 0).reshape(n, heads * HD, rows)
 
-    mamba_out_grad = matmul_tn(grad_mamba_all, mixed_low).astype(BF).reshape(m, D // m, wide)
-    grad_mixed = matmul_nt(grad_mamba_all, mamba_weight)
-    grad_y = grad_mixed * gate_z
-    grad_z = grad_mixed * ssm_out * silu_slope(z_branch)
-    z_grad = matmul_tn(normed_all, grad_z.astype(BF)).astype(BF)
+    z_grad = matmul_tn(normed_all, grad_z).astype(BF)
     step_grad, along_b, b_grad, c_grad, a_accum, (attn_out_grad, grad_attn) = ssm_backward(
         step_size,
         ssm_in,
@@ -1130,28 +1348,28 @@
         query_t,
         grad_attn,
         keys,
-        jnp.swapaxes(keys, 1, 2),
+        keys_t,
         values,
         lse,
         [Parcel(ff_grad, "swap", "ctx", BULK), Parcel(mamba_out_grad, "swap", "fsdp", BULK)],
         14,
     )
-    grad_kv = jnp.stack([grad_keys, grad_values]).astype(BF).transpose(2, 0, 1, 3).reshape(length, 2 * slots * HD)
+    grad_kv = jnp.concatenate([grad_keys, grad_values], 0).astype(BF).reshape(m, kv_part, length)
+    grad_head_t = jnp.concatenate([grad_query.reshape(m, q_part, length), grad_kv], 1)
+    grad_head_t = pad_to(grad_head_t, head_pad, 1).reshape(m * head_pad, length)
     mamba_out_grad = true_chans(jnp.sum(mamba_out_grad.astype(F32), 0).T)
-    query_grad = contract(grad_query, normed_all, 1, 0).astype(BF).reshape(m, q_part, D)
-    kv_grad = matmul_tn(grad_kv, normed_all).astype(BF).reshape(m, kv_part, D)
+    head_grad = contract(grad_head_t, normed_all, 1, 0).astype(BF).reshape(m, head_pad, D)
 
     grad_dt_pre = (step_grad * jax.nn.sigmoid(dt_pre)).astype(BF)
     dtproj_grad = contract(grad_dt_pre, dt_in_t, 0, 1)
     grad_xdbl_t = jnp.concatenate([contract(dtproj_weight, grad_dt_pre, 0, 1), b_grad.T, c_grad.T], 0)
-    grad_xdbl_t, (query_grad, kv_grad) = total_columns(
+    grad_xdbl_t, (head_grad,) = total_columns(
         pad_to(grad_xdbl_t, feats, 0),
         8,
-        [Parcel(query_grad, "swap", "fsdp", BULK), Parcel(kv_grad, "swap", "fsdp", BULK)],
+        [Parcel(head_grad, "swap", "fsdp", BULK)],
     )
     grad_xdbl_t = grad_xdbl_t[: R + 2 * DS]
-    head_grad = jnp.concatenate([jnp.sum(query_grad.astype(F32), 0), jnp.sum(kv_grad.astype(F32), 0)], 0)
-    head_grad = pad_to(head_grad.astype(BF).T, head_pad, 1).reshape(n, depth, head_pad)
+    head_grad = jnp.sum(head_grad.astype(F32), 0).astype(BF).T.reshape(n, depth, head_pad)
     xproj_grad = contract(ssm_low, grad_xdbl_t, 0, 1)
     grad_ssm_in = step_size * along_b + skip_vec * grad_y + contract(grad_xdbl_t, xproj_weight, 0, 1)
     grad_pre = grad_ssm_in * silu_slope(pre_conv)
@@ -1175,14 +1393,22 @@
     )
     small_grad = true_chans(small_grad).reshape(m, chans // m, -1)
 
+    def used(array, dim):
+        if head_pad == q_part + kv_part:
+            return array
+        split = array.reshape(array.shape[:dim] + (m, head_pad) + array.shape[dim + 1 :])
+        return lax.slice_in_dim(split, 0, q_part + kv_part, 1, dim + 1).reshape(
+            array.shape[:dim] + (-1,) + array.shape[dim + 1 :]
+        )
+
     def by_lanes(ref, peer, shape):
         if ref is None:
             return (shape[0], subp)
         return ref.at[:, pl.ds(pl.multiple_of(peer * subp, subp), subp)]
 
-    grad_normed, (ff_grad, small_grad, in_grad, head_grad) = reduce_tokens(
-        [grad_query.T, grad_kv, grad_x.astype(BF), grad_z.astype(BF)],
-        [query_weight.T, kv_weight.T, in_weight[:, :wide].T, in_weight[:, wide:].T],
+    (grad_normed,), (ff_grad, small_grad, in_grad, head_grad) = reduce_tokens(
+        [used(grad_head_t, 0).T, grad_x.astype(BF), grad_z],
+        [used(head_weight, 1), in_weight[:, :wide], in_weight[:, wide:]],
         9,
         [
             Parcel(ff_grad.reshape(m, n // m, 2, unit_pad, depth), "swap", "fsdp", BULK),

time: 1420 us -> 1330 us (0.937)
  matrix products: 153 us -> 89.1 us
  local copies, waits for them, and re-layouts: 240 us -> 218 us
    dot_general x22 -> x14, matrix products: 148 us -> 86.1 us  [contract(): lax.dot_general(left, right, (((left_dim,), (right_dim,)), ((), ())), pre...]
    unnamed x340 -> x318, local copies, waits for them, and re-layouts: 92.4 us -> 72.6 us
  transfers between devices with their start and end apart: 1 -> 1, of which waited for: 0 -> 0; matrix products, arithmetic and copies ran while one was open for 12% -> 12% of each run, Pallas kernels for 14% -> 15%
where the time goes in v2:
time: 1330 us; the launch traced here: 1320 us
  Pallas kernels  891 us (67%)
  local copies, waits for them, and re-layouts  218 us (16%)
  other arithmetic  98.8 us (7%)
  matrix products  89.1 us (7%)
  between operations  18.8 us (1%)
    pallas_call x15, Pallas kernels, talk(): pl.pallas_call(kernel, grid=(steps,) if steps else (), out_shape=list(out...  891 us
    dot_general x14, matrix products, contract(): lax.dot_general(left, right, (((left_dim,), (right_dim,)), ((), ())), pre...  86.1 us
    unnamed x318, local copies, waits for them, and re-layouts  72.6 us
  transfers between devices with their start and end apart: 1, of which 0 were waited for; matrix products, arithmetic and copies ran while one was open for 12% of the time, Pallas kernels for 15%

profile of v2, /device:TPU:9, one launch (start us, length us, event | category | flops | bytes accessed | tf_op | source)
XLA Modules:
  0.0 1315.6 jit_solution(8988041255590319657)
XLA Ops:
  28.3 95.3 %share_tokens.2 = (bf16[8,256,1600]{2,1,0:T(8,128)(2,1)S(1)}, bf16[8,200,400]{2,1,0:T(8,128)(2,1)S(1)}, bf16[2,4,200,256]{3,2,1,0:T(8,128)(2,1)}, f32[4,8,256]{2...) custom-call(bf16[256,1600]{1,0:T(8,128)(2,1)S(1)} %bitcast.276, ...), custom_call_target="tpu_custom_call" | custom-call | tf_op jit(solution)/shard_map/share_tokens/pallas_call | solution.py:575
  138.6 4.5 multiply_reduce_fusion
  143.4 4.4 fusion.1
  147.8 10.1 convolution_convert_fusion.1
  178.7 49.1 %total_columns.2 = (bf16[144,2048]{1,0:T(8,128)(2,1)S(1)}, bf16[8,200,128]{2,1,0:T(8,128)(2,1)}, bf16[8,200,512]{2,1,0:T(8,128)(2,1)S(1)}) custom-call(f32[144,2048]{1,0:T(8,128)S(1)} %pad.76.refs_0_, bf16[8,200,128]{2,1,0:T(8,128)(2,1)S(1)} %bitcast.302), custom_call_target="tpu_custom_call" | custom-call | tf_op jit(solution)/shard_map/total_columns/pallas_call | solution.py:575
  228.6 7.9 convolution_convert_fusion.5
  245.7 39.8 %attend.1 = (bf16[256,2048]{1,0:T(8,128)(2,1)S(1)}, f32[8,2048]{1,0:T(8,128)S(1)}, bf16[4,400,512]{2,1,0:T(8,128)(2,1)S(1)}, bf16[8,200,352]{2,1,0:T(8,128)(2,1)S(1)}) custom-call(bf16[256,2048]{1,0:T(8,128)(2,1)S(1)} %bitcast.279, bf16[2,2048,64]{2,1,0:T(8,128)(2,1)S(1)} %copy.446.refs_1_.refs_2_, bf16[2,64,2048]{2,1,0:T(8,128)(2,1)S(1)} %get-tuple-element.290.refs_2_, ...), custom_call_target="tpu_custom_call" | custom-call | tf_op jit(solution)/shard_map/attend/pallas_call | solution.py:575
  295.9 6.8 compare_select_fusion
  321.4 10.0 broadcast_in_dim.17.refs_2_.refs_3_
  331.4 9.9 broadcast_in_dim.18.refs_3_.refs_4_
  341.4 31.8 %ssm_forward.1 = (f32[2048,512]{1,0:T(8,128)S(1)}, f32[16,16,512]{2,1,0:T(8,128)S(1)}, bf16[8,256,256]{2,1,0:T(8,128)(2,1)S(1)}, bf16[4,400,704]{2,1,0:T(8,128)(2,1)S(1)}) custom-call(f32[2048,512]{1,0:T(8,128)S(1)} %copy-done.6, f32[2048,512]{1,0:T(8,128)S(1)} %copy-done.1, bf16[2048,16,128]{2,1,0:T(8,128)(2,1)} %broadcast_in_dim.17.refs_2_.refs_3_, ...), custom_call_target="tpu_custom_call" | custom-call | tf_op jit(solution)/shard_map/ssm_forward/pallas_call | solution.py:575
  377.2 66.8 %reduce_tokens.4 = (f32[256,1600]{1,0:T(8,128)}, bf16[4,400,1600]{2,1,0:T(8,128)(2,1)}) custom-call(bf16[2048,512]{1,0:T(8,128)(2,1)} %get-tuple-element.276.refs_0_.refs_4_, bf16[1600,512]{1,0:T(8,128)(2,1)} %bitcast.285, bf16[400,1600]{1,0:T(8,128)(2,1)} %bitcast.327), custom_call_target="tpu_custom_call" | custom-call | tf_op jit(solution)/shard_map/reduce_tokens/pallas_call | solution.py:575
  444.0 5.4 multiply_reduce_fusion.14
  457.0 4.5 multiply_reduce_fusion.12
  473.7 57.2 %share_tokens.3 = (bf16[8,256,1600]{2,1,0:T(8,128)(2,1)S(1)}, bf16[4,176,1600]{2,1,0:T(8,128)(2,1)S(1)}, bf16[4,176,1600]{2,1,0:T(8,128)(2,1)S(1)}) custom-call(bf16[256,1600]{1,0:T(8,128)(2,1)S(1)} %multiply_convert_fusion.2.refs_0_, bf16[176,1600]{1,0:T(8,128)(2,1)S(1)} %copy-done.18, bf16[176,1600]{1,0:T(8,128)(2,1)S(1)} %copy-done.17), custom_call_target="tpu_custom_call" | custom-call | tf_op jit(solution)/shard_map/share_tokens/pallas_call | solution.py:575
  531.0 7.9 fusion.65.refs_2_
  538.9 10.6 multiply_convert_fusion
  549.5 71.8 %reduce_tokens.5 = f32[256,1600]{1,0:T(8,128)} custom-call(bf16[2048,704]{1,0:T(8,128)(2,1)} %get-tuple-element.323.refs_0_.refs_4_, bf16[1600,704]{1,0:T(8,128)(2,1)} %bitcast.277), custom_call_target="tpu_custom_call" | custom-call | tf_op jit(solution)/shard_map/reduce_tokens/pallas_call | solution.py:575
  625.9 62.5 %feed_tokens.2 = (bf16[2048,704]{1,0:T(8,128)(2,1)}, bf16[2048,704]{1,0:T(8,128)(2,1)}, bf16[4,400,704]{2,1,0:T(8,128)(2,1)}) custom-call(bf16[256,1600]{1,0:T(8,128)(2,1)} %fusion.52.refs_0_, bf16[1600,704]{1,0:T(8,128)(2,1)} %bitcast.278, f32[2048,704]{1,0:T(8,128)} %fusion.65.refs_2_, f32[2048,704]{1,0:T(8,128)} %get-tuple-element.324.refs_3_, ...), custom_call_target="tpu_custom_call" | custom-call | tf_op jit(solution)/shard_map/feed_tokens/pallas_call | solution.py:575
  688.4 84.7 %reduce_tokens.6 = (f32[256,1600]{1,0:T(8,128)}, bf16[4,176,1600]{2,1,0:T(8,128)(2,1)}, bf16[4,176,1600]{2,1,0:T(8,128)(2,1)}, bf16[4,400,704]{2,1,0:T(8,128)(2,1)}) custom-call(bf16[2048,704]{1,0:T(8,128)(2,1)} %get-tuple-element.95.refs_0_, bf16[2048,704]{1,0:T(8,128)(2,1)} %get-tuple-element.96.refs_1_, bf16[704,1600]{1,0:T(8,128)(2,1)} %bitcast.296, ...), custom_call_target="tpu_custom_call" | custom-call | tf_op jit(solution)/shard_map/reduce_tokens/pallas_call | solution.py:575
  787.6 60.7 %feed_tokens.3 = (f32[2048,512]{1,0:T(8,128)}, bf16[2048,512]{1,0:T(8,128)(2,1)}, bf16[4,400,512]{2,1,0:T(8,128)(2,1)}, bf16[4,176,1600]{2,1,0:T(8,128)(2,1)}, bf16[4,176,1600]{2,1,0:T(8,128)(2,1)}) custom-call(bf16[256,1600]{1,0:T(8,128)(2,1)} %get-tuple-element.292.refs_0_, bf16[1600,512]{1,0:T(8,128)(2,1)} %bitcast.286, ...), custom_call_target="tpu_custom_call" | custom-call | tf_op jit(solution)/shard_map/feed_tokens/pallas_call | solution.py:575
  848.3 78.3 %ssm_backward.1 = (f32[2048,512]{1,0:T(8,128)S(1)}, f32[2048,512]{1,0:T(8,128)S(1)}, f32[16,8,2048]{2,1,0:T(8,128)S(1)}, f32[16,8,2048]{2,1,0:T(8,128)S(1)}, f32...) custom-call(f32[2048,512]{1,0:T(8,128)} %get-tuple-element.319.refs_0_, ...), custom_call_target="tpu_custom_call" | custom-call | tf_op jit(solution)/shard_map/ssm_backward/pallas_call | solution.py:575
  934.3 4.8 reduce_sum.331
  943.9 4.8 convert_reduce_fusion.1
  968.9 48.0 %attend_back.1 = (bf16[256,2048]{1,0:T(8,128)(2,1)S(1)}, f32[2,64,2048]{2,1,0:T(8,128)S(1)}, f32[2,64,2048]{2,1,0:T(8,128)S(1)}, bf16[8,352,200]{2,1,0:T(8,128)(2,1)S(1)}, bf16[4,400,512]{2,1,0:T(8,128)(2,1)S(1)}) custom-call(bf16[256,2048]{1,0:T(8,128)(2,1)S(1)} %bitcast.280, bf16[256,2048]{1,0:T(8,128)(2,1)S(1)} %bitcast.291, ...), custom_call_target="tpu_custom_call" | custom-call | tf_op jit(solution)/shard_map/attend_back/pallas_call | solution.py:575
  1018.6 9.3 convolution_convert_fusion.4
  1050.1 26.0 %total_columns.3 = (bf16[144,2048]{1,0:T(8,128)(2,1)S(1)}, bf16[4,128,1600]{2,1,0:T(8,128)(2,1)S(1)}) custom-call(f32[144,2048]{1,0:T(8,128)S(1)} %select_maximum_fusion.refs_0_, bf16[4,128,1600]{2,1,0:T(8,128)(2,1)S(1)} %bitcast.281), custom_call_target="tpu_custom_call" | custom-call | tf_op jit(solution)/shard_map/total_columns/pallas_call | solution.py:575
  1079.7 5.9 multiply_multiply_fusion
  1091.0 8.9 convolution_convert_fusion.3
  1100.0 4.9 convolution_convert_fusion.2
  1121.4 75.4 %reduce_tokens.7 = (f32[256,1600]{1,0:T(8,128)}, bf16[4,2,2,176,200]{4,3,2,1,0:T(8,128)(2,1)}, f32[4,100,255]{2,1,0:T(8,128)}, bf16[4,1600,256]{2,1,0:T(8,128)(2,1)}, bf16[8,200,128]{2,1,0:T(8,128)(2,1)}) custom-call(bf16[2048,512]{1,0:T(8,128)(2,1)} %bitcast.320, bf16[2048,512]{1,0:T(8,128)(2,1)} %copy-done.71, ...), custom_call_target="tpu_custom_call" | custom-call | tf_op jit(solution)/shard_map/reduce_tokens/pallas_call | solution.py:575
  1203.5 43.7 %send_only.1 = (f32[8,4,8,256]{3,2,1,0:T(8,128)}, bf16[8,200,256]{2,1,0:T(8,128)(2,1)}, bf16[4,8,200,128]{3,2,1,0:T(8,128)(2,1)S(1)}, f32[4,8,8,256]{3,2,1,0:T(8,128)S(1)}, bf16[2,4,200,256]{3,2,1,0:T(8,128)(2,1)S(1)}) custom-call(f32[8,4,8,256]{3,2,1,0:T(8,128)S(1)} %pad_select_fusion.refs_0_, bf16[8,200,256]{2,1,0:T(8,128)(2,1)S(1)} %bitcast.294, ...), custom_call_target="tpu_custom_call" | custom-call | tf_op jit(solution)/shard_map/send_only/pallas_call | solution.py:575
  (488 shorter events, 285.2 us)
Async XLA Ops:
  7.2 1298.0 %reduce-scatter.4.cloned.1.call-start = ((), (), s32[]{:S(2)}) async-start(), calls=%async_computation.1 | async-start | bytes 1843200
  13.7 10.5 copy-start.136
  228.6 7.9 copy-start.24
  321.4 10.0 copy-start.87
  321.4 19.9 %copy-start.12 = (bf16[256,8,256]{2,0,1:T(8,128)(2,1)S(1)}, bf16[256,8,256]{2,0,1:T(8,128)(2,1)}, u32[]{:S(2)}) copy-start(bf16[256,8,256]{2,0,1:T(8,128)(2,1)} %copy.449) | copy-start | bytes 3145732
  321.4 19.9 %copy-start.16 = (bf16[400,704]{1,0:T(8,128)(2,1)S(1)}, bf16[400,704]{1,0:T(8,128)(2,1)}, u32[]{:S(2)}) copy-start(bf16[400,704]{1,0:T(8,128)(2,1)} %copy.451.refs_6_) | copy-start | bytes 1689604
  331.4 9.9 copy-start.1
  331.4 9.9 copy-start.6
  341.3 31.9 %copy-start.65 = (bf16[2048,1024]{1,0:T(8,128)(2,1)S(1)}, bf16[2048,1024]{1,0:T(8,128)(2,1)}, u32[]{:S(2)}) copy-start(bf16[2048,1024]{1,0:T(8,128)(2,1)} %copy-done.64) | copy-start | bytes 12582916
  341.3 31.9 %copy-start.124 = (f32[512,1]{0,1:T(1,128)S(1)}, f32[512,1]{0,1:T(1,128)}, u32[]{:S(2)}) copy-start(f32[512,1]{0,1:T(1,128)} %get-tuple-element.304) | copy-start | bytes 6148
  373.2 70.8 %copy-start.41 = (bf16[8,256,256]{2,1,0:T(8,128)(2,1)}, bf16[8,256,256]{2,1,0:T(8,128)(2,1)S(1)}, u32[]{:S(2)}) copy-start(bf16[8,256,256]{2,1,0:T(8,128)(2,1)S(1)} %get-tuple-element.88) | copy-start | bytes 3145732
  462.0 9.9 copy-start.118
  531.0 7.9 copy-start.19
  531.0 7.9 copy-start.9
  531.0 7.9 copy-start.20
  549.5 72.5 %copy-start.122 = (f32[1,256]{1,0:T(1,128)S(1)}, f32[1,256]{1,0:T(1,128)}, u32[]{:S(2)}) copy-start(f32[1,256]{1,0:T(1,128)} %convert_element_type.183) | copy-start | bytes 3076
  688.3 84.7 %copy-start.58 = (f32[256,1600]{1,0:T(8,128)S(1)}, f32[256,1600]{1,0:T(8,128)}, u32[]{:S(2)}) copy-start(f32[256,1600]{1,0:T(8,128)} %get-tuple-element.275) | copy-start | bytes 4915204
  688.3 84.7 %copy-start.61 = (f32[256,1600]{1,0:T(8,128)S(1)}, f32[256,1600]{1,0:T(8,128)}, u32[]{:S(2)}) copy-start(f32[256,1600]{1,0:T(8,128)} %reduce_tokens.5) | copy-start | bytes 4915204
  688.4 84.7 %copy-start.70 = (bf16[1,256,1600]{2,1,0:T(8,128)(2,1)S(1)}, bf16[1,256,1600]{2,1,0:T(8,128)(2,1)}, u32[]{:S(2)}) copy-start(bf16[1,256,1600]{2,1,0:T(8,128)(2,1)} %copy.461) | copy-start | bytes 2457604
  688.4 84.7 %copy-start.119 = (f32[256]{0:T(256)S(1)}, f32[256]{0:T(256)}, u32[]{:S(2)}) copy-start(f32[256]{0:T(256)} %copy-done.118) | copy-start | bytes 3076
  688.4 84.7 %copy-start.123 = (f32[1,256]{1,0:T(1,128)S(1)}, f32[1,256]{1,0:T(1,128)}, u32[]{:S(2)}) copy-start(f32[1,256]{1,0:T(1,128)} %convert_element_type.183) | copy-start | bytes 3076
  773.2 8.4 slice-start.2
  787.6 60.7 %copy-start.44 = (f32[16,16,512]{2,1,0:T(8,128)S(1)}, f32[16,16,512]{2,1,0:T(8,128)}, u32[]{:S(2)}) copy-start(f32[16,16,512]{2,1,0:T(8,128)} %copy-done.43) | copy-start | bytes 1572868
  943.9 8.1 copy-start.67
  1040.0 8.9 copy-start.77
  1048.9 28.4 %copy-start.3 = (f32[2048,512]{1,0:T(8,128)S(1)}, f32[2048,512]{1,0:T(8,128)}, u32[]{:S(2)}) copy-start(f32[2048,512]{1,0:T(8,128)} %copy-done) | copy-start | bytes 12582916
  1086.8 13.1 slice-start
  1091.0 8.9 copy-start.71
  1091.0 8.9 slice-start.1
  1091.0 8.9 copy-start.86
  1100.0 9.7 copy-start.51
  1252.0 38.6 %copy-start.80 = (f32[100,255]{1,0:T(8,128)}, f32[100,255]{1,0:T(8,128)S(1)}, u32[]{:S(2)}) copy-start(f32[100,255]{1,0:T(8,128)S(1)} %reduce_sum.334) | copy-start | bytes 306004
  (111 other events, 358.1 us)
Sparse Core Ops, SparseCore 0:
  942.7 28.3 reduce-scatter.3

commit v3 on v2

--- a/solution.py
+++ b/solution.py
@@ -932,7 +932,7 @@
 
 
 def total_core(n, ins, outs, own, mail):
-    (x_ref,), (o_ref,) = ins, outs
+    x_ref, o_ref = ins[0], outs[0]
     from_side, summed, inbox, outbox, side_send, side_recv, send, recv, out_send, out_recv, back_send, back_recv, local = own
     chips = n // 2
     me, core, chip, sibling = line_place(n)
@@ -988,10 +988,21 @@
             line_copy(d).wait_send()
             out_copy(d).wait_send()
     keep.wait()
+    for number, spread_ref in enumerate(outs[1:]):
+
+        def fill(part, _):
+            first = pl.multiple_of(part * 128, 128)
+            values = o_ref[number * DS : (number + 1) * DS, pl.ds(first, 128)].astype(jnp.float32)
+            for k in range(128):
+                column = jnp.broadcast_to(values[:, k : k + 1], (DS, 128))
+                spread_ref[first + k] = column.astype(jnp.bfloat16)
+            return 0
+
+        lax.fori_loop(0, o_ref.shape[1] // 128, fill, 0)
     mail.end(1)
 
 
-def total_columns(partial, number, parcels=()):
+def total_columns(partial, number, parcels=(), spreads=0):
     n = lax.axis_size("ctx")
     chips = n // 2
     feats, length = partial.shape
@@ -1001,19 +1012,20 @@
         total_core,
         [partial],
         [vmem],
-        [jax.ShapeDtypeStruct((feats, length), jnp.bfloat16)],
-        [vmem],
+        [jax.ShapeDtypeStruct((feats, length), jnp.bfloat16)]
+        + [jax.ShapeDtypeStruct((length, DS, 128), jnp.bfloat16)] * spreads,
+        [vmem] * (1 + spreads),
         [pltpu.VMEM((chips, feats, cols), jnp.float32)] * 3
         + [pltpu.VMEM((feats, cols), jnp.bfloat16)]
         + [pltpu.SemaphoreType.DMA((chips,))] * 8
         + [pltpu.SemaphoreType.DMA],
         list(parcels),
         number,
-        32 << 20,
+        48 << 20,
         "total_columns",
         everyone=True,
     )
-    return outs[0], extra
+    return outs, extra
 
 
 def send_core(n, ins, outs, own, mail):
@@ -1071,8 +1083,6 @@
     q_part = heads * HD // m
     kv_part = 2 * slots * HD // m
     head_pad = -(-(q_part + kv_part) // 128) * 128
-    bases = [min(heads * c, H - 1) // group_size for c in range(n)]
-    slot_heads = [[min(bases[c] + s, KVH - 1) for s in range(slots)] for c in range(n)]
 
     def wide_chans(array):
         array = array.reshape((half, sub) + array.shape[1:])
@@ -1117,20 +1127,34 @@
     valid_sum = jnp.sum(meta_all[:, :, 1, 0])
     in_weight = in_all.reshape(D, 2 * wide)
     small = wide_chans(small_all.reshape(chans, -1))
-    xproj_weight = small[:, : R + 2 * DS]
+    xproj_weight = jnp.concatenate([small[:, R : R + 2 * DS], small[:, :R]], 1)
     dtproj_weight = small[:, R + 2 * DS : 2 * R + 2 * DS]
     rest = small[:, 2 * R + 2 * DS :].astype(F32)
     amat = wide_chans(-jnp.exp(small_all.reshape(chans, -1)[:, 2 * R + 2 * DS : 2 * R + 3 * DS].astype(F32))).T
     rate = amat * LOG2E
     taps = rest[:, DS : DS + KC].T
     conv_bias_vec, dt_bias_vec, skip_vec = rest[:, DS + KC], rest[:, DS + KC + 1], rest[:, DS + KC + 2]
-    query_rows = head_all[:, :, : w_query.shape[1]].transpose(1, 0, 2).reshape(depth, H * HD)
-    query_rows = pad_to(query_rows, n * heads * HD, 1).reshape(depth, n, m, q_part)
-    kv_rows = head_all[:, :, w_query.shape[1] :].transpose(1, 0, 2).reshape(depth, 2, KVH, HD)
-    kv_rows = jnp.stack([jnp.stack([kv_rows[:, :, h] for h in slot_heads[c]], 2) for c in range(n)], 1)
-    kv_rows = kv_rows.reshape(depth, n, m, kv_part)
-    head_rows = lax.dynamic_index_in_dim(jnp.concatenate([query_rows, kv_rows], 3), fsdp_index, 2, False)
-    head_rows = pad_to(head_rows.transpose(1, 0, 2), head_pad, 2)
+    query_wide, kv_wide = w_query.shape[1], w_keyval.shape[1]
+    head_wide = query_wide + kv_wide
+
+    def natural_column(part, shard, lane):
+        query = heads * HD * shard + q_part * part + lane
+        query_at = query // query_wide * head_wide + query % query_wide
+        inner = kv_part * part + lane - q_part
+        base = jnp.minimum(heads * shard, H - 1) // group_size
+        kv_head = jnp.minimum(base + inner // HD % slots, KVH - 1)
+        kv_column = inner // (slots * HD) * (KVH * HD) + kv_head * HD + inner % HD
+        kv_at = kv_column // kv_wide * head_wide + query_wide + kv_column % kv_wide
+        at = jnp.where(lane < q_part, jnp.where(query < H * HD, query_at, -1), kv_at)
+        return jnp.where(lane < q_part + kv_part, at, -1)
+
+    def counted(*shape):
+        return [lax.broadcasted_iota(jnp.int32, shape, d) for d in range(len(shape))]
+
+    row, shard, lane = counted(m * head_wide, n, head_pad)
+    chosen = (row == natural_column(fsdp_index, shard, lane)).astype(BF).reshape(m, head_wide, n * head_pad)
+    head_rows = sum(matmul(head_all[f], chosen[f]) for f in range(m)).astype(BF)
+    head_rows = head_rows.reshape(depth, n, head_pad).transpose(1, 0, 2)
 
     hidden = tokens[0].astype(F32)
     normed_all = norm_forward(tokens_all.reshape(length, D).astype(F32), gain_set[0])[0].astype(BF)
@@ -1146,13 +1170,14 @@
         pre_conv = pre_conv + taps[k] * padded[k : k + length]
     ssm_in = jax.nn.silu(pre_conv)
     ssm_low = ssm_in.astype(BF)
-    xdbl_t, (head_cols, head_cols_all) = total_columns(
+    (xdbl_t, b_wide, c_wide), (_, head_cols_all) = total_columns(
         pad_to(contract(xproj_weight, ssm_low, 0, 1), feats, 0),
         1,
         [
             Parcel(head_rows, "swap", "ctx", 0),
             Parcel(0, "lanes", "fsdp", 1),
         ],
+        2,
     )
     head_weight = head_cols_all.reshape(D, m * head_pad)
 
@@ -1161,12 +1186,15 @@
     kv_t = head_t[:, q_part : q_part + kv_part].reshape(2, slots, HD, length)
     keys_t, values_t = kv_t[0], kv_t[1]
     keys, values = jnp.swapaxes(keys_t, 1, 2), jnp.swapaxes(values_t, 1, 2)
+    row, column = counted(chans, wide)
+    chosen = (row // sub * subp + row % sub == column).astype(BF)
+    mamba_send = contract(w_mamba_out, chosen, 0, 0).astype(BF)
     (attn_part, lse), (mamba_all, ff_cols) = attend(
         query_t,
         keys,
         values_t,
         [
-            Parcel(wide_chans(w_mamba_out).T, "gather", "fsdp", BULK),
+            Parcel(mamba_send, "gather", "fsdp", BULK),
             Parcel(ff_all.reshape(n, depth, 2 * unit_pad), "swap", "ctx", BULK),
         ],
         11,
@@ -1175,12 +1203,12 @@
     mamba_weight_t = mamba_all.reshape(D, wide)
     ff_parts = ff_cols.reshape(D, 2 * unit_pad).T.reshape(2, unit_pad, D)
 
-    dt_in_t = xdbl_t[:R]
-    b_wide = jnp.broadcast_to(xdbl_t[R : R + DS].T[:, :, None], (length, DS, 128))
-    c_wide = jnp.broadcast_to(xdbl_t[R + DS : R + 2 * DS].T[:, :, None], (length, DS, 128))
+    dt_in_t = xdbl_t[2 * DS : 2 * DS + R]
     dt_pre = contract(dt_in_t, dtproj_weight, 0, 1) + dt_bias_vec
     step_size = jax.nn.softplus(dt_pre)
-    down_send = pad_to(w_down.T.reshape(-1, m, unit_sub), unit_pad, 2).reshape(-1, unit_wide)
+    row, column = counted(units, unit_wide)
+    chosen = (row // unit_sub * unit_pad + row % unit_sub == column).astype(BF)
+    down_send = contract(w_down, chosen, 0, 0).astype(BF)
     (state_rows, starts), (attn_t, down_all) = ssm_forward(
         step_size,
         ssm_in,
@@ -1362,8 +1390,8 @@
 
     grad_dt_pre = (step_grad * jax.nn.sigmoid(dt_pre)).astype(BF)
     dtproj_grad = contract(grad_dt_pre, dt_in_t, 0, 1)
-    grad_xdbl_t = jnp.concatenate([contract(dtproj_weight, grad_dt_pre, 0, 1), b_grad.T, c_grad.T], 0)
-    grad_xdbl_t, (head_grad,) = total_columns(
+    grad_xdbl_t = jnp.concatenate([b_grad.T, c_grad.T, contract(dtproj_weight, grad_dt_pre, 0, 1)], 0)
+    (grad_xdbl_t,), (head_grad,) = total_columns(
         pad_to(grad_xdbl_t, feats, 0),
         8,
         [Parcel(head_grad, "swap", "fsdp", BULK)],
@@ -1381,7 +1409,8 @@
     x_grad = matmul_tn(normed_all, grad_x.astype(BF)).astype(BF)
     small_grad = jnp.concatenate(
         [
-            xproj_grad,
+            xproj_grad[:, 2 * DS :],
+            xproj_grad[:, : 2 * DS],
             dtproj_grad,
             (a_accum * amat).T,
             taps_grad,
@@ -1417,8 +1446,11 @@
             Parcel(head_grad, "swap", "ctx", BULK),
         ],
     )
-    ff_grad = ff_grad[:, :, :, :unit_sub].transpose(2, 4, 1, 0, 3)
-    ff_grad = ff_grad.reshape(2, depth, units * n // m).astype(F32)
+    runs = n // m
+    row, column = counted(m * runs * unit_pad, units * runs)
+    piece, run, unit = row // (runs * unit_pad), row // unit_pad % runs, row % unit_pad
+    chosen = ((unit < unit_sub) & ((run * m + piece) * unit_sub + unit == column)).astype(BF)
+    ff_grad = [contract(ff_grad[:, :, i].reshape(-1, depth), chosen, 0, 0) for i in range(2)]
     small_grad = jnp.sum(small_grad, 0)
     in_grad = jnp.sum(in_grad.astype(F32), 0).astype(BF).reshape(n, depth, subp)
 
@@ -1452,16 +1484,12 @@
     gains_grad = meta_grad[0, : norm_gains.shape[0]]
     loss = meta_grad[1, 0] / (valid_sum * D)
     in_grad = in_grad[..., :sub].transpose(2, 1, 0, 3).reshape(depth, w_in.shape[1]).astype(F32)
-    query_grad = head_grad[..., :q_part].transpose(2, 1, 0, 3).reshape(depth, n * heads * HD)
-    query_grad = lax.dynamic_slice_in_dim(query_grad, fsdp_index * w_query.shape[1], w_query.shape[1], 1).astype(F32)
-    kv_parts = head_grad[..., q_part : q_part + kv_part].astype(F32)
-    kv_parts = kv_parts.transpose(1, 2, 0, 3).reshape(n, depth, 2, slots, HD)
-    kv_sums = []
-    for h in range(KVH):
-        owners = [(c, h - bases[c]) for c in range(n) if 0 <= h - bases[c] < slots]
-        kv_sums.append(sum(kv_parts[c, :, :, s] for c, s in owners))
-    kv_grad = jnp.stack(kv_sums, 2).reshape(depth, 2 * KVH * HD)
-    kv_grad = lax.dynamic_slice_in_dim(kv_grad, fsdp_index * w_keyval.shape[1], w_keyval.shape[1], 1)
+    part, shard, lane, column = counted(m, n, head_pad, head_wide)
+    chosen = (natural_column(part, shard, lane) - fsdp_index * head_wide == column).astype(BF)
+    head_grad = lax.dot_general(
+        head_grad, chosen, (((0, 1, 3), (0, 1, 2)), ((), ())), preferred_element_type=F32
+    )
+    query_grad, kv_grad = head_grad[:, :query_wide], head_grad[:, query_wide:]
 
     return (
         loss,

time: 1330 us -> 1260 us (0.947)
  local copies, waits for them, and re-layouts: 218 us -> 153 us
    broadcast_in_dim x2 -> x0, local copies, waits for them, and re-layouts: 19.9 us -> none  [the longest x1 9.99 us: body(): b_wide = jnp.broadcast_to(xdbl_t[R:R + DS].T[:, :, None], (length, DS, 128))]
    unnamed x318 -> x259, local copies, waits for them, and re-layouts: 72.6 us -> 60.4 us
    dot_general x14 -> x23, matrix products: 86.1 us -> 82 us  [contract(): lax.dot_general(left, right, (((left_dim,), (right_dim,)), ((), ())), pre...]
  transfers between devices with their start and end apart: 1 -> 1, of which waited for: 0 -> 0; matrix products, arithmetic and copies ran while one was open for 12% -> 11% of each run, Pallas kernels for 15% -> 15%
where the time goes in v3:
time: 1260 us
  Pallas kernels  898 us (71%)
  local copies, waits for them, and re-layouts  153 us (12%)
  other arithmetic  101 us (8%)
  matrix products  85.9 us (7%)
  between operations  18.6 us (1%)
    pallas_call x15, Pallas kernels, talk(): pl.pallas_call(kernel, grid=(steps,) if steps else (), out_shape=list(out...  898 us
    dot_general x23, matrix products, contract(): lax.dot_general(left, right, (((left_dim,), (right_dim,)), ((), ())), pre...  82 us
    unnamed x259, local copies, waits for them, and re-layouts  60.4 us
  transfers between devices with their start and end apart: 1, of which 0 were waited for; matrix products, arithmetic and copies ran while one was open for 11% of the time, Pallas kernels for 15%

profile of v3, /device:TPU:9, one launch (start us, length us, event | category | flops | bytes accessed | tf_op | source)
XLA Modules:
  0.0 1256.2 jit_solution(7352327809114562525)
XLA Ops:
  38.2 95.3 %share_tokens.2 = (bf16[8,256,1600]{2,1,0:T(8,128)(2,1)S(1)}, bf16[8,200,400]{2,1,0:T(8,128)(2,1)S(1)}, bf16[2,4,200,256]{3,2,1,0:T(8,128)(2,1)}, f32[4,8,256]{2...) custom-call(bf16[256,1600]{1,0:T(8,128)(2,1)S(1)} %bitcast.213, ...), custom_call_target="tpu_custom_call" | custom-call | tf_op jit(solution)/shard_map/share_tokens/pallas_call | solution.py:575
  152.2 4.4 multiply_reduce_fusion
  156.6 4.7 fusion.1
  161.4 7.9 convolution_convert_fusion.1
  178.0 54.8 %total_columns.2 = (bf16[144,2048]{1,0:T(8,128)(2,1)S(1)}, bf16[2048,16,128]{2,1,0:T(8,128)(2,1)}, bf16[2048,16,128]{2,1,0:T(8,128)(2,1)}, bf16[8,200,128]{2,1,0:T(8,128)(2,1)}, bf16[8,200,512]{2,1,0:T(8,128)(2,1)S(1)}) custom-call(f32[144,2048]{1,0:T(8,128)S(1)} %pad.64.refs_0_, bf16[8,200,128]{2,1,0:T(8,128)(2,1)S(1)} %bitcast.239), custom_call_target="tpu_custom_call" | custom-call | tf_op jit(solution)/shard_map/total_columns/pallas_call | solution.py:575
  232.9 4.7 convolution_convert_fusion.5
  249.7 39.7 %attend.1 = (bf16[256,2048]{1,0:T(8,128)(2,1)S(1)}, f32[8,2048]{1,0:T(8,128)S(1)}, bf16[4,400,512]{2,1,0:T(8,128)(2,1)S(1)}, bf16[8,200,352]{2,1,0:T(8,128)(2,1)S(1)}) custom-call(bf16[256,2048]{1,0:T(8,128)(2,1)S(1)} %bitcast.216, bf16[2,2048,64]{2,1,0:T(8,128)(2,1)S(1)} %copy-done.11, bf16[2,64,2048]{2,1,0:T(8,128)(2,1)S(1)} %get-tuple-element.296.refs_2_, ...), custom_call_target="tpu_custom_call" | custom-call | tf_op jit(solution)/shard_map/attend/pallas_call | solution.py:575
  303.4 5.5 compare_select_fusion
  312.9 31.8 %ssm_forward.1 = (f32[2048,512]{1,0:T(8,128)S(1)}, f32[16,16,512]{2,1,0:T(8,128)S(1)}, bf16[8,256,256]{2,1,0:T(8,128)(2,1)S(1)}, bf16[4,400,704]{2,1,0:T(8,128)(2,1)S(1)}) custom-call(f32[2048,512]{1,0:T(8,128)S(1)} %get-tuple-element.319.refs_0_, f32[2048,512]{1,0:T(8,128)S(1)} %copy-done.3, bf16[2048,16,128]{2,1,0:T(8,128)(2,1)} %get-tuple-element.84.refs_2_.refs_3_, ...), custom_call_target="tpu_custom_call" | custom-call | tf_op jit(solution)/shard_map/ssm_forward/pallas_call | solution.py:575
  348.7 66.3 %reduce_tokens.4 = (f32[256,1600]{1,0:T(8,128)}, bf16[4,400,1600]{2,1,0:T(8,128)(2,1)}) custom-call(bf16[2048,512]{1,0:T(8,128)(2,1)} %get-tuple-element.280.refs_0_.refs_4_, bf16[1600,512]{1,0:T(8,128)(2,1)} %bitcast.222, bf16[400,1600]{1,0:T(8,128)(2,1)} %bitcast.260), custom_call_target="tpu_custom_call" | custom-call | tf_op jit(solution)/shard_map/reduce_tokens/pallas_call | solution.py:575
  414.9 5.4 multiply_reduce_fusion.14
  424.9 4.4 multiply_reduce_fusion.12
  439.2 57.4 %share_tokens.3 = (bf16[8,256,1600]{2,1,0:T(8,128)(2,1)S(1)}, bf16[4,176,1600]{2,1,0:T(8,128)(2,1)S(1)}, bf16[4,176,1600]{2,1,0:T(8,128)(2,1)S(1)}) custom-call(bf16[256,1600]{1,0:T(8,128)(2,1)S(1)} %multiply_convert_fusion.2.refs_0_, bf16[176,1600]{1,0:T(8,128)(2,1)S(1)} %get-tuple-element.302.refs_1_, bf16[176,1600]{1,0:T(8,128)(2,1)S(1)} %get-tuple-element.301.refs_2_), custom_call_target="tpu_custom_call" | custom-call | tf_op jit(solution)/shard_map/share_tokens/pallas_call | solution.py:575
  496.7 6.0 fusion.233.refs_2_
  502.7 8.7 multiply_convert_fusion
  511.4 72.1 %reduce_tokens.5 = f32[256,1600]{1,0:T(8,128)} custom-call(bf16[2048,704]{1,0:T(8,128)(2,1)} %get-tuple-element.323.refs_0_.refs_4_, bf16[1600,704]{1,0:T(8,128)(2,1)} %bitcast.214), custom_call_target="tpu_custom_call" | custom-call | tf_op jit(solution)/shard_map/reduce_tokens/pallas_call | solution.py:575
  587.9 62.4 %feed_tokens.2 = (bf16[2048,704]{1,0:T(8,128)(2,1)}, bf16[2048,704]{1,0:T(8,128)(2,1)}, bf16[4,400,704]{2,1,0:T(8,128)(2,1)}) custom-call(bf16[256,1600]{1,0:T(8,128)(2,1)} %fusion.179.refs_0_, bf16[1600,704]{1,0:T(8,128)(2,1)} %bitcast.215, f32[2048,704]{1,0:T(8,128)} %copy-done.74, f32[2048,704]{1,0:T(8,128)} %get-tuple-element.324.refs_3_, ...), custom_call_target="tpu_custom_call" | custom-call | tf_op jit(solution)/shard_map/feed_tokens/pallas_call | solution.py:575
  650.3 84.4 %reduce_tokens.6 = (f32[256,1600]{1,0:T(8,128)}, bf16[4,176,1600]{2,1,0:T(8,128)(2,1)}, bf16[4,176,1600]{2,1,0:T(8,128)(2,1)}, bf16[4,400,704]{2,1,0:T(8,128)(2,1)}) custom-call(bf16[2048,704]{1,0:T(8,128)(2,1)} %get-tuple-element.99.refs_0_, bf16[2048,704]{1,0:T(8,128)(2,1)} %get-tuple-element.100.refs_1_, bf16[704,1600]{1,0:T(8,128)(2,1)} %bitcast.233, ...), custom_call_target="tpu_custom_call" | custom-call | tf_op jit(solution)/shard_map/reduce_tokens/pallas_call | solution.py:575
  749.1 61.1 %feed_tokens.3 = (f32[2048,512]{1,0:T(8,128)}, bf16[2048,512]{1,0:T(8,128)(2,1)}, bf16[4,400,512]{2,1,0:T(8,128)(2,1)}, bf16[4,176,1600]{2,1,0:T(8,128)(2,1)}, bf16[4,176,1600]{2,1,0:T(8,128)(2,1)}) custom-call(bf16[256,1600]{1,0:T(8,128)(2,1)} %get-tuple-element.298.refs_0_, bf16[1600,512]{1,0:T(8,128)(2,1)} %bitcast.223, ...), custom_call_target="tpu_custom_call" | custom-call | tf_op jit(solution)/shard_map/feed_tokens/pallas_call | solution.py:575
  810.2 79.3 %ssm_backward.1 = (f32[2048,512]{1,0:T(8,128)S(1)}, f32[2048,512]{1,0:T(8,128)S(1)}, f32[16,8,2048]{2,1,0:T(8,128)S(1)}, f32[16,8,2048]{2,1,0:T(8,128)S(1)}, f32...) custom-call(f32[2048,512]{1,0:T(8,128)} %copy-done.8, f32[2048,512]{1,0:T(8,128)} %copy-done.2, ...), custom_call_target="tpu_custom_call" | custom-call | tf_op jit(solution)/shard_map/ssm_backward/pallas_call | solution.py:575
  896.4 4.8 reduce_sum.331
  906.1 4.7 convert_reduce_fusion.1
  919.3 4.4 reshape.338
  927.0 48.0 %attend_back.1 = (bf16[256,2048]{1,0:T(8,128)(2,1)S(1)}, f32[2,64,2048]{2,1,0:T(8,128)S(1)}, f32[2,64,2048]{2,1,0:T(8,128)S(1)}, bf16[8,352,200]{2,1,0:T(8,128)(2,1)S(1)}, bf16[4,400,512]{2,1,0:T(8,128)(2,1)S(1)}) custom-call(bf16[256,2048]{1,0:T(8,128)(2,1)S(1)} %bitcast.217, bf16[256,2048]{1,0:T(8,128)(2,1)S(1)} %bitcast.228, ...), custom_call_target="tpu_custom_call" | custom-call | tf_op jit(solution)/shard_map/attend_back/pallas_call | solution.py:575
  977.9 6.9 convolution_convert_fusion.4
  997.8 26.1 %total_columns.3 = (bf16[144,2048]{1,0:T(8,128)(2,1)S(1)}, bf16[4,128,1600]{2,1,0:T(8,128)(2,1)S(1)}) custom-call(f32[144,2048]{1,0:T(8,128)S(1)} %select_maximum_fusion.refs_0_, bf16[4,128,1600]{2,1,0:T(8,128)(2,1)S(1)} %bitcast.218), custom_call_target="tpu_custom_call" | custom-call | tf_op jit(solution)/shard_map/total_columns/pallas_call | solution.py:575
  1035.6 8.1 multiply_multiply_fusion
  1044.7 8.6 fusion.224
  1053.4 5.4 convolution_convert_fusion.3
  1058.8 4.9 convolution_convert_fusion.2
  1078.8 75.4 %reduce_tokens.7 = (f32[256,1600]{1,0:T(8,128)}, bf16[4,2,2,176,200]{4,3,2,1,0:T(8,128)(2,1)}, f32[4,100,255]{2,1,0:T(8,128)}, bf16[4,1600,256]{2,1,0:T(8,128)(2,1)}, bf16[8,200,128]{2,1,0:T(8,128)(2,1)}) custom-call(bf16[2048,512]{1,0:T(8,128)(2,1)} %bitcast.251, bf16[2048,512]{1,0:T(8,128)(2,1)} %copy-done.68, ...), custom_call_target="tpu_custom_call" | custom-call | tf_op jit(solution)/shard_map/reduce_tokens/pallas_call | solution.py:575
  1160.4 43.4 %send_only.1 = (f32[8,4,8,256]{3,2,1,0:T(8,128)}, bf16[8,200,256]{2,1,0:T(8,128)(2,1)}, bf16[4,8,200,128]{3,2,1,0:T(8,128)(2,1)S(1)}, f32[4,8,8,256]{3,2,1,0:T(8,128)S(1)}, bf16[2,4,200,256]{3,2,1,0:T(8,128)(2,1)S(1)}) custom-call(f32[8,4,8,256]{3,2,1,0:T(8,128)S(1)} %pad_select_fusion.refs_0_, bf16[8,200,256]{2,1,0:T(8,128)(2,1)S(1)} %bitcast.231, ...), custom_call_target="tpu_custom_call" | custom-call | tf_op jit(solution)/shard_map/send_only/pallas_call | solution.py:575
  (443 shorter events, 240.7 us)
Async XLA Ops:
  7.2 301.7 %copy-start = (bf16[688,400]{0,1:T(8,128)(2,1)S(1)}, bf16[688,400]{0,1:T(8,128)(2,1)}, u32[]{:S(2)}) copy-start(bf16[688,400]{0,1:T(8,128)(2,1)} %param.31) | copy-start | bytes 1651204
  7.2 10.5 copy-start.80
  7.2 1238.9 %reduce-scatter.4.cloned.1.call-start = ((), (), s32[]{:S(2)}) async-start(), calls=%async_computation.1 | async-start | bytes 1843200
  7.8 137.5 %copy-start.106 = (pred[128]{0:T(512)(128)(4,1)}, pred[128]{0:T(512)(128)(4,1)S(1)}, u32[]{:S(2)}) copy-start(pred[128]{0:T(512)(128)(4,1)S(1)} %get-tuple-element.336) | copy-start | bytes 388
  13.6 411.2 %copy-start.6 = (bf16[1,256,1600]{2,1,0:T(8,128)(2,1)}, bf16[1,256,1600]{2,1,0:T(8,128)(2,1)S(1)}, u32[]{:S(2)}) copy-start(bf16[1,256,1600]{2,1,0:T(8,128)(2,1)S(1)} %copy.324) | copy-start | bytes 2457604
  13.6 11.4 copy-start.89
  13.6 12.1 copy-start.90
  13.7 12.8 %copy-start.100 = (bf16[100,16]{0,1:T(8,128)(2,1)S(1)}, bf16[100,16]{0,1:T(8,128)(2,1)}, u32[]{:S(2)}) copy-start(bf16[100,16]{0,1:T(8,128)(2,1)} %param.34) | copy-start | bytes 9604
  13.7 13.5 %copy-start.101 = (bf16[100,4]{0,1:T(4,128)(2,1)S(1)}, bf16[100,4]{0,1:T(4,128)(2,1)}, u32[]{:S(2)}) copy-start(bf16[100,4]{0,1:T(4,128)(2,1)} %param.35) | copy-start | bytes 2404
  13.7 13.7 %copy-start.103 = (bf16[100]{0:T(256)(128)(2,1)S(1)}, bf16[100]{0:T(256)(128)(2,1)}, u32[]{:S(2)}) copy-start(bf16[100]{0:T(256)(128)(2,1)} %param.36) | copy-start | bytes 604
  13.7 14.4 %copy-start.104 = (bf16[100]{0:T(256)(128)(2,1)S(1)}, bf16[100]{0:T(256)(128)(2,1)}, u32[]{:S(2)}) copy-start(bf16[100]{0:T(256)(128)(2,1)} %param.37) | copy-start | bytes 604
  13.7 15.1 %copy-start.105 = (bf16[100]{0:T(256)(128)(2,1)S(1)}, bf16[100]{0:T(256)(128)(2,1)}, u32[]{:S(2)}) copy-start(bf16[100]{0:T(256)(128)(2,1)} %param.38) | copy-start | bytes 604
  13.7 15.8 %copy-start.112 = (bf16[200]{0:T(256)(128)(2,1)S(1)}, bf16[200]{0:T(256)(128)(2,1)}, u32[]{:S(2)}) copy-start(bf16[200]{0:T(256)(128)(2,1)} %param.39) | copy-start | bytes 1204
  13.7 15.8 %copy-start.102 = (s32[1,256]{1,0:T(1,128)S(1)}, s32[1,256]{1,0:T(1,128)}, u32[]{:S(2)}) copy-start(s32[1,256]{1,0:T(1,128)} %param.23) | copy-start | bytes 3076
  161.4 71.5 %copy-start.72 = (bf16[2048,1600]{1,0:T(8,128)(2,1)}, bf16[2048,1600]{1,0:T(8,128)(2,1)S(1)}, u32[]{:S(2)}) copy-start(bf16[2048,1600]{1,0:T(8,128)(2,1)S(1)} %fusion.1) | copy-start | bytes 19660804
  308.9 35.8 %copy-start.8 = (f32[2048,512]{1,0:T(8,128)}, f32[2048,512]{1,0:T(8,128)S(1)}, u32[]{:S(2)}) copy-start(f32[2048,512]{1,0:T(8,128)S(1)} %get-tuple-element.319.refs_0_) | copy-start | bytes 12582916
  312.9 31.8 %copy-start.61 = (bf16[2048,1024]{1,0:T(8,128)(2,1)S(1)}, bf16[2048,1024]{1,0:T(8,128)(2,1)}, u32[]{:S(2)}) copy-start(bf16[2048,1024]{1,0:T(8,128)(2,1)} %copy-done.60) | copy-start | bytes 12582916
  344.7 70.2 %copy-start.39 = (bf16[8,256,256]{2,1,0:T(8,128)(2,1)}, bf16[8,256,256]{2,1,0:T(8,128)(2,1)S(1)}, u32[]{:S(2)}) copy-start(bf16[8,256,256]{2,1,0:T(8,128)(2,1)S(1)} %get-tuple-element.92) | copy-start | bytes 3145732
  511.4 72.8 %copy-start.66 = (bf16[1,256,1600]{2,1,0:T(8,128)(2,1)S(1)}, bf16[1,256,1600]{2,1,0:T(8,128)(2,1)}, u32[]{:S(2)}) copy-start(bf16[1,256,1600]{2,1,0:T(8,128)(2,1)} %copy.354) | copy-start | bytes 2457604
  650.3 84.5 %copy-start.54 = (f32[256,1600]{1,0:T(8,128)S(1)}, f32[256,1600]{1,0:T(8,128)}, u32[]{:S(2)}) copy-start(f32[256,1600]{1,0:T(8,128)} %get-tuple-element.279) | copy-start | bytes 4915204
  650.3 84.5 %copy-start.57 = (f32[256,1600]{1,0:T(8,128)S(1)}, f32[256,1600]{1,0:T(8,128)}, u32[]{:S(2)}) copy-start(f32[256,1600]{1,0:T(8,128)} %reduce_tokens.5) | copy-start | bytes 4915204
  749.1 61.2 %copy-start.42 = (f32[16,16,512]{2,1,0:T(8,128)S(1)}, f32[16,16,512]{2,1,0:T(8,128)}, u32[]{:S(2)}) copy-start(f32[16,16,512]{2,1,0:T(8,128)} %copy-done.41) | copy-start | bytes 1572868
  926.9 51.0 %slice-start = ((s8[6815744]{0:T(1024)(128)(4,1)}), s8[4194304]{0:T(1024)(128)(4,1)S(1)}, s32[]{:S(2)}) async-start(s8[6815744]{0:T(1024)(128)(4,1)} %bitcast.254), calls=%async_computation.2 | async-start | bytes 8388608
  927.0 51.0 %slice-start.1 = ((s8[6815744]{0:T(1024)(128)(4,1)}), s8[2621440]{0:T(1024)(128)(4,1)S(1)}, s32[]{:S(2)}) async-start(s8[6815744]{0:T(1024)(128)(4,1)} %bitcast.254), calls=%async_computation.3 | async-start | bytes 5242880
  996.3 28.8 %copy-start.4 = (f32[2048,512]{1,0:T(8,128)S(1)}, f32[2048,512]{1,0:T(8,128)}, u32[]{:S(2)}) copy-start(f32[2048,512]{1,0:T(8,128)} %copy-done.2) | copy-start | bytes 12582916
  1031.5 21.9 %slice-start.2 = ((s8[6815744]{0:T(1024)(128)(4,1)}), s8[4194304]{0:T(1024)(128)(4,1)S(1)}, s32[]{:S(2)}) async-start(s8[6815744]{0:T(1024)(128)(4,1)} %bitcast.256), calls=%async_computation.4 | async-start | bytes 8388608
  1035.6 17.8 %slice-start.3 = ((s8[6815744]{0:T(1024)(128)(4,1)}), s8[2621440]{0:T(1024)(128)(4,1)S(1)}, s32[]{:S(2)}) async-start(s8[6815744]{0:T(1024)(128)(4,1)} %bitcast.256), calls=%async_computation.5 | async-start | bytes 5242880
  1157.3 46.5 %copy-start.107 = (pred[128]{0:T(512)(128)(4,1)S(1)}, pred[128]{0:T(512)(128)(4,1)}, u32[]{:S(2)}) copy-start(pred[128]{0:T(512)(128)(4,1)} %copy-done.106) | copy-start | bytes 388
  1157.3 46.5 %copy-start.108 = (s32[8]{0:T(128)S(1)}, s32[8]{0:T(128)}, u32[]{:S(2)}) copy-start(s32[8]{0:T(128)} %get-tuple-element.337) | copy-start | bytes 100
  1157.3 46.5 %copy-start.109 = (s32[8]{0:T(128)S(1)}, s32[8]{0:T(128)}, u32[]{:S(2)}) copy-start(s32[8]{0:T(128)} %get-tuple-element.338) | copy-start | bytes 100
  1157.3 46.5 %copy-start.110 = (pred[8]{0:T(512)(128)(4,1)S(1)}, pred[8]{0:T(512)(128)(4,1)}, u32[]{:S(2)}) copy-start(pred[8]{0:T(512)(128)(4,1)} %compare_and_fusion.1) | copy-start | bytes 28
  1157.3 46.5 %copy-start.111 = (pred[128]{0:T(512)(128)(4,1)S(1)}, pred[128]{0:T(512)(128)(4,1)}, u32[]{:S(2)}) copy-start(pred[128]{0:T(512)(128)(4,1)} %iota_compare_fusion.14) | copy-start | bytes 388
  (90 other events, 357.3 us)
Sparse Core Ops, SparseCore 0:
  904.9 46.4 reduce-scatter.3

commit v4 on v3

--- a/solution.py
+++ b/solution.py
@@ -382,8 +382,13 @@
 
 def line_of(axis, sizes):
     n, m = sizes
+    ctx = lax.axis_index("ctx")
     if axis == "ctx":
-        return Line(n, lax.axis_index("ctx"), lambda peer: {"ctx": peer})
+        return Line(n, ctx, lambda peer: {"ctx": peer})
+    if axis == "chip":
+        return Line(n // 2, lax.div(ctx, 2), lambda peer: {"ctx": 2 * peer + lax.rem(ctx, 2)})
+    if axis == "core":
+        return Line(2, lax.rem(ctx, 2), lambda peer: {"ctx": ctx - lax.rem(ctx, 2) + peer})
     me = lax.axis_index("fsdp")
     if axis == "fsdp":
         return Line(m, me, lambda peer: {"fsdp": peer})
@@ -392,16 +397,21 @@
     return Line(half, own, lambda peer: {"fsdp": me - own + peer})
 
 
+def size_of(axis, sizes):
+    n, m = sizes
+    return {"ctx": n, "chip": n // 2, "core": 2, "fsdp": m, "pair": m // 2}[axis]
+
+
 def parcel_shapes(parcels, sizes):
-    n, m = sizes
-    sizes_of = {"ctx": n, "fsdp": m, "pair": m // 2}
     shapes = []
     for parcel in parcels:
         source = shapes[parcel.source] if isinstance(parcel.source, int) else parcel.source
-        size = sizes_of[parcel.axis]
+        size = size_of(parcel.axis, sizes)
         shape = source.shape
         if parcel.kind == "gather":
             shape = (size,) + shape
+        elif parcel.kind == "inner":
+            shape = shape[:1] + (size,) + shape[1:]
         elif parcel.kind == "lanes":
             shape = shape[:-1] + (size * shape[-1],)
         elif parcel.pick is not None:
@@ -420,7 +430,7 @@
         total = 0
         for p in parcels:
             self.base.append(total)
-            total += {"ctx": sizes[0], "fsdp": sizes[1], "pair": sizes[1] // 2}[p.axis]
+            total += size_of(p.axis, sizes)
 
     def parts(self, number, line, peer, owner):
         parcel, source, out = self.parcels[number], self.sources[number], self.outs[number]
@@ -430,6 +440,8 @@
             lanes = self.sources[number].shape[-1]
             spot = pl.ds(pl.multiple_of(owner * lanes, lanes), lanes)
             return source, out.at[(slice(None),) * (len(out.shape) - 1) + (spot,)]
+        if parcel.kind == "inner":
+            return source, out.at[:, owner]
         return source, out.at[owner]
 
     def copies(self, group, incoming):
@@ -542,9 +554,9 @@
     sizes = (lax.axis_size("ctx"), lax.axis_size("fsdp"))
     arrays = [p.source for p in parcels if not isinstance(p.source, int)]
     shapes = parcel_shapes(parcels, sizes)
-    total = sum({"ctx": sizes[0], "fsdp": sizes[1], "pair": sizes[1] // 2}[p.axis] for p in parcels)
-    everyone = everyone or any(p.axis == "ctx" for p in parcels)
-    fsdp = any(p.axis != "ctx" for p in parcels)
+    total = sum(size_of(p.axis, sizes) for p in parcels)
+    everyone = everyone or any(p.axis in ("ctx", "chip", "core") for p in parcels)
+    fsdp = any(p.axis in ("fsdp", "pair") for p in parcels)
     anywhere = pl.BlockSpec(memory_space=pl.ANY)
     sems = []
     if parcels:
@@ -566,11 +578,17 @@
             greet(sizes, everyone, fsdp)
             mail.begin()
 
+        if mail.has(1):
+
+            @pl.when(pl.program_id(0) == steps // 2)
+            def _():
+                mail.step(0, 1)
+
         core_kernel(*ins, *outs, *own)
 
         @pl.when(pl.program_id(0) == steps - 1)
         def _():
-            mail.end(0)
+            mail.end(1 if mail.has(1) else 0)
 
     results = pl.pallas_call(
         kernel,
@@ -1092,7 +1110,16 @@
         return array.reshape((half, subp) + array.shape[1:])[:, :sub].reshape((chans,) + array.shape[1:])
 
     mask_rows = valid[0].astype(F32)
-    meta = jnp.stack([pad_to(norm_gains.astype(F32), 256, 0), jnp.full((256,), jnp.sum(mask_rows))])
+    hidden = tokens[0].astype(F32)
+    factor_one = lax.rsqrt(jnp.mean(hidden * hidden, axis=-1, keepdims=True) + 1e-06)
+    meta_wide = max(256, rows)
+    meta = jnp.stack(
+        [
+            pad_to(norm_gains.astype(F32), meta_wide, 0),
+            jnp.full((meta_wide,), jnp.sum(mask_rows)),
+            pad_to(factor_one[:, 0], meta_wide, 0),
+        ]
+    )
     meta = pad_to(meta, 8, 0)
     in_send = pad_to(w_in.reshape(depth, chunks, half, sub).transpose(2, 1, 0, 3), subp, 3)
     head_send = jnp.concatenate([w_query, w_keyval], 1)
@@ -1108,8 +1135,8 @@
             return shape[2:]
         return ref.at[lax.div(peer, chunks), lax.rem(peer, chunks)]
 
-    (tokens_all, attn_rows), entry = share_tokens(
-        [tokens[0], w_attn_out],
+    (tokens_all,), entry = share_tokens(
+        [tokens[0]],
         0,
         [
             Parcel(in_send, "swap", "pair", 0),
@@ -1119,10 +1146,9 @@
             Parcel(2, "lanes", "fsdp", 2),
             Parcel(head_send, "gather", "fsdp", BULK),
             Parcel(small_send, "gather", "fsdp", BULK),
-            Parcel(ff_send, "swap", "fsdp", BULK),
         ],
     )
-    meta_all, in_all, head_all, small_all, ff_all = entry[3:]
+    meta_all, in_all, head_all, small_all = entry[3:]
     gain_set = meta_all[:, :, 0, : norm_gains.shape[0]].reshape(4, D)
     valid_sum = jnp.sum(meta_all[:, :, 1, 0])
     in_weight = in_all.reshape(D, 2 * wide)
@@ -1156,10 +1182,9 @@
     head_rows = sum(matmul(head_all[f], chosen[f]) for f in range(m)).astype(BF)
     head_rows = head_rows.reshape(depth, n, head_pad).transpose(1, 0, 2)
 
-    hidden = tokens[0].astype(F32)
-    normed_all = norm_forward(tokens_all.reshape(length, D).astype(F32), gain_set[0])[0].astype(BF)
+    factor_all = lax.dynamic_index_in_dim(meta_all, fsdp_index, 1, False)[:, 2, :rows].reshape(length, 1)
+    normed_all = (tokens_all.reshape(length, D).astype(F32) * factor_all * gain_set[0]).astype(BF)
     normed_all = lax.optimization_barrier(normed_all)
-    factor_one = norm_forward(hidden, gain_set[0])[1]
 
     inner_low = matmul(normed_all, in_weight).astype(BF)
     x_branch = inner_low[:, :wide].astype(F32)
@@ -1170,12 +1195,13 @@
         pre_conv = pre_conv + taps[k] * padded[k : k + length]
     ssm_in = jax.nn.silu(pre_conv)
     ssm_low = ssm_in.astype(BF)
-    (xdbl_t, b_wide, c_wide), (_, head_cols_all) = total_columns(
+    (xdbl_t, b_wide, c_wide), (_, head_cols_all, ff_all) = total_columns(
         pad_to(contract(xproj_weight, ssm_low, 0, 1), feats, 0),
         1,
         [
             Parcel(head_rows, "swap", "ctx", 0),
             Parcel(0, "lanes", "fsdp", 1),
+            Parcel(ff_send, "swap", "fsdp", BULK),
         ],
         2,
     )
@@ -1189,11 +1215,13 @@
     row, column = counted(chans, wide)
     chosen = (row // sub * subp + row % sub == column).astype(BF)
     mamba_send = contract(w_mamba_out, chosen, 0, 0).astype(BF)
-    (attn_part, lse), (mamba_all, ff_cols) = attend(
+    (attn_part, lse), (_, attn_rows, mamba_all, ff_cols) = attend(
         query_t,
         keys,
         values_t,
         [
+            Parcel(w_attn_out, "gather", "chip", 0),
+            Parcel(0, "inner", "core", 1),
             Parcel(mamba_send, "gather", "fsdp", BULK),
             Parcel(ff_all.reshape(n, depth, 2 * unit_pad), "swap", "ctx", BULK),
         ],

time: 1260 us -> 1260 us (level)
    unnamed x259 -> x272, local copies, waits for them, and re-layouts: 60.4 us -> 55.9 us
where the time goes in v4:
time: 1260 us; the launch traced here: 1250 us
  Pallas kernels  899 us (71%)
  local copies, waits for them, and re-layouts  145 us (12%)
  other arithmetic  91.4 us (7%)
  matrix products  90.6 us (7%)
  between operations  18.7 us (1%)
    pallas_call x15, Pallas kernels, talk(): pl.pallas_call(kernel, grid=(steps,) if steps else (), out_shape=list(out...  899 us
    dot_general x23, matrix products, contract(): lax.dot_general(left, right, (((left_dim,), (right_dim,)), ((), ())), pre...  86.6 us
    unnamed x272, local copies, waits for them, and re-layouts  55.9 us
  transfers between devices with their start and end apart: 1, of which 0 were waited for; matrix products, arithmetic and copies ran while one was open for 11% of the time, Pallas kernels for 15%

profile of v4, /device:TPU:9, one launch (start us, length us, event | category | flops | bytes accessed | tf_op | source)
XLA Modules:
  0.0 1245.4 jit_solution(16341552491963404236)
XLA Ops:
  13.4 4.7 reshape.316
  23.6 84.9 %share_tokens.2 = (bf16[8,256,1600]{2,1,0:T(8,128)(2,1)S(1)}, bf16[2,4,200,256]{3,2,1,0:T(8,128)(2,1)}, f32[4,8,256]{2,1,0:T(8,128)}, bf16[8,200,256]{2,1,0:T(8,...) custom-call(bf16[256,1600]{1,0:T(8,128)(2,1)S(1)} %bitcast.212, ...), custom_call_target="tpu_custom_call" | custom-call | tf_op jit(solution)/shard_map/share_tokens/pallas_call | solution.py:593
  120.5 4.7 fusion.1
  125.2 7.9 convolution_convert_fusion.1
  144.2 4.3 reshape.358
  148.5 4.3 reshape.359
  155.2 52.5 %total_columns.2 = (bf16[144,2048]{1,0:T(8,128)(2,1)S(1)}, bf16[2048,16,128]{2,1,0:T(8,128)(2,1)}, bf16[2048,16,128]{2,1,0:T(8,128)(2,1)}, bf16[8,200,128]{2,1,0...) custom-call(f32[144,2048]{1,0:T(8,128)S(1)} %copy-done.15, ...), custom_call_target="tpu_custom_call" | custom-call | tf_op jit(solution)/shard_map/total_columns/pallas_call | solution.py:593
  207.7 8.1 convolution_convert_fusion.5
  226.2 54.2 %attend.1 = (bf16[256,2048]{1,0:T(8,128)(2,1)S(1)}, f32[8,2048]{1,0:T(8,128)S(1)}, bf16[4,200,400]{2,1,0:T(8,128)(2,1)}, bf16[4,2,200,400]{3,2,1,0:T(8,128)(2,1)...) custom-call(bf16[256,2048]{1,0:T(8,128)(2,1)S(1)} %bitcast.215, ...), custom_call_target="tpu_custom_call" | custom-call | tf_op jit(solution)/shard_map/attend/pallas_call | solution.py:593
  295.5 5.5 compare_select_fusion
  305.0 31.5 %ssm_forward.1 = (f32[2048,512]{1,0:T(8,128)S(1)}, f32[16,16,512]{2,1,0:T(8,128)S(1)}, bf16[8,256,256]{2,1,0:T(8,128)(2,1)S(1)}, bf16[4,400,704]{2,1,0:T(8,128)(2,1)S(1)}) custom-call(f32[2048,512]{1,0:T(8,128)S(1)} %get-tuple-element.318.refs_0_, f32[2048,512]{1,0:T(8,128)S(1)} %copy-done.3, bf16[2048,16,128]{2,1,0:T(8,128)(2,1)} %get-tuple-element.84.refs_2_.refs_3_, ...), custom_call_target="tpu_custom_call" | custom-call | tf_op jit(solution)/shard_map/ssm_forward/pallas_call | solution.py:593
  340.6 66.2 %reduce_tokens.4 = (f32[256,1600]{1,0:T(8,128)}, bf16[4,400,1600]{2,1,0:T(8,128)(2,1)}) custom-call(bf16[2048,512]{1,0:T(8,128)(2,1)} %get-tuple-element.280.refs_0_.refs_4_, bf16[1600,512]{1,0:T(8,128)(2,1)} %bitcast.221, bf16[400,1600]{1,0:T(8,128)(2,1)} %bitcast.257), custom_call_target="tpu_custom_call" | custom-call | tf_op jit(solution)/shard_map/reduce_tokens/pallas_call | solution.py:593
  406.8 5.4 multiply_reduce_fusion.13
  431.7 57.4 %share_tokens.3 = (bf16[8,256,1600]{2,1,0:T(8,128)(2,1)S(1)}, bf16[4,176,1600]{2,1,0:T(8,128)(2,1)S(1)}, bf16[4,176,1600]{2,1,0:T(8,128)(2,1)S(1)}) custom-call(bf16[256,1600]{1,0:T(8,128)(2,1)S(1)} %multiply_convert_fusion.2.refs_0_, bf16[176,1600]{1,0:T(8,128)(2,1)S(1)} %get-tuple-element.302.refs_1_, bf16[176,1600]{1,0:T(8,128)(2,1)S(1)} %copy-done.23), custom_call_target="tpu_custom_call" | custom-call | tf_op jit(solution)/shard_map/share_tokens/pallas_call | solution.py:593
  489.1 6.0 fusion.233.refs_2_
  495.2 8.7 multiply_convert_fusion
  503.9 72.1 %reduce_tokens.5 = f32[256,1600]{1,0:T(8,128)} custom-call(bf16[2048,704]{1,0:T(8,128)(2,1)} %get-tuple-element.322.refs_0_.refs_4_, bf16[1600,704]{1,0:T(8,128)(2,1)} %bitcast.213), custom_call_target="tpu_custom_call" | custom-call | tf_op jit(solution)/shard_map/reduce_tokens/pallas_call | solution.py:593
  580.2 62.4 %feed_tokens.2 = (bf16[2048,704]{1,0:T(8,128)(2,1)}, bf16[2048,704]{1,0:T(8,128)(2,1)}, bf16[4,400,704]{2,1,0:T(8,128)(2,1)}) custom-call(bf16[256,1600]{1,0:T(8,128)(2,1)} %fusion.179.refs_0_, bf16[1600,704]{1,0:T(8,128)(2,1)} %bitcast.214, f32[2048,704]{1,0:T(8,128)} %copy-done.76, f32[2048,704]{1,0:T(8,128)} %get-tuple-element.323.refs_3_, ...), custom_call_target="tpu_custom_call" | custom-call | tf_op jit(solution)/shard_map/feed_tokens/pallas_call | solution.py:593
  642.6 84.6 %reduce_tokens.6 = (f32[256,1600]{1,0:T(8,128)}, bf16[4,176,1600]{2,1,0:T(8,128)(2,1)}, bf16[4,176,1600]{2,1,0:T(8,128)(2,1)}, bf16[4,400,704]{2,1,0:T(8,128)(2,1)}) custom-call(bf16[2048,704]{1,0:T(8,128)(2,1)} %get-tuple-element.99.refs_0_, bf16[2048,704]{1,0:T(8,128)(2,1)} %get-tuple-element.100.refs_1_, bf16[704,1600]{1,0:T(8,128)(2,1)} %bitcast.232, ...), custom_call_target="tpu_custom_call" | custom-call | tf_op jit(solution)/shard_map/reduce_tokens/pallas_call | solution.py:593
  741.3 61.2 %feed_tokens.3 = (f32[2048,512]{1,0:T(8,128)}, bf16[2048,512]{1,0:T(8,128)(2,1)}, bf16[4,400,512]{2,1,0:T(8,128)(2,1)}, bf16[4,176,1600]{2,1,0:T(8,128)(2,1)}, bf16[4,176,1600]{2,1,0:T(8,128)(2,1)}) custom-call(bf16[256,1600]{1,0:T(8,128)(2,1)} %get-tuple-element.298.refs_0_, bf16[1600,512]{1,0:T(8,128)(2,1)} %bitcast.222, ...), custom_call_target="tpu_custom_call" | custom-call | tf_op jit(solution)/shard_map/feed_tokens/pallas_call | solution.py:593
  802.4 79.3 %ssm_backward.1 = (f32[2048,512]{1,0:T(8,128)S(1)}, f32[2048,512]{1,0:T(8,128)S(1)}, f32[16,8,2048]{2,1,0:T(8,128)S(1)}, f32[16,8,2048]{2,1,0:T(8,128)S(1)}, f32...) custom-call(f32[2048,512]{1,0:T(8,128)} %copy-done.7, f32[2048,512]{1,0:T(8,128)} %copy-done.2, ...), custom_call_target="tpu_custom_call" | custom-call | tf_op jit(solution)/shard_map/ssm_backward/pallas_call | solution.py:593
  896.4 4.7 convert_reduce_fusion.1
  909.7 4.5 reshape.341
  917.4 48.2 %attend_back.1 = (bf16[256,2048]{1,0:T(8,128)(2,1)S(1)}, f32[2,64,2048]{2,1,0:T(8,128)S(1)}, f32[2,64,2048]{2,1,0:T(8,128)S(1)}, bf16[8,352,200]{2,1,0:T(8,128)(2,1)S(1)}, bf16[4,400,512]{2,1,0:T(8,128)(2,1)S(1)}) custom-call(bf16[256,2048]{1,0:T(8,128)(2,1)S(1)} %bitcast.216, bf16[256,2048]{1,0:T(8,128)(2,1)S(1)} %bitcast.227, ...), custom_call_target="tpu_custom_call" | custom-call | tf_op jit(solution)/shard_map/attend_back/pallas_call | solution.py:593
  968.6 6.7 convolution_convert_fusion.4
  983.8 26.1 %total_columns.3 = (bf16[144,2048]{1,0:T(8,128)(2,1)S(1)}, bf16[4,128,1600]{2,1,0:T(8,128)(2,1)S(1)}) custom-call(f32[144,2048]{1,0:T(8,128)S(1)} %select_maximum_fusion.refs_0_, bf16[4,128,1600]{2,1,0:T(8,128)(2,1)S(1)} %bitcast.217), custom_call_target="tpu_custom_call" | custom-call | tf_op jit(solution)/shard_map/total_columns/pallas_call | solution.py:593
  1022.0 8.4 multiply_multiply_fusion
  1031.3 8.4 fusion.224
  1039.7 5.4 convolution_convert_fusion.3
  1045.1 4.9 convolution_convert_fusion.2
  1064.4 75.4 %reduce_tokens.7 = (f32[256,1600]{1,0:T(8,128)}, bf16[4,2,2,176,200]{4,3,2,1,0:T(8,128)(2,1)}, f32[4,100,255]{2,1,0:T(8,128)}, bf16[4,1600,256]{2,1,0:T(8,128)(2,1)}, bf16[8,200,128]{2,1,0:T(8,128)(2,1)}) custom-call(bf16[2048,512]{1,0:T(8,128)(2,1)} %bitcast.248, bf16[2048,512]{1,0:T(8,128)(2,1)} %copy-done.70, ...), custom_call_target="tpu_custom_call" | custom-call | tf_op jit(solution)/shard_map/reduce_tokens/pallas_call | solution.py:593
  1147.7 43.3 %send_only.1 = (f32[8,4,8,256]{3,2,1,0:T(8,128)}, bf16[8,200,256]{2,1,0:T(8,128)(2,1)}, bf16[4,8,200,128]{3,2,1,0:T(8,128)(2,1)S(1)}, f32[4,8,8,256]{3,2,1,0:T(8,128)S(1)}, bf16[2,4,200,256]{3,2,1,0:T(8,128)(2,1)S(1)}) custom-call(f32[8,4,8,256]{3,2,1,0:T(8,128)S(1)} %pad_select_fusion.refs_0_, bf16[8,200,256]{2,1,0:T(8,128)(2,1)S(1)} %bitcast.230, ...), custom_call_target="tpu_custom_call" | custom-call | tf_op jit(solution)/shard_map/send_only/pallas_call | solution.py:593
  (458 shorter events, 225.0 us)
Async XLA Ops:
  7.2 293.8 %copy-start = (bf16[688,400]{0,1:T(8,128)(2,1)S(1)}, bf16[688,400]{0,1:T(8,128)(2,1)}, u32[]{:S(2)}) copy-start(bf16[688,400]{0,1:T(8,128)(2,1)} %param.31) | copy-start | bytes 1651204
  7.2 12.2 copy-start.90
  7.2 12.3 copy-start.91
  7.2 12.4 copy-start.104
  7.2 12.6 %copy-start.105 = (bf16[100,4]{0,1:T(4,128)(2,1)S(1)}, bf16[100,4]{0,1:T(4,128)(2,1)}, u32[]{:S(2)}) copy-start(bf16[100,4]{0,1:T(4,128)(2,1)} %param.35) | copy-start | bytes 2404
  7.2 12.7 %copy-start.107 = (bf16[100]{0:T(256)(128)(2,1)S(1)}, bf16[100]{0:T(256)(128)(2,1)}, u32[]{:S(2)}) copy-start(bf16[100]{0:T(256)(128)(2,1)} %param.36) | copy-start | bytes 604
  7.3 12.8 %copy-start.108 = (bf16[100]{0:T(256)(128)(2,1)S(1)}, bf16[100]{0:T(256)(128)(2,1)}, u32[]{:S(2)}) copy-start(bf16[100]{0:T(256)(128)(2,1)} %param.37) | copy-start | bytes 604
  7.3 13.0 %copy-start.109 = (bf16[100]{0:T(256)(128)(2,1)S(1)}, bf16[100]{0:T(256)(128)(2,1)}, u32[]{:S(2)}) copy-start(bf16[100]{0:T(256)(128)(2,1)} %param.38) | copy-start | bytes 604
  7.3 1228.0 %reduce-scatter.4.cloned.1.call-start = ((), (), s32[]{:S(2)}) async-start(), calls=%async_computation.1 | async-start | bytes 1843200
  7.3 107.6 %copy-start.110 = (pred[128]{0:T(512)(128)(4,1)}, pred[128]{0:T(512)(128)(4,1)S(1)}, u32[]{:S(2)}) copy-start(pred[128]{0:T(512)(128)(4,1)S(1)} %get-tuple-element.333) | copy-start | bytes 388
  9.0 106.0 %copy-start.112 = (s32[8]{0:T(128)}, s32[8]{0:T(128)S(1)}, u32[]{:S(2)}) copy-start(s32[8]{0:T(128)S(1)} %get-tuple-element.334) | copy-start | bytes 100
  9.0 106.0 %copy-start.114 = (s32[8]{0:T(128)}, s32[8]{0:T(128)S(1)}, u32[]{:S(2)}) copy-start(s32[8]{0:T(128)S(1)} %get-tuple-element.335) | copy-start | bytes 100
  9.0 106.0 %copy-start.116 = (pred[8]{0:T(512)(128)(4,1)}, pred[8]{0:T(512)(128)(4,1)S(1)}, u32[]{:S(2)}) copy-start(pred[8]{0:T(512)(128)(4,1)S(1)} %compare_and_fusion.1) | copy-start | bytes 28
  9.0 105.9 %copy-start.118 = (pred[128]{0:T(512)(128)(4,1)}, pred[128]{0:T(512)(128)(4,1)S(1)}, u32[]{:S(2)}) copy-start(pred[128]{0:T(512)(128)(4,1)S(1)} %iota_compare_fusion.13) | copy-start | bytes 388
  10.6 406.2 %copy-start.5 = (bf16[1,256,1600]{2,1,0:T(8,128)(2,1)}, bf16[1,256,1600]{2,1,0:T(8,128)(2,1)S(1)}, u32[]{:S(2)}) copy-start(bf16[1,256,1600]{2,1,0:T(8,128)(2,1)S(1)} %copy.324) | copy-start | bytes 2457604
  301.0 35.5 %copy-start.7 = (f32[2048,512]{1,0:T(8,128)}, f32[2048,512]{1,0:T(8,128)S(1)}, u32[]{:S(2)}) copy-start(f32[2048,512]{1,0:T(8,128)S(1)} %get-tuple-element.318.refs_0_) | copy-start | bytes 12582916
  305.0 31.6 %copy-start.64 = (bf16[2048,1024]{1,0:T(8,128)(2,1)S(1)}, bf16[2048,1024]{1,0:T(8,128)(2,1)}, u32[]{:S(2)}) copy-start(bf16[2048,1024]{1,0:T(8,128)(2,1)} %copy-done.63) | copy-start | bytes 12582916
  336.6 70.2 %copy-start.43 = (bf16[8,256,256]{2,1,0:T(8,128)(2,1)}, bf16[8,256,256]{2,1,0:T(8,128)(2,1)S(1)}, u32[]{:S(2)}) copy-start(bf16[8,256,256]{2,1,0:T(8,128)(2,1)S(1)} %get-tuple-element.92) | copy-start | bytes 3145732
  503.9 72.8 %copy-start.69 = (bf16[1,256,1600]{2,1,0:T(8,128)(2,1)S(1)}, bf16[1,256,1600]{2,1,0:T(8,128)(2,1)}, u32[]{:S(2)}) copy-start(bf16[1,256,1600]{2,1,0:T(8,128)(2,1)} %copy.354) | copy-start | bytes 2457604
  642.6 84.6 %copy-start.57 = (f32[256,1600]{1,0:T(8,128)S(1)}, f32[256,1600]{1,0:T(8,128)}, u32[]{:S(2)}) copy-start(f32[256,1600]{1,0:T(8,128)} %get-tuple-element.279) | copy-start | bytes 4915204
  642.6 84.6 %copy-start.60 = (f32[256,1600]{1,0:T(8,128)S(1)}, f32[256,1600]{1,0:T(8,128)}, u32[]{:S(2)}) copy-start(f32[256,1600]{1,0:T(8,128)} %reduce_tokens.5) | copy-start | bytes 4915204
  741.2 61.2 %copy-start.48 = (f32[16,16,512]{2,1,0:T(8,128)S(1)}, f32[16,16,512]{2,1,0:T(8,128)}, u32[]{:S(2)}) copy-start(f32[16,16,512]{2,1,0:T(8,128)} %copy-done.47) | copy-start | bytes 1572868
  917.4 51.2 %slice-start = ((s8[6815744]{0:T(1024)(128)(4,1)}), s8[4194304]{0:T(1024)(128)(4,1)S(1)}, s32[]{:S(2)}) async-start(s8[6815744]{0:T(1024)(128)(4,1)} %bitcast.251), calls=%async_computation.2 | async-start | bytes 8388608
  917.4 51.1 %slice-start.1 = ((s8[6815744]{0:T(1024)(128)(4,1)}), s8[2621440]{0:T(1024)(128)(4,1)S(1)}, s32[]{:S(2)}) async-start(s8[6815744]{0:T(1024)(128)(4,1)} %bitcast.251), calls=%async_computation.3 | async-start | bytes 5242880
  982.4 29.6 %copy-start.4 = (f32[2048,512]{1,0:T(8,128)S(1)}, f32[2048,512]{1,0:T(8,128)}, u32[]{:S(2)}) copy-start(f32[2048,512]{1,0:T(8,128)} %copy-done.2) | copy-start | bytes 12582916
  1017.8 21.9 %slice-start.2 = ((s8[6815744]{0:T(1024)(128)(4,1)}), s8[4194304]{0:T(1024)(128)(4,1)S(1)}, s32[]{:S(2)}) async-start(s8[6815744]{0:T(1024)(128)(4,1)} %bitcast.253), calls=%async_computation.4 | async-start | bytes 8388608
  1021.9 17.8 %slice-start.3 = ((s8[6815744]{0:T(1024)(128)(4,1)}), s8[2621440]{0:T(1024)(128)(4,1)S(1)}, s32[]{:S(2)}) async-start(s8[6815744]{0:T(1024)(128)(4,1)} %bitcast.253), calls=%async_computation.5 | async-start | bytes 5242880
  1143.4 48.4 %copy-start.111 = (pred[128]{0:T(512)(128)(4,1)S(1)}, pred[128]{0:T(512)(128)(4,1)}, u32[]{:S(2)}) copy-start(pred[128]{0:T(512)(128)(4,1)} %copy-done.110) | copy-start | bytes 388
  1143.4 48.4 %copy-start.113 = (s32[8]{0:T(128)S(1)}, s32[8]{0:T(128)}, u32[]{:S(2)}) copy-start(s32[8]{0:T(128)} %copy-done.112) | copy-start | bytes 100
  1143.5 48.4 %copy-start.115 = (s32[8]{0:T(128)S(1)}, s32[8]{0:T(128)}, u32[]{:S(2)}) copy-start(s32[8]{0:T(128)} %copy-done.114) | copy-start | bytes 100
  1143.5 48.4 %copy-start.117 = (pred[8]{0:T(512)(128)(4,1)S(1)}, pred[8]{0:T(512)(128)(4,1)}, u32[]{:S(2)}) copy-start(pred[8]{0:T(512)(128)(4,1)} %copy-done.116) | copy-start | bytes 28
  1143.5 48.4 %copy-start.119 = (pred[128]{0:T(512)(128)(4,1)S(1)}, pred[128]{0:T(512)(128)(4,1)}, u32[]{:S(2)}) copy-start(pred[128]{0:T(512)(128)(4,1)} %copy-done.118) | copy-start | bytes 388
  (97 other events, 453.1 us)
Sparse Core Ops, SparseCore 0:
  895.2 46.6 reduce-scatter.3
